TPU v7x, 128 devices: a whole 4x4x4 slice. The times are simulated.
128 devices in a mesh: row: 4 (over z), col: 32 (over y, x, core).
Axes of the slice: x: 4, y: 4, z: 4, core: 2. Of those that a mesh axis runs over, the one named last changes fastest.
Arguments:
- tokens: bfloat16 [128, 512, 512], P('row', 'col'), may hold values from -6 to 6
- tile_mask: int32 [8, 32], P('row', 'col'), may hold values 0 or 1
- norm_gain: float32 [512], replicated, may hold values from 0.5 to 1.5
- w_in: bfloat16 [512, 2048], P(None, ('row', 'col')), may hold values from -0.25 to 0.25
- conv_weight: float32 [9, 1024], replicated, may hold values from -2 to 2
- conv_bias: float32 [1024], replicated, may hold values from -3 to 3
- w_proj: bfloat16 [1024, 256], P(('row', 'col')), may hold values from -0.1875 to 0.1875
- dt_bias: float32 [4, 32], replicated, may hold values from 0.25 to 1.25
- decay_rate: float32 [4, 32], replicated, may hold values from 0.006 to 0.12, as said below
- skip_gain: float32 [1024], replicated, may hold values from 0.5 to 1.5
- out_gain: float32 [1024], replicated, may hold values from 0.5 to 1.5
- w_out: bfloat16 [1024, 512], P(('row', 'col')), may hold values from -0.1875 to 0.1875
Outputs:
- result: bfloat16 [128, 512, 512], P('row', 'col')
Inputs may be any that keep to these rules, and one draw needn't show every extreme that they name: `decay_rate`: decay rates of each direction and head.
All inputs are finite; a program needn't handle non-finite values. No bound on the sum of `tile_mask` on one device may be relied on, other than what follows from the above.
Results may differ from a plain program's by a relative error of at most 0.01.
Values may be sent and summed in bfloat16 or wider, within the bound.
No kernel may reach another device: no remote copies, remote signals or barrier semaphores. Data moves between devices by JAX's collectives and lax.ppermute only.
A program may use at most 448 MiB of HBM per device.

v0:
```python
import jax
import jax.numpy as jnp
from jax import lax
from jax.sharding import PartitionSpec as P

STATE = 16
HEADS = 32
BLOCK = 16
TILE = 16


highest = lax.Precision.HIGHEST


def extended(x, sides, width):
    for axis, dim in sides:
        count, length = (lax.axis_size(axis), x.shape[dim])
        up = [(i, (i + 1) % count) for i in range(count - 1)]
        down = [(j, i) for i, j in up]
        last = lax.slice_in_dim(x, length - width, length, axis=dim)
        initial = lax.slice_in_dim(x, 0, width, axis=dim)
        before = lax.ppermute(last, axis, up)
        after = lax.ppermute(initial, axis, down)
        x = jnp.concatenate([before, x, after], axis=dim)
    return x


def prefix(x, axis, combine, identity, reverse):
    count, position = (lax.axis_size(axis), lax.axis_index(axis))
    everything = jax.tree.map(
        lambda part, kind: lax.all_gather(part.astype(kind), axis),
        x,
        jax.tree.map(lambda a: jnp.bfloat16 if a.dtype == jnp.float32 else a.dtype, x),
    )
    start = jax.tree.map(
        lambda part, zero: jnp.broadcast_to(jnp.asarray(zero, part.dtype), part.shape), x, identity
    )

    def hop(k, before):
        at = count - 1 - k if reverse else k
        reached = at > position if reverse else at < position
        new = combine(
            before, jax.tree.map(lambda part, own: part[at].astype(own.dtype), everything, x)
        )
        return jax.tree.map(lambda a, b: jnp.where(reached, a, b), new, before)

    return lax.fori_loop(0, count, hop, start)


def layer_norm(values, factor):
    average = jnp.mean(values, axis=-1, keepdims=True)
    centered = values - average
    spread = jnp.mean(centered * centered, axis=-1, keepdims=True)
    return centered * lax.rsqrt(spread + 1e-05) * factor


def block_terms(inputs, step_sizes, write_coef, read_coef, decays, block_len):
    line_count, length, expand = inputs.shape
    heads = step_sizes.shape[-1]
    head_width = expand // heads
    blocks = length // block_len
    states = write_coef.shape[-1]
    values = inputs.reshape(line_count, blocks, block_len, heads, head_width)
    step_blk = step_sizes.reshape(line_count, blocks, block_len, heads)
    write_blk = write_coef.reshape(line_count, blocks, block_len, states)
    read_blk = read_coef.reshape(line_count, blocks, block_len, states)
    cumulative = jnp.cumsum(-step_blk * decays, axis=2)
    affinity = jnp.einsum("lbtn,lbsn->lbts", read_blk, write_blk, precision=highest)
    target_idx = lax.broadcasted_iota(jnp.int32, (block_len, block_len), 0)
    source_idx = lax.broadcasted_iota(jnp.int32, (block_len, block_len), 1)
    causal = (source_idx <= target_idx)[None, None, None]
    cum_heads = jnp.moveaxis(cumulative, 3, 2)
    difference = cum_heads[:, :, :, :, None] - cum_heads[:, :, :, None, :]
    step_heads = jnp.moveaxis(step_blk, 3, 2)
    mixing = jnp.where(
        causal,
        affinity[:, :, None]
        * jnp.exp(jnp.where(causal, difference, 0.0))
        * step_heads[:, :, :, None, :],
        0.0,
    ).astype(jnp.bfloat16)
    local_out = jnp.einsum("lbhts,lbshp->lbthp", mixing, values, preferred_element_type=jnp.float32)
    local_out = local_out.reshape(line_count, blocks, block_len, expand)
    tail_weight = jnp.exp(cumulative[:, :, -1:, :] - cumulative) * step_blk
    weighted = (values.astype(jnp.float32) * tail_weight[..., None]).reshape(
        line_count, blocks, block_len, expand
    )
    zstate = jnp.einsum("lbse,lbsn->lbne", weighted, write_blk, precision=highest)
    bdecay = jnp.repeat(jnp.exp(cumulative[:, :, -1, :]), head_width, axis=-1)
    return (local_out, cumulative, read_blk, zstate, bdecay)


def block_prefix(zstate, bdecay):
    line_count, blocks, states, expand = zstate.shape

    def advance(carried, current):
        running, product = carried
        block_state, block_decay = current
        return (
            (block_decay[:, None, :] * running + block_state, block_decay * product),
            (running, product),
        )

    initial = (
        jnp.zeros((line_count, states, expand), jnp.float32),
        jnp.ones((line_count, expand), jnp.float32),
    )
    closing, entering = lax.scan(
        advance, initial, (jnp.moveaxis(zstate, 1, 0), jnp.moveaxis(bdecay, 1, 0))
    )
    return (
        jnp.moveaxis(entering[0], 0, 1),
        jnp.moveaxis(entering[1], 0, 1),
        closing[0],
        closing[1],
    )


def readout(local_out, cumulative, read_blk, entering):
    line_count, blocks, block_len, expand = local_out.shape
    head_width = expand // cumulative.shape[-1]
    carried = jnp.einsum("lbtn,lbne->lbte", read_blk, entering, precision=highest)
    combined = local_out + jnp.repeat(jnp.exp(cumulative), head_width, axis=-1) * carried
    return combined.reshape(line_count, blocks * block_len, expand)


def local_pass(inputs, step_sizes, write_coef, read_coef, decays):
    local_out, cumulative, read_blk, zstate, bdecay = block_terms(
        inputs, step_sizes, write_coef, read_coef, decays, BLOCK
    )
    entering, before, closing_state, closing_decay = block_prefix(zstate, bdecay)
    return ((local_out, cumulative, read_blk, entering, before), (closing_decay, closing_state))


def finish(pieces, incoming):
    local_out, cumulative, read_blk, entering, before = pieces
    initial = incoming[1]
    full_entering = entering + before[:, :, None, :] * initial[:, None, :, :]
    return readout(local_out, cumulative, read_blk, full_entering)


def link(earlier, later):
    return (earlier[0] * later[0], later[0][:, None, :] * earlier[1] + later[1])


def neutral(summary):
    return (jnp.ones_like(summary[0]), jnp.zeros_like(summary[1]))


def swapped(array):
    return jnp.swapaxes(array, 0, 1)


def on_device(
    tokens,
    tile_mask,
    norm_gain,
    w_in,
    conv_weight,
    conv_bias,
    w_proj,
    dt_bias,
    decay_rate,
    skip_gain,
    out_gain,
    w_out,
):
    full_in, full_proj, full_out = (
        lax.all_gather(w_in, ("row", "col"), axis=1, tiled=True),
        lax.all_gather(w_proj, ("row", "col"), axis=0, tiled=True),
        lax.all_gather(w_out, ("row", "col"), axis=0, tiled=True),
    )
    height, breadth, channels = tokens.shape
    expand = full_out.shape[0]
    normed = layer_norm(tokens.astype(jnp.float32), norm_gain).astype(jnp.bfloat16)
    flat = normed.reshape(height * breadth, channels)
    branch = (
        jnp.dot(flat, full_in[:, :expand], preferred_element_type=jnp.float32)
        .astype(jnp.bfloat16)
        .reshape(height, breadth, expand)
    )
    gating = (
        jnp.dot(flat, full_in[:, expand:], preferred_element_type=jnp.float32)
        .astype(jnp.bfloat16)
        .reshape(height, breadth, expand)
    )
    padded = extended(branch, (("row", 0), ("col", 1)), 1)
    convolved = conv_bias * jnp.ones((height, breadth, expand), jnp.float32)
    for row_tap in range(3):
        for col_tap in range(3):
            convolved = (
                convolved
                + padded[row_tap : row_tap + height, col_tap : col_tap + breadth].astype(
                    jnp.float32
                )
                * conv_weight[3 * row_tap + col_tap]
            )
    activated = jax.nn.silu(convolved).astype(jnp.bfloat16)
    coefs_all = jnp.dot(
        activated.reshape(height * breadth, expand), full_proj, preferred_element_type=jnp.float32
    ).reshape(height, breadth, -1)
    kept = (
        jnp.broadcast_to(tile_mask[:, None, :, None], (height // TILE, TILE, breadth // TILE, TILE))
        .reshape(height, breadth)
        .astype(jnp.float32)
    )
    group_len = HEADS + 2 * STATE

    def coefs(direction):
        coef_block = coefs_all[..., direction * group_len : (direction + 1) * group_len]
        step_sizes = kept[..., None] * jax.nn.softplus(coef_block[..., :HEADS] + dt_bias[direction])
        return (
            step_sizes,
            coef_block[..., HEADS : HEADS + STATE],
            coef_block[..., HEADS + STATE :],
        )

    step_sizes, write_coef, read_coef = coefs(0)
    pieces, summary = local_pass(activated, step_sizes, write_coef, read_coef, decay_rate[0])
    incoming = prefix(summary, "col", link, neutral(summary), False)
    eastward = finish(pieces, incoming)
    step_sizes, write_coef, read_coef = coefs(1)
    pieces, summary = local_pass(
        activated[:, ::-1],
        step_sizes[:, ::-1],
        write_coef[:, ::-1],
        read_coef[:, ::-1],
        decay_rate[1],
    )
    incoming = prefix(summary, "col", link, neutral(summary), True)
    westward = finish(pieces, incoming)[:, ::-1]
    across = eastward + westward
    columns_in = swapped(activated)
    step_sizes, write_coef, read_coef = coefs(2)
    pieces, summary = local_pass(
        columns_in, swapped(step_sizes), swapped(write_coef), swapped(read_coef), decay_rate[2]
    )
    incoming = prefix(summary, "row", link, neutral(summary), False)
    southward = finish(pieces, incoming)
    step_sizes, write_coef, read_coef = coefs(3)
    pieces, summary = local_pass(
        columns_in[:, ::-1],
        swapped(step_sizes)[:, ::-1],
        swapped(write_coef)[:, ::-1],
        swapped(read_coef)[:, ::-1],
        decay_rate[3],
    )
    incoming = prefix(summary, "row", link, neutral(summary), True)
    northward = finish(pieces, incoming)[:, ::-1]
    downward = swapped(southward + northward)
    summed = skip_gain * activated.astype(jnp.float32) + across + downward
    mixed = (layer_norm(summed, out_gain) * jax.nn.silu(gating.astype(jnp.float32))).astype(
        jnp.bfloat16
    )
    projected = jnp.dot(
        mixed.reshape(height * breadth, expand), full_out, preferred_element_type=jnp.float32
    ).reshape(height, breadth, channels)
    return (tokens.astype(jnp.float32) + projected).astype(jnp.bfloat16)


def solution(mesh):
    placed = (
        P("row", "col", None),
        P("row", "col"),
        P(),
        P(None, ("row", "col")),
        P(),
        P(),
        P(("row", "col"), None),
        P(),
        P(),
        P(),
        P(),
        P(("row", "col"), None),
    )
    return jax.shard_map(
        on_device, mesh=mesh, in_specs=placed, out_specs=P("row", "col", None), check_vma=False
    )
```

profile of v0, /device:TPU:1, one launch (start us, length us, event | category | flops | bytes accessed | tf_op | source)
XLA Modules:
  0.0 769.8 jit_solution(5429008536737727301)
XLA Ops:
  12.3 42.3 %all_gather.50 = bf16[1024,256]{1,0:T(8,128)(2,1)} all-gather(bf16[8,256]{1,0:T(8,128)(2,1)S(1)} %copy-done.30), channel_id=1, replica_groups=mesh['row'=4,'col'=32] {'row','col'}, dimensions={0}, use_global_device_ids=true | all-gather | bytes 528384 | tf_op jit(solution)/shard_map/all_gather | solution.py:170
  54.5 25.0 %all-gather.15.cloned.1.call-done = bf16[512,2048]{0,1:T(8,128)(2,1)} async-done(((bf16[512,16]{0,1:T(8,128)(2,1)}), bf16[512,2048]{0,1:T(8,128)(2,1)}) %all-gather.15.cloned.1.call-update) | async-done | bytes 2097168 | tf_op jit(solution)/shard_map/all_gather | solution.py:169
  101.4 4.8 multiply_convert_fusion
  113.1 4.6 mul.689
  117.7 7.7 %mul.690 = f32[16,2,16,1024]{3,2,1,0:T(8,128)} reshape(f32[16,2,16,32,32]{4,3,2,1,0:T(8,128)} %mul.689) | data formatting | bytes 4194304 | tf_op jit(solution)/shard_map/mul | solution.py:85
  135.8 6.6 fusion.68
  144.6 6.1 while.112
  155.1 4.6 mul.673
  159.7 7.8 %mul.674 = f32[16,2,16,1024]{3,2,1,0:T(8,128)} reshape(f32[16,2,16,32,32]{4,3,2,1,0:T(8,128)} %mul.673) | data formatting | bytes 4194304 | tf_op jit(solution)/shard_map/mul | solution.py:85
  170.0 6.6 fusion.65
  187.5 4.6 mul.660
  192.1 7.9 %mul.661 = f32[32,16,1024]{2,1,0:T(8,128)} reshape(f32[32,16,32,32]{3,2,1,0:T(8,128)} %mul.660) | data formatting | bytes 4194304 | tf_op jit(solution)/shard_map/mul | solution.py:85
  207.0 4.6 mul.642
  211.6 7.8 %mul.643 = f32[32,16,1024]{2,1,0:T(8,128)} reshape(f32[32,16,32,32]{3,2,1,0:T(8,128)} %mul.642) | data formatting | bytes 4194304 | tf_op jit(solution)/shard_map/mul | solution.py:85
  228.3 6.3 reshape.459
  234.5 6.3 reshape.470
  247.4 4.4 reshape.456
  259.7 7.6 fusion.42
  267.4 6.8 copy.117
  274.2 8.0 %reshape.461 = f32[32,16,1024]{2,1,0:T(8,128)} reshape(f32[32,1,16,32,32]{4,3,2,0,1:T(8,128)} %copy.117) | data formatting | bytes 4194304 | tf_op jit(solution)/shard_map/reshape | solution.py:83
  282.1 5.7 broadcast_in_dim.189
  287.8 8.2 %broadcast_in_dim.190 = f32[32,16,1024]{2,1,0:T(8,128)} reshape(f32[32,16,32,32]{3,2,1,0:T(8,128)} %broadcast_in_dim.189) | data formatting | bytes 4194304 | tf_op jit(solution)/shard_map/broadcast_in_dim | solution.py:123
  296.0 10.5 %all-gather.4 = bf16[64,1024]{1,0:T(8,128)(2,1)} all-gather(bf16[16,1024]{1,0:T(8,128)(2,1)S(1)} %convert_element_type.312), channel_id=6, replica_groups=mesh['row'=4,'col'=32] {'row'}, dimensions={0}, use_global_device_ids=true | all-gather | bytes 163840 | tf_op jit(solution)/shard_map/all_gather | solution.py:31
  313.5 8.3 %fusion.36 = f32[16,2,16,32,32]{4,2,3,1,0:T(8,128)S(1)} fusion(bf16[16,2,16,32,32]{4,3,0,2,1:T(8,128)(2,1)} %reshape.470, f32[16,2,32,16]{3,2,1,0:T(8,128)} %copy.143, f32[16,2,32,16]{3,2,1,0:T(8,128)} %copy.141, f32[16,2,16,16]{3,2,1,0:T(8,128)} %fusion.111, pred[16,16]{1,0:T(8,128)(4,1)S(1)} %iota_compare_fusion), kind=kOutput, calls=%fused_computation.58 | convolution fusion | flops 18350080 | bytes 3309824 | tf_op jit(solution)/shard_map/lbhts,lbshp->lbthp/dot_general | solution.py:82
  321.8 6.8 copy.145
  328.5 7.9 %reshape.474 = f32[16,2,16,1024]{3,2,1,0:T(8,128)} reshape(f32[16,2,16,32,32]{4,3,2,1,0:T(8,128)} %copy.145) | data formatting | bytes 4194304 | tf_op jit(solution)/shard_map/reshape | solution.py:83
  336.6 4.7 broadcast_in_dim.197
  341.3 8.0 %reshape.475 = f32[16,2,16,1024]{3,2,1,0:T(8,128)} reshape(f32[16,2,16,32,32]{4,3,2,1,0:T(8,128)} %broadcast_in_dim.197) | data formatting | bytes 4194304 | tf_op jit(solution)/shard_map/reshape | solution.py:123
  349.3 10.7 %all-gather.2 = bf16[64,1024]{1,0:T(8,128)(2,1)} all-gather(bf16[16,1024]{1,0:T(8,128)(2,1)S(1)} %convert_element_type.307), channel_id=4, replica_groups=mesh['row'=4,'col'=32] {'row'}, dimensions={0}, use_global_device_ids=true | all-gather | bytes 163840 | tf_op jit(solution)/shard_map/all_gather | solution.py:31
  360.2 4.8 broadcast_in_dim.195
  365.0 8.1 %reshape.467 = f32[16,2,16,1024]{3,2,1,0:T(8,128)} reshape(f32[16,2,16,32,32]{4,3,2,1,0:T(8,128)} %broadcast_in_dim.195) | data formatting | bytes 4194304 | tf_op jit(solution)/shard_map/reshape | solution.py:123
  378.3 8.2 %fusion.39 = f32[16,2,16,32,32]{4,2,3,1,0:T(8,128)S(1)} fusion(bf16[16,2,16,32,32]{4,3,0,2,1:T(8,128)(2,1)} %reshape.462, f32[16,2,32,16]{3,2,1,0:T(8,128)} %copy.126, f32[16,2,32,16]{3,2,1,0:T(8,128)} %copy.124, f32[16,2,16,16]{3,2,1,0:T(8,128)} %fusion.115, pred[16,16]{1,0:T(8,128)(4,1)S(1)} %iota_compare_fusion), kind=kOutput, calls=%fused_computation.59 | convolution fusion | flops 18350080 | bytes 3309824 | tf_op jit(solution)/shard_map/lbhts,lbshp->lbthp/dot_general | solution.py:82
  386.5 6.8 copy.128
  393.3 7.8 %reshape.466 = f32[16,2,16,1024]{3,2,1,0:T(8,128)} reshape(f32[16,2,16,32,32]{4,3,2,1,0:T(8,128)} %copy.128) | data formatting | bytes 4194304 | tf_op jit(solution)/shard_map/reshape | solution.py:83
  404.1 7.9 %fusion.45 = f32[32,1,16,32,32]{4,2,3,0,1:T(8,128)S(1)} fusion(bf16[32,16,32,32]{3,2,1,0:T(8,128)(2,1)} %reshape.456, f32[32,32,16]{2,1,0:T(8,128)} %copy.107, f32[32,32,16]{2,1,0:T(8,128)} %copy.105, f32[32,16,16]{2,1,0:T(8,128)} %fusion.105, pred[16,16]{1,0:T(8,128)(4,1)S(1)} %iota_compare_fusion), kind=kOutput, calls=%fused_computation.61 | convolution fusion | flops 18350080 | bytes 3309824 | tf_op jit(solution)/shard_map/lbhts,lbshp->lbthp/dot_general | solution.py:82
  411.9 6.8 copy.109
  418.7 7.8 %reshape.458 = f32[32,16,1024]{2,1,0:T(8,128)} reshape(f32[32,1,16,32,32]{4,3,2,0,1:T(8,128)} %copy.109) | data formatting | bytes 4194304 | tf_op jit(solution)/shard_map/reshape | solution.py:83
  426.5 4.6 broadcast_in_dim.185
  431.1 8.1 %broadcast_in_dim.186 = f32[32,16,1024]{2,1,0:T(8,128)} reshape(f32[32,16,32,32]{3,2,1,0:T(8,128)} %broadcast_in_dim.185) | data formatting | bytes 4194304 | tf_op jit(solution)/shard_map/broadcast_in_dim | solution.py:123
  439.2 13.2 %while.113 = (s32[]{:T(128)}, f32[16,16,1024]{2,1,0:T(8,128)}, s32[]{:T(128)}, bf16[4,16,1024]{2,1,0:T(8,128)(2,1)}, bf16[4,16,16,1024]{3,2,1,0:T(8,128)(2,1)}, ...) while((s32[]{:T(128)}, f32[16,16,1024]{2,1,0:T(8,128)}, s32[]{:T(128)}, ...), condition=%wide.region_17.18_spmd.clone, body=%wide.region_16.17_spmd.clone.sunk | while | flops 1327112 | bytes 2785447 | solution.py:47
  452.4 5.3 multiply_add_fusion
  460.4 13.8 %while.111 = (s32[]{:T(128)}, f32[16,16,1024]{2,1,0:T(8,128)}, s32[]{:T(128)}, bf16[4,16,1024]{2,1,0:T(8,128)(2,1)}, bf16[4,16,16,1024]{3,2,1,0:T(8,128)(2,1)}, /*index=5*/s32[]{:T(128)}, s32[]{:T(128)}) while((s32[]{:T(128)}, f32[16,16,1024]{2,1,0:T(8,128)}, s32[]{:T(128)}, bf16[4,16,1024]{2,1,0:T(8,128)(2,1)}, ...), condition=%wide.region_12.13_spmd.clone, body=%wide.region_11.12_spmd.clone.sunk | while | flops 1327108 | bytes 2785385 | solution.py:47
  474.2 6.0 multiply_add_fusion.1
  482.7 147.6 %while.109 = (s32[]{:T(128)}, f32[32,16,1024]{2,1,0:T(8,128)}, s32[]{:T(128)}, bf16[32,32,1024]{2,1,0:T(8,128)(2,1)}, bf16[32,32,16,1024]{3,2,1,0:T(8,128)(2,1)}...) while((s32[]{:T(128)}, f32[32,16,1024]{2,1,0:T(8,128)}, s32[]{:T(128)}, ...), condition=%wide.region_7.8_spmd.clone, body=%wide.region_6.7_spmd.clone.sunk | while | flops 2654216 | bytes 5570727 | solution.py:47
  630.3 106.5 %while.108 = (s32[]{:T(128)}, f32[32,16,1024]{2,1,0:T(8,128)S(1)}, s32[]{:T(128)}, bf16[32,32,1024]{2,1,0:T(8,128)(2,1)}, bf16[32,32,16,1024]{3,2,1,0:T(8,128)(2,1)}, /*index=5*/s32[]{:T(128)}, s32[]{:T(128)}) while((s32[]{:T(128)}, f32[32,16,1024]{2,1,0:T(8,128)S(1)}, s32[]{:T(128)}, bf16[32,32,1024]{2,1,0:T(8,128)(2,1)}, ...), condition=%wide.region_4.5_spmd.clone, body=%wide.region_3.4_spmd.clone.sunk | while | flops 2654212 | bytes 5570665 | solution.py:47
  736.8 6.1 multiply_add_fusion.2
  742.9 5.7 rev.34
  748.6 8.1 %fusion.49 = f32[32,16,1024]{2,1,0:T(8,128)} fusion(bf16[32,16,1024]{2,1,0:T(8,128)(2,1)S(1)} %multiply_convert_fusion, f32[16,2,16,1024]{3,0,2,1:T(8,128)} %copy.137, f32[16,32,1024]{2,0,1:T(8,128)} %bitcast.302, f32[32,16,1024]{2,1,0:T(8,128)} %rev.34, f32[32,16,1024]{2,1,0:T(8,128)} %reshape.458, f32[32,16,1024]{2,1,0:T(8,128)} %broadcast_in_dim.186, ...), kind=kOutput, calls=%fused_computation.67 | convolution fusion | flops 104857600 | bytes 15994880 | tf_op jit(solution)/shard_map/lbtn,lbne->lbte/dot_general | solution.py:122
  (374 shorter events, 410.9 us)
Async XLA Ops:
  6.5 5.7 copy-start.30
  6.5 73.0 %all-gather.15.cloned.1.call-start = ((), (), s32[]{:S(2)}) async-start(), calls=%async_computation | async-start | bytes 2113536 | tf_op jit(solution)/shard_map/all_gather | solution.py:169
  7.3 432.0 %all-gather.29.cloned.1.call-start = ((), (), s32[]{:S(2)}) async-start(), calls=%async_computation.7 | async-start | bytes 2621440 | tf_op jit(solution)/shard_map/all_gather | solution.py:31
  12.2 76.6 %copy-start.28 = (bf16[32,16,512]{2,1,0:T(8,128)(2,1)}, bf16[32,16,512]{2,1,0:T(8,128)(2,1)S(1)}, u32[]{:S(2)}) copy-start(bf16[32,16,512]{2,1,0:T(8,128)(2,1)S(1)} %fusion.78) | copy-start | bytes 1572868
  12.2 72.4 %copy-start.34 = (f32[4,32]{1,0:T(4,128)S(1)}, f32[4,32]{1,0:T(4,128)}, u32[]{:S(2)}) copy-start(f32[4,32]{1,0:T(4,128)} %param.32) | copy-start | bytes 1540
  12.3 72.4 %copy-start.35 = (f32[4,32]{1,0:T(4,128)S(1)}, f32[4,32]{1,0:T(4,128)}, u32[]{:S(2)}) copy-start(f32[4,32]{1,0:T(4,128)} %param.31) | copy-start | bytes 1540
  79.5 15.3 %copy-start.37 = (s32[2,1]{0,1:T(1,128)S(1)}, s32[2,1]{0,1:T(1,128)}, u32[]{:S(2)}) copy-start(s32[2,1]{0,1:T(1,128)} %param.25) | copy-start | bytes 28
  81.5 19.9 %copy-start.5 = (bf16[512,1024]{1,0:T(8,128)(2,1)}, bf16[512,1024]{1,0:T(8,128)(2,1)S(1)}, u32[]{:S(2)}) copy-start(bf16[512,1024]{1,0:T(8,128)(2,1)S(1)} %convolution_convert_fusion.1) | copy-start | bytes 3145732
  81.5 3.6 collective-permute-start
  83.3 4.7 collective-permute-start.1
  88.9 6.2 collective-permute-start.2
  92.7 6.7 collective-permute-start.3
  95.1 6.3 copy-start.29
  101.4 4.9 copy-start.20
  106.7 1.9 copy-start
  108.6 1.8 copy-start.13
  144.6 2.6 copy-start.2
  147.7 2.6 copy-start.2
  151.7 308.7 %all-gather.27.cloned.1.call-start = ((), (), s32[]{:S(2)}) async-start(), calls=%async_computation.6 | async-start | bytes 2621440 | tf_op jit(solution)/shard_map/all_gather | solution.py:31
  153.1 16.4 %copy-start.11 = (f32[16,2,16,32]{3,0,1,2:T(8,128)}, f32[16,2,16,32]{3,0,1,2:T(8,128)S(1)}, u32[]{:S(2)}) copy-start(f32[16,2,16,32]{3,0,1,2:T(8,128)S(1)} %fusion.101) | copy-start | bytes 196612
  159.7 7.8 %copy-start.22 = (f32[32,16,16]{2,1,0:T(8,128)S(1)}, f32[32,16,16]{2,1,0:T(8,128)}, u32[]{:S(2)}) copy-start(f32[32,16,16]{2,1,0:T(8,128)} %get-tuple-element.839) | copy-start | bytes 98308
  167.8 2.2 copy-start.17
  178.8 1.7 copy-start.3
  181.0 1.7 copy-start.3
  184.1 298.6 %all-gather.19.cloned.1.call-start = ((), (), s32[]{:S(2)}) async-start(), calls=%async_computation.2 | async-start | bytes 2162688 | tf_op jit(solution)/shard_map/all_gather | solution.py:31
  184.2 3.3 copy-start.8
  184.3 7.8 %copy-start.12 = (f32[32,1,16,32]{3,0,1,2:T(8,128)}, f32[32,1,16,32]{3,0,1,2:T(8,128)S(1)}, u32[]{:S(2)}) copy-start(f32[32,1,16,32]{3,0,1,2:T(8,128)S(1)} %fusion.94) | copy-start | bytes 196612
  185.5 297.2 %all-gather.25.cloned.1.call-start = ((), (), s32[]{:S(2)}) async-start(), calls=%async_computation.5 | async-start | bytes 34603008 | tf_op jit(solution)/shard_map/all_gather | solution.py:31
  186.5 14.1 %copy-start.6 = (bf16[32,16,1024]{2,1,0:T(8,128)(2,1)}, bf16[32,16,1024]{2,1,0:T(8,128)(2,1)S(1)}, u32[]{:S(2)}) copy-start(bf16[32,16,1024]{2,1,0:T(8,128)(2,1)S(1)} %rev.30) | copy-start | bytes 3145732
  192.1 8.3 %copy-start.21 = (f32[32,16,16]{2,1,0:T(8,128)S(1)}, f32[32,16,16]{2,1,0:T(8,128)}, u32[]{:S(2)}) copy-start(f32[32,16,16]{2,1,0:T(8,128)} %get-tuple-element.836) | copy-start | bytes 98308
  200.5 4.3 copy-start.19
  200.5 6.5 copy-start.26
  204.9 425.4 %all-gather.17.cloned.1.call-start = ((), (), s32[]{:S(2)}) async-start(), calls=%async_computation.1 | async-start | bytes 2162688 | tf_op jit(solution)/shard_map/all_gather | solution.py:31
  206.8 423.5 %all-gather.23.cloned.1.call-start = ((), (), s32[]{:S(2)}) async-start(), calls=%async_computation.4 | async-start | bytes 34603008 | tf_op jit(solution)/shard_map/all_gather | solution.py:31
  211.6 8.3 %copy-start.1 = (f32[32,16,256]{2,1,0:T(8,128)S(1)}, f32[32,16,256]{2,1,0:T(8,128)}, u32[]{:S(2)}) copy-start(f32[32,16,256]{2,1,0:T(8,128)} %copy-done) | copy-start | bytes 1572868
  224.3 535.0 %all-gather.21.cloned.1.call-start = ((), (), s32[]{:S(2)}) async-start(), calls=%async_computation.3 | async-start | bytes 1056768 | tf_op jit(solution)/shard_map/all_gather | solution.py:171
  328.5 7.9 %copy-start.23 = (f32[16,2,16,32]{3,0,1,2:T(8,128)S(1)}, f32[16,2,16,32]{3,0,1,2:T(8,128)}, u32[]{:S(2)}) copy-start(f32[16,2,16,32]{3,0,1,2:T(8,128)} %get-tuple-element.850) | copy-start | bytes 196612
  341.3 18.7 %copy-start.24 = (f32[16,2,16,32]{3,0,1,2:T(8,128)S(1)}, f32[16,2,16,32]{3,0,1,2:T(8,128)}, u32[]{:S(2)}) copy-start(f32[16,2,16,32]{3,0,1,2:T(8,128)} %get-tuple-element.852) | copy-start | bytes 196612
  365.0 12.3 %copy-start.9 = (f32[32,16,32]{2,1,0:T(8,128)S(1)}, f32[32,16,32]{2,1,0:T(8,128)}, u32[]{:S(2)}) copy-start(f32[32,16,32]{2,1,0:T(8,128)} %get-tuple-element.834) | copy-start | bytes 196612
  393.3 9.8 %copy-start.14 = (f32[32,1,16,32]{3,0,1,2:T(8,128)S(1)}, f32[32,1,16,32]{3,0,1,2:T(8,128)}, u32[]{:S(2)}) copy-start(f32[32,1,16,32]{3,0,1,2:T(8,128)} %copy-done.13) | copy-start | bytes 196612
  418.7 7.8 %copy-start.25 = (f32[32,16,32]{2,1,0:T(8,128)S(1)}, f32[32,16,32]{2,1,0:T(8,128)}, u32[]{:S(2)}) copy-start(f32[32,16,32]{2,1,0:T(8,128)} %get-tuple-element.844) | copy-start | bytes 196612
  439.2 13.2 %copy-start.18 = (f32[16,32,16]{2,0,1:T(8,128)S(1)}, f32[16,32,16]{2,0,1:T(8,128)}, u32[]{:S(2)}) copy-start(f32[16,32,16]{2,0,1:T(8,128)} %rev.36) | copy-start | bytes 98308
  460.4 13.8 %copy-start.15 = (f32[32,16,16]{2,1,0:T(8,128)S(1)}, f32[32,16,16]{2,1,0:T(8,128)}, u32[]{:S(2)}) copy-start(f32[32,16,16]{2,1,0:T(8,128)} %get-tuple-element.840) | copy-start | bytes 98308
  630.3 106.5 %copy-start.16 = (f32[32,16,16]{2,1,0:T(8,128)S(1)}, f32[32,16,16]{2,1,0:T(8,128)}, u32[]{:S(2)}) copy-start(f32[32,16,16]{2,1,0:T(8,128)} %rev.31) | copy-start | bytes 98308
  742.9 5.7 copy-start.31
  756.7 2.2 copy-start.4
  756.7 2.6 copy-start.7
  756.7 2.6 copy-start.36
  (4 other events, 4.1 us)
Sparse Core Ops, SparseCore 0:
  10.5 68.9 all-gather.14
  151.8 32.8 all-gather.28
  186.3 30.9 all-gather.26
  219.4 43.9 all-gather.18
  265.5 112.9 all-gather.24
  380.6 43.0 all-gather.16
  426.0 112.9 all-gather.22
  541.7 62.8 all-gather.20
where the time goes:
time: 784 us; the launch traced here: 770 us
  other arithmetic  318 us (41%)
  local copies, waits for them, and re-layouts  232 us (30%)
  matrix products  97.2 us (12%)
  blocking collectives  63.5 us (8%)
  waiting for transfers between devices  33.7 us (4%)
  between operations  14.6 us (2%)
  starting transfers between devices  9.89 us (1%)
    select_n x72, other arithmetic, hop(): return jax.tree.map(lambda a, b: jnp.where(reached, a, b), new, before)  219 us
    convert_element_type x72, other arithmetic, hop(): part[at].astype(own.dtype)  60.8 us
    mul x8, local copies, waits for them, and re-layouts, block_terms(): values.astype(jnp.float32) * tail_weight[..., None]  49.8 us
    all_gather x1, blocking collectives, on_device(): lax.all_gather(w_proj, ('row', 'col'), axis=0, tiled=True)  42.3 us
    broadcast_in_dim x6, local copies, waits for them, and re-layouts, readout(): jnp.repeat(jnp.exp(cumulative), head_width, axis=-1) * carried  36.2 us
    dot_general x4, matrix products, block_terms(): jnp.einsum('lbhts,lbshp->lbthp', mixing, values, preferred_element_type=j...  32 us
    reshape x4, local copies, waits for them, and re-layouts, block_terms(): local_out = local_out.reshape(line_count, blocks, block_len, expand)  31.4 us
    transpose x4, local copies, waits for them, and re-layouts, block_terms(): jnp.einsum('lbhts,lbshp->lbthp', mixing, values, preferred_element_type=j...  27.1 us
  transfers between devices with their start and end apart: 12, of which 3 were waited for; matrix products, arithmetic and copies ran while one was open for 76% of the time, Pallas kernels for 0%

commit v1 on v0

v1 whole, which is shorter than its diff:
```python
import functools

import jax
import jax.numpy as jnp
from jax import lax
from jax.experimental import pallas as pl
from jax.experimental.pallas import tpu as pltpu
from jax.sharding import PartitionSpec as P

STATE = 16
HEADS = 32
TILE = 16
CHUNK = 128
LANES = 128
STRIDE = 24
LOG2E = 1.4426950408889634

f32 = jnp.float32
bf16 = jnp.bfloat16


def dot(a, b, contract=((1,), (0,))):
    return lax.dot_general(a, b, (contract, ((), ())), preferred_element_type=f32)


def shifted(x, axis, step):
    count = lax.axis_size(axis)
    pairs = [(i, i + step) for i in range(count) if 0 <= i + step < count]
    return lax.ppermute(x, axis, pairs)


def normalized(x, gain):
    average = jnp.mean(x, axis=-1, keepdims=True)
    centered = x - average
    spread = jnp.mean(centered * centered, axis=-1, keepdims=True)
    return centered * lax.rsqrt(spread + 1e-05) * gain


def filter_kernel(
    x_ref, gain_ref, w_ref, taps_ref, bias_ref, act_ref, turned_ref, normed, branch, order
):
    padded = x_ref.shape[0]
    tokens, width = act_ref.shape
    height = padded // STRIDE - 2
    breadth = tokens // height

    @pl.when(pl.program_id(0) == 0)
    def _():
        step = 64
        for at in range(0, padded, step):
            x = x_ref[at : at + step, :].astype(f32)
            normed[at : at + step, :] = normalized(x, gain_ref[...]).astype(bf16)
        to = lax.broadcasted_iota(jnp.int32, (tokens, tokens), 0)
        source = lax.broadcasted_iota(jnp.int32, (tokens, tokens), 1)
        w, h = to // height, to % height
        order[...] = (source == h * breadth + w).astype(f32).astype(bf16)

    product = dot(normed[...], w_ref[...], ((1,), (1,)))
    branch[...] = product.astype(bf16).astype(f32)
    rows = 4
    span = rows * STRIDE + 8
    for lane in range(0, width, LANES):
        lanes = slice(lane, lane + LANES)
        taps = [taps_ref[k : k + 1, lanes] for k in range(9)]
        for h in range(0, height, rows):
            windows = [
                branch[(h + i) * STRIDE : (h + i) * STRIDE + span, lanes] for i in range(3)
            ]
            left, middle, right = [
                windows[0] * taps[j] + windows[1] * taps[3 + j] + windows[2] * taps[6 + j]
                for j in range(3)
            ]
            convolved = (
                middle
                + pltpu.roll(left, 1, 0)
                + pltpu.roll(right, span - 1, 0)
                + bias_ref[:, lanes]
            )
            activated = convolved / (1.0 + jnp.exp(-convolved))
            kept = activated[: rows * STRIDE].reshape(rows, STRIDE, LANES)[:, 8:, :]
            act_ref[h * breadth : (h + rows) * breadth, lanes] = kept.reshape(
                rows * breadth, LANES
            ).astype(bf16)
    turned_ref[...] = dot(order[...], act_ref[...]).astype(bf16)


def filtered(x, gain, w_in, taps, bias, tokens):
    expand = bias.shape[1]
    padded, channels = x.shape
    width = 256
    return pl.pallas_call(
        filter_kernel,
        grid=(expand // width,),
        in_specs=[
            pl.BlockSpec((padded, channels), lambda c: (0, 0)),
            pl.BlockSpec((1, channels), lambda c: (0, 0)),
            pl.BlockSpec((width, channels), lambda c: (c, 0)),
            pl.BlockSpec((9, width), lambda c: (0, c)),
            pl.BlockSpec((1, width), lambda c: (0, c)),
        ],
        out_specs=[
            pl.BlockSpec((tokens, width), lambda c: (0, c)),
            pl.BlockSpec((tokens, width), lambda c: (0, c)),
        ],
        out_shape=[jax.ShapeDtypeStruct((tokens, expand), bf16)] * 2,
        scratch_shapes=[
            pltpu.VMEM((padded, channels), bf16),
            pltpu.VMEM((padded, width), f32),
            pltpu.VMEM((tokens, tokens), bf16),
        ],
        compiler_params=pltpu.CompilerParams(vmem_limit_bytes=48 * 2**20),
        name="norm_project_filter",
    )(x, gain, w_in, taps, bias)


def chunk_terms(values, w_proj, bias, rate, mask, first):
    coefs = dot(values, w_proj)
    at = lax.broadcasted_iota(jnp.int32, (CHUNK, LANES), 0)
    lane = lax.broadcasted_iota(jnp.int32, (CHUNK, LANES), 1)
    kept = jnp.sum(
        jnp.where(lane == (at + first) // TILE, mask, 0.0), axis=1, keepdims=True
    )
    v = coefs + bias
    steps = kept * (jnp.maximum(v, 0.0) + jnp.log1p(jnp.exp(-jnp.abs(v))))
    decays = steps * rate
    lower = (lane <= at).astype(f32).astype(bf16)
    high = decays.astype(bf16)
    rest = decays - high.astype(f32)
    middle = rest.astype(bf16)
    low = (rest - middle.astype(f32)).astype(bf16)
    total = dot(lower, high) + (dot(lower, middle) + dot(lower, low))
    sums = jnp.where(lane < 64, total, total - decays)
    return coefs, steps, sums, total[CHUNK - 1 :, :]


def local_weights(coefs):
    at = lax.broadcasted_iota(jnp.int32, (CHUNK, CHUNK), 0)
    source = lax.broadcasted_iota(jnp.int32, (CHUNK, CHUNK), 1)
    c = coefs.astype(bf16)
    forward = dot(c[:, 48:64], c[:, 32:48], ((1,), (1,)))
    backward = dot(c[:, 112:128], c[:, 96:112], ((1,), (1,)))
    return (
        source <= at,
        jnp.where(source <= at, forward, 0.0),
        jnp.where(source >= at, backward, 0.0),
    )


def local_tile(values, tile, weights, sums, sums_t, steps_t):
    causal, forward, backward = weights
    lane = lax.broadcasted_iota(jnp.int32, (CHUNK, LANES), 1)
    inputs = values[:, tile * LANES : (tile + 1) * LANES]
    mixing, sources = [], []
    for k in range(4):
        j = 4 * tile + k
        exponent = jnp.where(
            causal,
            sums_t[j : j + 1, :] - sums[:, j : j + 1],
            sums[:, 64 + j : 65 + j] - sums_t[64 + j : 65 + j, :],
        )
        scale = forward * steps_t[j : j + 1, :] + backward * steps_t[64 + j : 65 + j, :]
        mixing.append(jnp.exp2(exponent) * scale)
        sources.append(jnp.where(lane // 32 == k, inputs, jnp.zeros_like(inputs)))
    left = jnp.concatenate([m.astype(bf16) for m in mixing], axis=1)
    right = jnp.concatenate(sources, axis=0)
    return dot(left, right)


def line_kernel(a_ref, w_ref, bias_ref, rate_ref, mask_ref, out_ref, coefs, steps, sums, ends, states, entering):
    length, expand = a_ref.shape
    chunks = length // CHUNK
    lane = lax.broadcasted_iota(jnp.int32, (CHUNK, LANES), 1)
    head = lax.broadcasted_iota(jnp.int32, (LANES, expand), 0)
    channel = lax.broadcasted_iota(jnp.int32, (LANES, expand), 1)
    spread = [
        (head == channel // 32 + 64 * d).astype(f32).astype(bf16) for d in range(2)
    ]
    w_proj = w_ref[...]
    for c in range(chunks):
        at = slice(c * CHUNK, (c + 1) * CHUNK)
        values = a_ref[at, :]
        k, s, q, end = chunk_terms(
            values, w_proj, bias_ref[...], rate_ref[...], mask_ref[...], c * CHUNK
        )
        coefs[at, :], steps[at, :], sums[at, :] = k, s, q
        ends[8 * c : 8 * c + 8, :] = jnp.broadcast_to(end, (8, LANES))
        tail = (jnp.exp2(jnp.where(lane < 64, q - end, -q)) * s).astype(bf16)
        wide = values.astype(f32)
        for d in range(2):
            if (c == chunks - 1, c == 0)[d]:
                continue
            weighted = (wide * dot(tail, spread[d])).astype(bf16)
            write = k[:, 64 * d + 32 : 64 * d + 48].astype(bf16)
            states[d, c] = dot(write, weighted, ((0,), (0,)))
    fade = jnp.exp2(-ends[...])
    high = fade.astype(bf16)
    low = (fade - high.astype(f32)).astype(bf16)
    for d in range(2):
        decay = dot(high, spread[d]) + dot(low, spread[d])
        order = range(chunks) if d == 0 else range(chunks - 1, -1, -1)
        running = None
        for c in order:
            if running is not None:
                entering[d, c] = running.astype(bf16)
            if c == order[-1]:
                break
            new = states[d, c]
            if running is not None:
                new = new + running * decay[8 * c : 8 * c + 1, :]
            running = new
    for c in range(chunks):
        at = slice(c * CHUNK, (c + 1) * CHUNK)
        values = a_ref[at, :]
        k, q = coefs[at, :], sums[at, :]
        end = ends[8 * c : 8 * c + 1, :]
        q_t, steps_t = q.T, steps[at, :].T
        weights = local_weights(k)
        head_in = jnp.exp2(jnp.where(lane < 64, -q, q - end)).astype(bf16)
        read = k.astype(bf16)
        for tile in range(expand // LANES):
            lanes = slice(tile * LANES, (tile + 1) * LANES)
            total = local_tile(values, tile, weights, q, q_t, steps_t)
            for d in range(2):
                if (c == 0, c == chunks - 1)[d]:
                    continue
                carried = dot(read[:, 64 * d + 48 : 64 * d + 64], entering[d, c, :, lanes])
                total = total + dot(head_in, spread[d][:, lanes]) * carried
            out_ref[at, lanes] = total.astype(bf16)


def swept_lines(values, gathered, bias, rate, mask):
    length, expand = values.shape
    chunks = length // CHUNK
    return pl.pallas_call(
        line_kernel,
        grid=(1,),
        in_specs=[
            pl.BlockSpec((length, expand), lambda i: (0, 0)),
            pl.BlockSpec((expand, LANES), lambda i: (0, 4)),
            pl.BlockSpec((1, LANES), lambda i: (0, 0)),
            pl.BlockSpec((1, LANES), lambda i: (0, 0)),
            pl.BlockSpec((1, LANES), lambda i: (0, 0)),
        ],
        out_specs=pl.BlockSpec((length, expand), lambda i: (0, 0)),
        out_shape=jax.ShapeDtypeStruct((length, expand), bf16),
        scratch_shapes=[
            pltpu.VMEM((length, LANES), f32),
            pltpu.VMEM((length, LANES), f32),
            pltpu.VMEM((length, LANES), f32),
            pltpu.VMEM((8 * chunks, LANES), f32),
            pltpu.VMEM((2, chunks, STATE, expand), f32),
            pltpu.VMEM((2, chunks, STATE, expand), bf16),
        ],
        compiler_params=pltpu.CompilerParams(vmem_limit_bytes=48 * 2**20),
        name="sweep_rows",
    )(values, gathered, bias, rate, mask)


def column_kernel(a_ref, w_ref, bias_ref, rate_ref, mask_ref, out_ref):
    sources, _, height, expand = a_ref.shape
    values = a_ref[...].reshape(CHUNK, expand)
    k, s, q, _ = chunk_terms(values, w_ref[...], bias_ref[...], rate_ref[...], mask_ref[...], 0)
    weights = local_weights(k)
    q_t, steps_t = q.T, s.T
    for tile in range(expand // LANES):
        lanes = slice(tile * LANES, (tile + 1) * LANES)
        total = local_tile(values, tile, weights, q, q_t, steps_t)
        out_ref[:, :, :, lanes] = total.astype(bf16).reshape(sources, 1, height, LANES)


def swept_columns(values, gathered, bias, rate, mask):
    sources, lines, height, expand = values.shape
    return pl.pallas_call(
        column_kernel,
        grid=(lines,),
        in_specs=[
            pl.BlockSpec((sources, 1, height, expand), lambda i: (0, i, 0, 0)),
            pl.BlockSpec((expand, LANES), lambda i: (0, 5)),
            pl.BlockSpec((1, LANES), lambda i: (0, 0)),
            pl.BlockSpec((1, LANES), lambda i: (0, 0)),
            pl.BlockSpec((1, LANES), lambda i: (0, 0)),
        ],
        out_specs=pl.BlockSpec((sources, 1, height, expand), lambda i: (0, i, 0, 0)),
        out_shape=jax.ShapeDtypeStruct(values.shape, bf16),
        compiler_params=pltpu.CompilerParams(vmem_limit_bytes=48 * 2**20),
        name="sweep_columns",
    )(values, gathered, bias, rate, mask)


def output_kernel(
    act_ref, rows_ref, columns_ref, x_ref, gain_ref, wg_ref, wo_ref, skip_ref, out_gain_ref, out_ref, *, height
):
    block, expand = act_ref.shape
    tokens = columns_ref.shape[0]
    breadth = tokens // height
    x = x_ref[...].astype(f32)
    normed = normalized(x, gain_ref[...]).astype(bf16)
    gating = dot(normed, wg_ref[...], ((1,), (1,))).astype(bf16).astype(f32)
    at = lax.broadcasted_iota(jnp.int32, (block, tokens), 0) + pl.program_id(0) * block
    source = lax.broadcasted_iota(jnp.int32, (block, tokens), 1)
    h, w = at // breadth, at % breadth
    back = (source == w * height + h).astype(f32).astype(bf16)
    summed = (
        dot(back, columns_ref[...])
        + rows_ref[...].astype(f32)
        + skip_ref[...] * act_ref[...].astype(f32)
    )
    gate = gating / (1.0 + jnp.exp(-gating))
    mixed = (normalized(summed, out_gain_ref[...]) * gate).astype(bf16)
    out_ref[...] = (x + dot(mixed, wo_ref[...])).astype(bf16)


def projected(act, rows, columns, x, gain, w_in, gathered, skip, out_gain, height):
    tokens, expand = act.shape
    channels = x.shape[1]
    block = 128
    one = lambda i: (0, 0)
    return pl.pallas_call(
        functools.partial(output_kernel, height=height),
        grid=(tokens // block,),
        in_specs=[
            pl.BlockSpec((block, expand), lambda i: (i, 0)),
            pl.BlockSpec((block, expand), lambda i: (i, 0)),
            pl.BlockSpec((tokens, expand), one),
            pl.BlockSpec((block, channels), lambda i: (i, 0)),
            pl.BlockSpec((1, channels), one),
            pl.BlockSpec((expand, channels), lambda i: (1, 0)),
            pl.BlockSpec((expand, channels), one),
            pl.BlockSpec((1, expand), one),
            pl.BlockSpec((1, expand), one),
        ],
        out_specs=pl.BlockSpec((block, channels), lambda i: (i, 0)),
        out_shape=jax.ShapeDtypeStruct((tokens, channels), bf16),
        compiler_params=pltpu.CompilerParams(vmem_limit_bytes=48 * 2**20),
        name="gate_and_project",
    )(act, rows, columns, x, gain, w_in, gathered, skip, out_gain)


def head_lanes(pair):
    gap = jnp.zeros((2, 64 - HEADS), f32)
    return jnp.concatenate([pair, gap], axis=1).reshape(1, LANES)


def on_device(
    tokens, tile_mask, norm_gain, w_in, conv_weight, conv_bias, w_proj, dt_bias, decay_rate, skip_gain, out_gain, w_out
):
    both = ("row", "col")
    count_row, count_col = lax.axis_size("row"), lax.axis_size("col")
    row, col = lax.axis_index("row"), lax.axis_index("col")
    height, breadth, channels = tokens.shape
    local = height * breadth
    expand = conv_bias.shape[0]
    devices = count_row * count_col

    flags = jnp.broadcast_to(
        jnp.pad(tile_mask.reshape(1, -1).astype(bf16), ((0, 0), (0, LANES - tile_mask.size))),
        (w_out.shape[0], LANES),
    )
    gathered = lax.all_gather(
        jnp.concatenate([w_out, w_proj, flags], axis=1), both, axis=0, tiled=True
    )

    own = w_in.T
    weights = lax.all_to_all(
        jnp.broadcast_to(own[None], (devices,) + own.shape), both, 0, 0, tiled=True
    ).reshape(2 * expand, channels)

    above, below = shifted(tokens[-1:], "row", 1), shifted(tokens[:1], "row", -1)
    tall = jnp.concatenate([above, tokens, below], axis=0)
    before, after = shifted(tall[:, -1:], "col", 1), shifted(tall[:, :1], "col", -1)
    after_last = jnp.concatenate([jnp.zeros_like(after[:1]), after], axis=0)
    body = jnp.concatenate(
        [after_last[:-1], jnp.zeros((height + 2, 6, channels), bf16), before, tall], axis=1
    ).reshape((height + 2) * STRIDE, channels)
    x_ext = jnp.concatenate([body, after_last[-1], jnp.zeros((15, channels), bf16)], axis=0)

    act, turned = filtered(
        x_ext,
        norm_gain.reshape(1, -1),
        weights,
        conv_weight,
        conv_bias.reshape(1, -1),
        local,
    )

    marks = gathered[:: w_out.shape[0], channels + w_proj.shape[1] :][:, :2].astype(f32)
    marks = marks.reshape(count_row, count_col, 2)
    line = row * height + col
    mask_line = lax.dynamic_slice_in_dim(
        marks.transpose(0, 2, 1).reshape(2 * count_row, count_col), line // TILE, 1, axis=0
    )
    mask_line = jnp.pad(mask_line, ((0, 0), (0, LANES - count_col)))
    mask_column = lax.dynamic_slice_in_dim(marks, col, 1, axis=1).reshape(1, 2 * count_row)
    mask_column = jnp.pad(mask_column, ((0, 0), (0, LANES - 2 * count_row)))
    rate = decay_rate * LOG2E

    lines = lax.all_to_all(
        act.reshape(height, breadth, expand), "col", 0, 0, tiled=True
    ).reshape(count_col * breadth, expand)
    rows_out = swept_lines(
        lines, gathered, head_lanes(dt_bias[:2]), head_lanes(rate[:2]), mask_line
    )
    rows_back = lax.all_to_all(
        rows_out.reshape(count_col, breadth, expand), "col", 0, 0, tiled=True
    ).reshape(local, expand)

    columns = lax.all_to_all(
        turned.reshape(count_row, breadth // count_row * height, expand), "row", 0, 0, tiled=True
    ).reshape(count_row, breadth // count_row, height, expand)
    columns_out = swept_columns(
        columns, gathered, head_lanes(dt_bias[2:]), head_lanes(rate[2:]), mask_column
    )
    columns_back = lax.all_to_all(
        columns_out.reshape(count_row, breadth // count_row * height, expand),
        "row",
        0,
        0,
        tiled=True,
    ).reshape(local, expand)

    result = projected(
        act,
        rows_back,
        columns_back,
        tokens.reshape(local, channels),
        norm_gain.reshape(1, -1),
        weights,
        gathered,
        skip_gain.reshape(1, -1),
        out_gain.reshape(1, -1),
        height,
    )
    return result.reshape(height, breadth, channels)


def solution(mesh):
    placed = (
        P("row", "col", None),
        P("row", "col"),
        P(),
        P(None, ("row", "col")),
        P(),
        P(),
        P(("row", "col"), None),
        P(),
        P(),
        P(),
        P(),
        P(("row", "col"), None),
    )
    return jax.shard_map(
        on_device, mesh=mesh, in_specs=placed, out_specs=P("row", "col", None), check_vma=False
    )
```

time: 784 us -> 168 us (0.21); the launches traced: 770 us -> 168 us
  other arithmetic: 318 us -> 1.3 us
  local copies, waits for them, and re-layouts: 232 us -> 7.85 us
  matrix products: 97.2 us -> 0 us
  starting transfers between devices: 9.89 us -> 48.3 us
  Pallas kernels: 0 us -> 30.7 us
  blocking collectives: 63.5 us -> 41.9 us
  waiting for transfers between devices: 33.7 us -> 23.8 us
    select_n x72 -> x0, other arithmetic: 219 us -> none  [hop(): return jax.tree.map(lambda a, b: jnp.where(reached, a, b), new, before)]
    dot_general x20 -> x0, matrix products: 97.2 us -> none  [the longest x4 32 us: block_terms(): jnp.einsum('lbhts,lbshp->lbthp', mixing, values, preferred_element_type=j...]
    convert_element_type x81 -> x1, other arithmetic: 73.3 us -> 0.01 us  [on_device(): tile_mask.reshape(1, -1).astype(bf16)]
    all_gather x3 -> x0, blocking collectives: 63.5 us -> none  [the longest x1 42.3 us: on_device(): lax.all_gather(w_proj, ('row', 'col'), axis=0, tiled=True)]
    reshape x12 -> x5, local copies, waits for them, and re-layouts: 62.1 us -> 0.41 us  [the longest x4 0.33 us: head_lanes(): return jnp.concatenate([pair, gap], axis=1).reshape(1, LANES)]
    mul x15 -> x0, local copies, waits for them, and re-layouts: 55 us -> none  [the longest x8 49.8 us: block_terms(): values.astype(jnp.float32) * tail_weight[..., None]]
    all_to_all x0 -> x2, blocking collectives: none -> 41.9 us  [the longest x1 24.7 us: on_device(): lax.all_to_all(rows_out.reshape(count_col, breadth, expand), 'col', 0, 0,...]
    broadcast_in_dim x13 -> x4, local copies, waits for them, and re-layouts: 38.2 us -> 2.33 us  [the longest x1 2.32 us: on_device(): jnp.broadcast_to(own[None], (devices,) + own.shape)]
  transfers between devices with their start and end apart: 12 -> 8, of which waited for: 3 -> 6; matrix products, arithmetic and copies ran while one was open for 76% -> 2% of each run, Pallas kernels for 0% -> 14%
where the time goes in v1:
time: 168 us
  starting transfers between devices  48.3 us (29%)
  blocking collectives  41.9 us (25%)
  Pallas kernels  30.7 us (18%)
  waiting for transfers between devices  23.8 us (14%)
  between operations  13.8 us (8%)
  local copies, waits for them, and re-layouts  7.85 us (5%)
    all_to_all x1, blocking collectives, on_device(): lax.all_to_all(rows_out.reshape(count_col, breadth, expand), 'col', 0, 0,...  24.7 us
    ppermute x4, starting transfers between devices, shifted(): return lax.ppermute(x, axis, pairs)  21.1 us
    all_to_all x1, blocking collectives, on_device(): lax.all_to_all(turned.reshape(count_row, breadth // count_row * height, e...  17.2 us
    all_to_all x1, starting transfers between devices, on_device(): lax.all_to_all(jnp.broadcast_to(own[None], (devices,) + own.shape), both,...  11.5 us
    all_gather x1, waiting for transfers between devices, on_device(): lax.all_gather(jnp.concatenate([w_out, w_proj, flags], axis=1), both, axi...  11.1 us
    all_to_all x1, starting transfers between devices, on_device(): lax.all_to_all(act.reshape(height, breadth, expand), 'col', 0, 0, tiled=T...  11.1 us
    pallas_call x1, Pallas kernels, swept_lines(): pl.pallas_call(line_kernel, grid=(1,), in_specs=[pl.BlockSpec((length, ex...  8.51 us
    pallas_call x1, Pallas kernels, swept_columns(): pl.pallas_call(column_kernel, grid=(lines,), in_specs=[pl.BlockSpec((sour...  8.2 us
  transfers between devices with their start and end apart: 8, of which 6 were waited for; matrix products, arithmetic and copies ran while one was open for 2% of the time, Pallas kernels for 14%

profile of v1, /device:TPU:1, one launch (start us, length us, event | category | flops | bytes accessed | tf_op | source)
XLA Modules:
  0.0 167.6 jit_solution(11125092029003767646)
XLA Ops:
  6.5 2.3 %broadcast_in_dim.22 = bf16[128,16,512]{2,1,0:T(8,128)(2,1)} broadcast(bf16[16,512]{1,0:T(8,128)(2,1)} %bitcast.50), dimensions={1,2} | broadcast | bytes 2113536 | tf_op jit(solution)/shard_map/broadcast_in_dim | solution.py:365
  8.9 11.5 %all-to-all-start = ((bf16[128,16,512]{2,1,0:T(8,128)(2,1)}), bf16[128,16,512]{2,1,0:T(8,128)(2,1)S(1)}, u32[]{:S(2)}, u32[]{:S(2)}) async-start(bf16[128,16,512]{2,1,0:T(8,128)(2,1)} %broadcast_in_dim.22), calls=%async_computation | async-start | bytes 4194304 | tf_op jit(solution)/shard_map/all_to_all | solution.py:364
  20.4 0.0 all-gather.2.cloned.1.call-start
  20.5 0.6 maximum_maximum_fusion.1
  21.1 0.0 all-gather.2.cloned.1.call-update
  21.1 3.4 %collective-permute-start = (bf16[1,16,512]{2,1,0:T(8,128)(2,1)S(1)}, bf16[1,16,512]{2,1,0:T(8,128)(2,1)S(1)}, u32[]{:S(2)}, u32[]{:S(2)}) collective-permute-start(bf16[1,16,512]{2,1,0:T(8,128)(2,1)S(1)} %get-tuple-element.12), channel_id=1, source_target_pairs={{0,32},{32,64},{64,96},{1,33},{33,65},{65,97},{2,34},{34,66},{66,9... | collective-permute-start | bytes 49160 | tf_op jit(solution)/shard_map/ppermute | solution.py:29
  24.6 1.3 collective-permute-start.1
  25.9 0.0 collective-permute-done
  25.9 3.6 %collective-permute-done.1 = bf16[1,16,512]{2,1,0:T(8,128)(2,1)S(1)} collective-permute-done((bf16[1,16,512]{2,1,0:T(8,128)(2,1)S(1)}, bf16[1,16,512]{2,1,0:T(8,128)(2,1)S(1)}, u32[]{:S(2)}, u32[]{:S(2)}) %collective-permute-start.1) | collective-permute-done | bytes 16416 | tf_op jit(solution)/shard_map/ppermute | solution.py:29
  29.6 0.1 fusion
  29.7 0.0 copy-start.9
  29.7 0.0 copy-start.10
  29.7 0.0 copy-start.11
  29.7 10.9 %collective-permute-start.2 = (bf16[34,1,512]{2,1,0:T(2,128)(2,1)S(1)}, bf16[34,1,512]{2,1,0:T(2,128)(2,1)S(1)}, u32[]{:S(2)}, u32[]{:S(2)}) collective-permute-start(bf16[34,1,512]{2,1,0:T(2,128)(2,1)S(1)} %get-tuple-element.10), channel_id=1, source_target_pairs={{1,0},{2,1},{3,2},{4,3},{5,4},{6,5},{7,6},{8,7},{9,8},{10,9},{11,1... | collective-permute-start | bytes 104456 | tf_op jit(solution)/shard_map/ppermute | solution.py:29
  40.6 0.1 pad.27.clone
  40.7 0.1 pad.25.clone
  40.8 5.5 %collective-permute-start.3 = (bf16[34,1,512]{2,1,0:T(2,128)(2,1)S(1)}, bf16[34,1,512]{2,1,0:T(2,128)(2,1)S(1)}, u32[]{:S(2)}, u32[]{:S(2)}) collective-permute-start(bf16[34,1,512]{2,1,0:T(2,128)(2,1)S(1)} %get-tuple-element.9), channel_id=1, source_target_pairs={{0,1},{1,2},{2,3},{3,4},{4,5},{5,6},{6,7},{7,8},{8,9},{9,10},{10,1... | collective-permute-start | bytes 104456 | tf_op jit(solution)/shard_map/ppermute | solution.py:29
  46.3 0.3 collective-permute-done.2
  46.6 0.1 pad_slice_fusion
  46.7 1.0 collective-permute-done.3
  47.6 0.4 pad_maximum_fusion
  48.0 0.3 maximum_maximum_fusion.x_ref
  48.3 2.7 %all-to-all-done = bf16[128,16,512]{2,1,0:T(8,128)(2,1)S(1)} async-done(((bf16[128,16,512]{2,1,0:T(8,128)(2,1)}), bf16[128,16,512]{2,1,0:T(8,128)(2,1)S(1)}, u32[]{:S(2)}, u32[]{:S(2)}) %all-to-all-start) | async-done | bytes 2097184 | tf_op jit(solution)/shard_map/all_to_all | solution.py:364
  51.0 0.0 copy-done.9
  51.1 6.4 %norm_project_filter.1 = (bf16[512,1024]{1,0:T(8,128)(2,1)S(1)}, bf16[512,1024]{1,0:T(8,128)(2,1)S(1)}) custom-call(bf16[832,512]{1,0:T(8,128)(2,1)S(1)} %maximum_maximum_fusion.x_ref, f32[1,512]{1,0:T(1,128)S(1)} %bitcast.42, bf16[2048,512]{1,0:T(8,128)(2,1)S(1)} %bitcast.32, f32[9,1024]{1,0:T(8,128)S(1)} %copy-done.9, f32[1,1024]{1,0:T(1,128)S(1)} %bitcast.44), custom_call_target="tpu_custom_call" | custom-call | tf_op jit(solution)/shard_map/norm_project_filter/pallas_call | solution.py:91
  57.5 0.0 copy-start.16
  57.5 0.0 copy-start.17
  57.5 17.2 %all_to_all.25 = bf16[4,128,1024]{2,1,0:T(8,128)(2,1)S(1)} all-to-all(bf16[4,128,1024]{2,1,0:T(8,128)(2,1)S(1)} %bitcast.41), channel_id=1, replica_groups=mesh['row'=4,'col'=32] {'row'}, dimensions={0} | all-to-all | bytes 2097152 | tf_op jit(solution)/shard_map/all_to_all | solution.py:407
  74.8 0.0 copy-done
  74.8 11.1 %all-to-all-start.1 = ((bf16[32,16,1024]{2,1,0:T(8,128)(2,1)}), bf16[32,16,1024]{2,1,0:T(8,128)(2,1)S(1)}, u32[]{:S(2)}, u32[]{:S(2)}) async-start(bf16[32,16,1024]{2,1,0:T(8,128)(2,1)} %bitcast.38), calls=%async_computation.1 | async-start | bytes 2097152 | tf_op jit(solution)/shard_map/all_to_all | solution.py:397
  85.9 0.1 reshape.104.rate_ref
  86.0 0.1 reshape.103.bias_ref
  86.1 11.1 %all-gather.2.cloned.1.call-done.w_ref.wo_ref = bf16[1024,896]{1,0:T(8,128)(2,1)} async-done(((bf16[8,896]{1,0:T(8,128)(2,1)}), bf16[1024,896]{1,0:T(8,128)(2,1)}) %all-gather.2.cloned.1.call-update) | async-done | bytes 1835024 | tf_op jit(solution)/shard_map/all_gather | solution.py:359
  97.2 1.0 slice.44
  98.3 0.1 reshape.105
  98.4 1.5 copy-done.1
  99.9 8.2 %sweep_columns.1 = bf16[4,4,32,1024]{3,2,1,0:T(8,128)(2,1)S(1)} custom-call(bf16[4,4,32,1024]{3,2,1,0:T(8,128)(2,1)S(1)} %bitcast.36, bf16[1024,896]{1,0:T(8,128)(2,1)S(1)} %copy-done.1, f32[1,128]{1,0:T(1,128)S(1)} %reshape.103.bias_ref, f32[1,128]{1,0:T(1,128)S(1)} %reshape.104.rate_ref, f32[1,128]{1,0:T(1,128)S(1)} %pad.19.mask_ref), custom_call_target="tpu_custom_call" | custom-call | tf_op jit(solution)/shard_map/sweep_columns/pallas_call | solution.py:273
  108.1 1.0 copy-done.3
  109.0 0.0 all-to-all-done.1
  109.0 4.6 %all-to-all-start.4 = ((bf16[4,128,1024]{2,1,0:T(8,128)(2,1)}), bf16[4,128,1024]{2,1,0:T(8,128)(2,1)}, u32[]{:S(2)}, u32[]{:S(2)}) async-start(bf16[4,128,1024]{2,1,0:T(8,128)(2,1)} %bitcast.35), calls=%async_computation.4 | async-start | bytes 2097152 | tf_op jit(solution)/shard_map/all_to_all | solution.py:413
  113.7 0.1 reshape.95.rate_ref
  113.8 0.1 reshape.94.bias_ref
  113.8 0.1 copy.15
  114.0 8.5 %sweep_rows.1 = bf16[512,1024]{1,0:T(8,128)(2,1)S(1)} custom-call(bf16[512,1024]{1,0:T(8,128)(2,1)S(1)} %bitcast.34, bf16[1024,896]{1,0:T(8,128)(2,1)S(1)} %copy-done.2, f32[1,128]{1,0:T(1,128)S(1)} %reshape.94.bias_ref, f32[1,128]{1,0:T(1,128)S(1)} %reshape.95.rate_ref, f32[1,128]{1,0:T(1,128)S(1)} %pad.18.mask_ref), custom_call_target="tpu_custom_call" | custom-call | tf_op jit(solution)/shard_map/sweep_rows/pallas_call | solution.py:234
  122.5 1.0 copy-done.4
  123.5 5.0 %all-to-all-done.4 = bf16[4,128,1024]{2,1,0:T(8,128)(2,1)} async-done(((bf16[4,128,1024]{2,1,0:T(8,128)(2,1)}), bf16[4,128,1024]{2,1,0:T(8,128)(2,1)}, u32[]{:S(2)}, u32[]{:S(2)}) %all-to-all-start.4) | async-done | bytes 1048608 | tf_op jit(solution)/shard_map/all_to_all | solution.py:413
  128.5 24.7 %all_to_all.26 = bf16[32,16,1024]{2,1,0:T(8,128)(2,1)S(1)} all-to-all(bf16[32,16,1024]{2,1,0:T(8,128)(2,1)} %bitcast.37), channel_id=1, replica_groups=mesh['row'=4,'col'=32] {'col'}, dimensions={0} | all-to-all | bytes 2097152 | tf_op jit(solution)/shard_map/all_to_all | solution.py:403
  153.2 7.5 %gate_and_project.1 = bf16[512,512]{1,0:T(8,128)(2,1)} custom-call(bf16[512,1024]{1,0:T(8,128)(2,1)S(1)} %copy-done.6, bf16[512,1024]{1,0:T(8,128)(2,1)S(1)} %bitcast.39, bf16[512,1024]{1,0:T(8,128)(2,1)} %bitcast.19.columns_ref, bf16[512,512]{1,0:T(8,128)(2,1)S(1)} %bitcast.40, f32[1,512]{1,0:T(1,128)S(1)} %bitcast.43, bf16[2048,512]{1,0:T(8,128)(2,1)} %bitcast.33, ...), custom_call_target="tpu_custom_call" | custom-call | tf_op jit(solution)/shard_map/gate_and_project/pallas_call | solution.py:318
  (51 shorter events, 0.2 us)
Async XLA Ops:
  8.9 11.6 %copy-start.18 = (s32[2,1]{0,1:T(1,128)S(1)}, s32[2,1]{0,1:T(1,128)}, u32[]{:S(2)}) copy-start(s32[2,1]{0,1:T(1,128)} %param.13) | copy-start | bytes 28
  8.9 11.6 %copy-start.14 = (bf16[8,512]{1,0:T(8,128)(2,1)S(1)}, bf16[8,512]{1,0:T(8,128)(2,1)}, u32[]{:S(2)}) copy-start(bf16[8,512]{1,0:T(8,128)(2,1)} %param.23) | copy-start | bytes 24580
  8.9 11.6 %copy-start.15 = (bf16[8,256]{1,0:T(8,128)(2,1)S(1)}, bf16[8,256]{1,0:T(8,128)(2,1)}, u32[]{:S(2)}) copy-start(bf16[8,256]{1,0:T(8,128)(2,1)} %param.18) | copy-start | bytes 12292
  8.9 12.3 %copy-start.7 = (bf16[32,16,512]{2,1,0:T(8,128)(2,1)S(1)}, bf16[32,16,512]{2,1,0:T(8,128)(2,1)}, u32[]{:S(2)}) copy-start(bf16[32,16,512]{2,1,0:T(8,128)(2,1)} %param.12) | copy-start | bytes 1572868
  8.9 42.2 %all-to-all-start = ((bf16[128,16,512]{2,1,0:T(8,128)(2,1)}), bf16[128,16,512]{2,1,0:T(8,128)(2,1)S(1)}, u32[]{:S(2)}, u32[]{:S(2)}) async-start(bf16[128,16,512]{2,1,0:T(8,128)(2,1)} %broadcast_in_dim.22), calls=%async_computation | async-start | bytes 4194304 | tf_op jit(solution)/shard_map/all_to_all | solution.py:364
  20.4 76.8 %all-gather.2.cloned.1.call-start = ((), (), s32[]{:S(2)}) async-start(), calls=%async_computation.5 | async-start | bytes 1849344 | tf_op jit(solution)/shard_map/all_gather | solution.py:359
  21.1 4.7 %collective-permute-start = (bf16[1,16,512]{2,1,0:T(8,128)(2,1)S(1)}, bf16[1,16,512]{2,1,0:T(8,128)(2,1)S(1)}, u32[]{:S(2)}, u32[]{:S(2)}) collective-permute-start(bf16[1,16,512]{2,1,0:T(8,128)(2,1)S(1)} %get-tuple-element.12), channel_id=1, source_target_pairs={{0,32},{32,64},{64,96},{1,33},{33,65},{65,97},{2,34},{34,66},{66,9... | collective-permute-start | bytes 49160 | tf_op jit(solution)/shard_map/ppermute | solution.py:29
  24.6 5.0 %collective-permute-start.1 = (bf16[1,16,512]{2,1,0:T(8,128)(2,1)S(1)}, bf16[1,16,512]{2,1,0:T(8,128)(2,1)S(1)}, u32[]{:S(2)}, u32[]{:S(2)}) collective-permute-start(bf16[1,16,512]{2,1,0:T(8,128)(2,1)S(1)} %get-tuple-element.11), channel_id=1, source_target_pairs={{32,0},{64,32},{96,64},{33,1},{65,33},{97,65},{34,2},{66,34},{98,6... | collective-permute-start | bytes 49160 | tf_op jit(solution)/shard_map/ppermute | solution.py:29
  29.7 21.4 %copy-start.9 = (f32[9,1024]{1,0:T(8,128)S(1)}, f32[9,1024]{1,0:T(8,128)}, u32[]{:S(2)}) copy-start(f32[9,1024]{1,0:T(8,128)} %taps_ref.1) | copy-start | bytes 110596
  29.7 21.4 %copy-start.10 = (f32[512]{0:T(512)S(1)}, f32[512]{0:T(512)}, u32[]{:S(2)}) copy-start(f32[512]{0:T(512)} %param.14) | copy-start | bytes 6148
  29.7 21.3 %copy-start.11 = (f32[1024]{0:T(1024)S(1)}, f32[1024]{0:T(1024)}, u32[]{:S(2)}) copy-start(f32[1024]{0:T(1024)} %param.17) | copy-start | bytes 12292
  29.7 16.9 %collective-permute-start.2 = (bf16[34,1,512]{2,1,0:T(2,128)(2,1)S(1)}, bf16[34,1,512]{2,1,0:T(2,128)(2,1)S(1)}, u32[]{:S(2)}, u32[]{:S(2)}) collective-permute-start(bf16[34,1,512]{2,1,0:T(2,128)(2,1)S(1)} %get-tuple-element.10), channel_id=1, source_target_pairs={{1,0},{2,1},{3,2},{4,3},{5,4},{6,5},{7,6},{8,7},{9,8},{10,9},{11,1... | collective-permute-start | bytes 104456 | tf_op jit(solution)/shard_map/ppermute | solution.py:29
  40.8 6.8 %collective-permute-start.3 = (bf16[34,1,512]{2,1,0:T(2,128)(2,1)S(1)}, bf16[34,1,512]{2,1,0:T(2,128)(2,1)S(1)}, u32[]{:S(2)}, u32[]{:S(2)}) collective-permute-start(bf16[34,1,512]{2,1,0:T(2,128)(2,1)S(1)} %get-tuple-element.9), channel_id=1, source_target_pairs={{0,1},{1,2},{2,3},{3,4},{4,5},{5,6},{6,7},{7,8},{8,9},{9,10},{10,1... | collective-permute-start | bytes 104456 | tf_op jit(solution)/shard_map/ppermute | solution.py:29
  51.0 23.7 %copy-start = (bf16[128,16,512]{2,1,0:T(8,128)(2,1)}, bf16[128,16,512]{2,1,0:T(8,128)(2,1)S(1)}, u32[]{:S(2)}) copy-start(bf16[128,16,512]{2,1,0:T(8,128)(2,1)S(1)} %all-to-all-done) | copy-start | bytes 6291460
  57.5 17.3 %copy-start.5 = (bf16[512,1024]{1,0:T(8,128)(2,1)}, bf16[512,1024]{1,0:T(8,128)(2,1)S(1)}, u32[]{:S(2)}) copy-start(bf16[512,1024]{1,0:T(8,128)(2,1)S(1)} %get-tuple-element.7.act_ref) | copy-start | bytes 3145732
  57.5 28.4 %copy-start.16 = (f32[4,32]{1,0:T(4,128)S(1)}, f32[4,32]{1,0:T(4,128)}, u32[]{:S(2)}) copy-start(f32[4,32]{1,0:T(4,128)} %param.20) | copy-start | bytes 1540
  57.5 28.5 %copy-start.17 = (f32[4,32]{1,0:T(4,128)S(1)}, f32[4,32]{1,0:T(4,128)}, u32[]{:S(2)}) copy-start(f32[4,32]{1,0:T(4,128)} %param.19) | copy-start | bytes 1540
  74.8 34.3 %all-to-all-start.1 = ((bf16[32,16,1024]{2,1,0:T(8,128)(2,1)}), bf16[32,16,1024]{2,1,0:T(8,128)(2,1)S(1)}, u32[]{:S(2)}, u32[]{:S(2)}) async-start(bf16[32,16,1024]{2,1,0:T(8,128)(2,1)} %bitcast.38), calls=%async_computation.1 | async-start | bytes 2097152 | tf_op jit(solution)/shard_map/all_to_all | solution.py:397
  98.3 1.5 copy-start.1
  108.1 1.0 copy-start.3
  109.0 4.9 %copy-start.2 = (bf16[1024,896]{1,0:T(8,128)(2,1)S(1)}, bf16[1024,896]{1,0:T(8,128)(2,1)}, u32[]{:S(2)}) copy-start(bf16[1024,896]{1,0:T(8,128)(2,1)} %all-gather.2.cloned.1.call-done.w_ref.wo_ref) | copy-start | bytes 5505028
  109.0 19.5 %all-to-all-start.4 = ((bf16[4,128,1024]{2,1,0:T(8,128)(2,1)}), bf16[4,128,1024]{2,1,0:T(8,128)(2,1)}, u32[]{:S(2)}, u32[]{:S(2)}) async-start(bf16[4,128,1024]{2,1,0:T(8,128)(2,1)} %bitcast.35), calls=%async_computation.4 | async-start | bytes 2097152 | tf_op jit(solution)/shard_map/all_to_all | solution.py:413
  122.5 1.0 copy-start.4
  123.5 29.7 %copy-start.6 = (bf16[512,1024]{1,0:T(8,128)(2,1)S(1)}, bf16[512,1024]{1,0:T(8,128)(2,1)}, u32[]{:S(2)}) copy-start(bf16[512,1024]{1,0:T(8,128)(2,1)} %copy-done.5) | copy-start | bytes 3145732
  123.5 29.7 %copy-start.8 = (bf16[32,16,512]{2,1,0:T(8,128)(2,1)S(1)}, bf16[32,16,512]{2,1,0:T(8,128)(2,1)}, u32[]{:S(2)}) copy-start(bf16[32,16,512]{2,1,0:T(8,128)(2,1)} %param.12) | copy-start | bytes 1572868
  123.5 29.7 %copy-start.12 = (f32[1024]{0:T(1024)S(1)}, f32[1024]{0:T(1024)}, u32[]{:S(2)}) copy-start(f32[1024]{0:T(1024)} %param.21) | copy-start | bytes 12292
  123.5 29.7 %copy-start.13 = (f32[1024]{0:T(1024)S(1)}, f32[1024]{0:T(1024)}, u32[]{:S(2)}) copy-start(f32[1024]{0:T(1024)} %param.22) | copy-start | bytes 12292
Sparse Core Ops, SparseCore 0:
  24.1 73.0 all-gather.1

commit v2 on v1

v2 whole, which is shorter than its diff:
```python
import functools

import jax
import jax.numpy as jnp
from jax import lax
from jax.experimental import pallas as pl
from jax.experimental.pallas import tpu as pltpu
from jax.sharding import Mesh, PartitionSpec as P

STATE = 16
HEADS = 32
TILE = 16
CHUNK = 128
LANES = 128
STRIDE = 24
LOG2E = 1.4426950408889634
GRANT = 56 * 2**20

f32 = jnp.float32
bf16 = jnp.bfloat16


def dot(a, b, contract=((1,), (0,))):
    return lax.dot_general(a, b, (contract, ((), ())), preferred_element_type=f32)


def shifted(x, axis, step):
    count = lax.axis_size(axis)
    pairs = [(i, i + step) for i in range(count) if 0 <= i + step < count]
    return lax.ppermute(x, axis, pairs)


def diagonal(x, down, right):
    axes = ("row", "chip", "core")
    rows, columns = lax.axis_size("row"), lax.axis_size(("chip", "core"))
    pairs = [
        (r * columns + c, (r + down) * columns + c + right)
        for r in range(rows)
        for c in range(columns)
        if 0 <= r + down < rows and 0 <= c + right < columns
    ]
    return lax.ppermute(x, axes, pairs)


def here():
    return lax.axis_index("row"), 2 * lax.axis_index("chip") + lax.axis_index("core")


def normalized(x, gain):
    average = jnp.mean(x, axis=-1, keepdims=True)
    centered = x - average
    spread = jnp.mean(centered * centered, axis=-1, keepdims=True)
    return centered * lax.rsqrt(spread + 1e-05) * gain


def paired(own_ref, other_ref, core):
    own, other = own_ref[...].astype(f32), other_ref[...].astype(f32)
    return jnp.where(core == 0, own, other), jnp.where(core == 0, other, own)


def rows_of_eight(*pieces):
    count = pieces[0].shape[0] // 8
    parts = [p.reshape(count, 8, p.shape[1]) for p in pieces]
    return jnp.concatenate(parts, axis=1).reshape(-1, pieces[0].shape[1]).astype(bf16)


def input_weights(own_ref, other_ref, core):
    half = own_ref.shape[1] // 2
    even, odd = paired(own_ref, other_ref, core)
    return rows_of_eight(even[:, :half], even[:, half:], odd[:, :half], odd[:, half:])


def parcel_kernel(mask, in_ref, out_ref, proj_ref, parcel_ref):
    place = here()
    row = lax.broadcasted_iota(jnp.int32, (8, LANES), 0)
    lane = lax.broadcasted_iota(jnp.int32, (8, LANES), 1)
    flags = jnp.zeros((8, LANES), f32)
    for i in range(mask.shape[1]):
        flags = jnp.where(
            (row == i) & (lane == place[1]), mask[:, i : i + 1].astype(f32), flags
        )
    turned = in_ref[...].astype(f32)
    parts = [turned[:8], turned[8:], out_ref[...].astype(f32), proj_ref[...].astype(f32), flags]
    at = 0
    for part in parts:
        width = part.shape[1]
        parcel_ref[:, :, at : at + width] = jnp.broadcast_to(
            part.astype(bf16)[None], (parcel_ref.shape[0], 8, width)
        )
        at += width


def parcels(mask, turned, w_out, w_proj, groups):
    width = 2 * turned.shape[1] + w_out.shape[1] + w_proj.shape[1] + LANES
    block = 16
    one = lambda i: (0, 0)
    return pl.pallas_call(
        parcel_kernel,
        grid=(groups // block,),
        in_specs=[
            pl.BlockSpec(mask.shape, one),
            pl.BlockSpec(turned.shape, one),
            pl.BlockSpec(w_out.shape, one),
            pl.BlockSpec(w_proj.shape, one),
        ],
        out_specs=pl.BlockSpec((block, 8, width), lambda i: (i, 0, 0)),
        out_shape=jax.ShapeDtypeStruct((groups, 8, width), bf16),
        compiler_params=pltpu.CompilerParams(vmem_limit_bytes=GRANT),
        name="parcels",
    )(mask, turned, w_out, w_proj)


def filter_kernel(
    x_ref, gain_ref, own_ref, other_ref, taps_ref, bias_ref, act_ref, turned_ref, normed, branch, order
):
    place = here()
    padded = x_ref.shape[0]
    tokens, width = act_ref.shape
    height = padded // STRIDE - 2
    breadth = tokens // height

    @pl.when(pl.program_id(0) == 0)
    def _():
        step = 64
        for at in range(0, padded, step):
            x = x_ref[at : at + step, :].astype(f32)
            normed[at : at + step, :] = normalized(x, gain_ref[...]).astype(bf16)
        to = lax.broadcasted_iota(jnp.int32, (tokens, tokens), 0)
        source = lax.broadcasted_iota(jnp.int32, (tokens, tokens), 1)
        w, h = to // height, to % height
        order[...] = (source == h * breadth + w).astype(f32).astype(bf16)

    weights = input_weights(own_ref, other_ref, place[1] % 2)
    product = dot(normed[...], weights, ((1,), (1,)))
    branch[...] = product.astype(bf16).astype(f32)
    rows = 4
    span = rows * STRIDE + 8
    for lane in range(0, width, LANES):
        lanes = slice(lane, lane + LANES)
        taps = [taps_ref[k : k + 1, lanes] for k in range(9)]
        for h in range(0, height, rows):
            windows = [
                branch[(h + i) * STRIDE : (h + i) * STRIDE + span, lanes] for i in range(3)
            ]
            left, middle, right = [
                windows[0] * taps[j] + windows[1] * taps[3 + j] + windows[2] * taps[6 + j]
                for j in range(3)
            ]
            convolved = (
                middle
                + pltpu.roll(left, 1, 0)
                + pltpu.roll(right, span - 1, 0)
                + bias_ref[:, lanes]
            )
            activated = convolved / (1.0 + jnp.exp(-convolved))
            kept = activated[: rows * STRIDE].reshape(rows, STRIDE, LANES)[:, 8:, :]
            act_ref[h * breadth : (h + rows) * breadth, lanes] = kept.reshape(
                rows * breadth, LANES
            ).astype(bf16)
    turned_ref[...] = dot(order[...], act_ref[...]).astype(bf16)


def filtered(x, gain, own, other, taps, bias, tokens):
    expand = bias.shape[1]
    padded, channels = x.shape
    width = 256
    piece = pl.BlockSpec((width // 4, 2 * channels), lambda c: (c, 0))
    return pl.pallas_call(
        filter_kernel,
        grid=(expand // width,),
        in_specs=[
            pl.BlockSpec((padded, channels), lambda c: (0, 0)),
            pl.BlockSpec((1, channels), lambda c: (0, 0)),
            piece,
            piece,
            pl.BlockSpec((9, width), lambda c: (0, c)),
            pl.BlockSpec((1, width), lambda c: (0, c)),
        ],
        out_specs=[pl.BlockSpec((tokens, width), lambda c: (0, c))] * 2,
        out_shape=[jax.ShapeDtypeStruct((tokens, expand), bf16)] * 2,
        scratch_shapes=[
            pltpu.VMEM((padded, channels), bf16),
            pltpu.VMEM((padded, width), f32),
            pltpu.VMEM((tokens, tokens), bf16),
        ],
        compiler_params=pltpu.CompilerParams(vmem_limit_bytes=GRANT),
        cost_estimate=pl.CostEstimate(
            flops=2 * padded * channels * expand, bytes_accessed=6 * 2**20, transcendentals=tokens * expand
        ),
        name="norm_project_filter",
    )(x, gain, own, other, taps, bias)


def head_lanes(ref, first):
    heads = ref.shape[1]
    head = lax.broadcasted_iota(jnp.int32, (heads, LANES), 0)
    lane = lax.broadcasted_iota(jnp.int32, (heads, LANES), 1)
    placed = [
        lax.dot_general(
            ref[...],
            (lane == head + 64 * d).astype(f32),
            (((1,), (0,)), ((), ())),
            precision=lax.Precision.HIGHEST,
            preferred_element_type=f32,
        )
        for d in range(2)
    ]
    return placed[0][first : first + 1] + placed[1][first + 1 : first + 2]


def chunk_terms(values, w_proj, bias, rate, kept):
    coefs = dot(values, w_proj)
    at = lax.broadcasted_iota(jnp.int32, (CHUNK, LANES), 0)
    lane = lax.broadcasted_iota(jnp.int32, (CHUNK, LANES), 1)
    v = coefs + bias
    steps = kept * (jnp.maximum(v, 0.0) + jnp.log1p(jnp.exp(-jnp.abs(v))))
    decays = steps * rate
    lower = (lane <= at).astype(f32).astype(bf16)
    high = decays.astype(bf16)
    rest = decays - high.astype(f32)
    middle = rest.astype(bf16)
    low = (rest - middle.astype(f32)).astype(bf16)
    total = dot(lower, high) + (dot(lower, middle) + dot(lower, low))
    sums = jnp.where(lane < 64, total, total - decays)
    return coefs, steps, sums, total[CHUNK - 1 :, :]


def local_weights(coefs, span):
    at = lax.broadcasted_iota(jnp.int32, (CHUNK, CHUNK), 0)
    source = lax.broadcasted_iota(jnp.int32, (CHUNK, CHUNK), 1)
    c = coefs.astype(bf16)
    forward = dot(c[:, 48:64], c[:, 32:48], ((1,), (1,)))
    backward = dot(c[:, 112:128], c[:, 96:112], ((1,), (1,)))
    together = source // span == at // span
    return (
        source <= at,
        jnp.where((source <= at) & together, forward, 0.0).astype(bf16),
        jnp.where((source >= at) & together, backward, 0.0).astype(bf16),
    )


def local_tile(values, tile, weights, sums, sums_t, steps_t):
    causal, forward, backward = weights
    lane = lax.broadcasted_iota(jnp.int32, (CHUNK, LANES), 1)
    inputs = values[:, tile * LANES : (tile + 1) * LANES]
    mixing, sources = [], []
    for k in range(4):
        j = 4 * tile + k
        exponent = jnp.where(
            causal,
            sums_t[j : j + 1, :] - sums[:, j : j + 1],
            sums[:, 64 + j : 65 + j] - sums_t[64 + j : 65 + j, :],
        )
        scale = forward * steps_t[j : j + 1, :] + backward * steps_t[64 + j : 65 + j, :]
        mixing.append(jnp.exp2(exponent.astype(bf16)) * scale)
        sources.append(jnp.where(lane // 32 == k, inputs, jnp.zeros_like(inputs)))
    left = jnp.concatenate(mixing, axis=1)
    right = jnp.concatenate(sources, axis=0)
    return dot(left, right)


def line_kernel(
    a_ref, own_ref, other_ref, own_flags, other_flags, bias_ref, rate_ref, out_ref, coefs, steps, sums, ends, states, entering
):
    place = here()
    length, expand = a_ref.shape
    chunks = length // CHUNK
    lane = lax.broadcasted_iota(jnp.int32, (CHUNK, LANES), 1)
    spread = head_spread(expand)
    w_proj = rows_of_eight(*paired(own_ref, other_ref, place[1] % 2))
    bias, rate = head_lanes(bias_ref, 0), head_lanes(rate_ref, 0) * LOG2E
    flags = own_flags[...].astype(f32) + other_flags[...].astype(f32)
    line = lax.broadcasted_iota(jnp.int32, flags.shape, 0)
    mine = (line // (flags.shape[0] // 4) == place[0]) & (line % 8 == place[1] // TILE)
    mask = jnp.sum(jnp.where(mine, flags, 0.0), axis=0, keepdims=True)
    position = lax.broadcasted_iota(jnp.int32, (CHUNK, LANES), 0)
    for c in range(chunks):
        tile_at = lane == (position + c * CHUNK) // TILE
        kept = jnp.sum(jnp.where(tile_at, mask, 0.0), axis=1, keepdims=True)
        at = slice(c * CHUNK, (c + 1) * CHUNK)
        values = a_ref[at, :]
        k, s, q, end = chunk_terms(values, w_proj, bias, rate, kept)
        coefs[at, :], steps[at, :], sums[at, :] = k, s, q
        ends[8 * c : 8 * c + 8, :] = jnp.broadcast_to(end, (8, LANES))
        tail = (jnp.exp2(jnp.where(lane < 64, q - end, -q)) * s).astype(bf16)
        wide = values.astype(f32)
        for d in range(2):
            if (c == chunks - 1, c == 0)[d]:
                continue
            weighted = (wide * dot(tail, spread[d])).astype(bf16)
            write = k[:, 64 * d + 32 : 64 * d + 48].astype(bf16)
            states[d, c] = dot(write, weighted, ((0,), (0,)))
    fade = jnp.exp2(-ends[...])
    high = fade.astype(bf16)
    low = (fade - high.astype(f32)).astype(bf16)
    for d in range(2):
        decay = dot(high, spread[d]) + dot(low, spread[d])
        order = range(chunks) if d == 0 else range(chunks - 1, -1, -1)
        running = None
        for c in order:
            if running is not None:
                entering[d, c] = running.astype(bf16)
            if c == order[-1]:
                break
            new = states[d, c]
            if running is not None:
                new = new + running * decay[8 * c : 8 * c + 1, :]
            running = new
    for c in range(chunks):
        at = slice(c * CHUNK, (c + 1) * CHUNK)
        values = a_ref[at, :]
        k, q = coefs[at, :], sums[at, :]
        end = ends[8 * c : 8 * c + 1, :]
        q_t, steps_t = q.T, steps[at, :].T.astype(bf16)
        weights = local_weights(k, CHUNK)
        head_in = jnp.exp2(jnp.where(lane < 64, -q, q - end)).astype(bf16)
        read = k.astype(bf16)
        for tile in range(expand // LANES):
            lanes = slice(tile * LANES, (tile + 1) * LANES)
            total = local_tile(values, tile, weights, q, q_t, steps_t)
            for d in range(2):
                if (c == 0, c == chunks - 1)[d]:
                    continue
                carried = dot(read[:, 64 * d + 48 : 64 * d + 64], entering[d, c, :, lanes])
                total = total + dot(head_in, spread[d][:, lanes]) * carried
            out_ref[at, lanes] = total.astype(bf16)


def piece_specs(rows, *columns):
    return [pl.BlockSpec((rows, LANES), lambda i, c=c: (0, c)) for c in columns for _ in range(2)]


def swept_lines(values, own, other, bias, rate):
    length, expand = values.shape
    chunks = length // CHUNK
    small = pl.BlockSpec(bias.shape, lambda i: (0, 0))
    return pl.pallas_call(
        line_kernel,
        grid=(1,),
        in_specs=[
            pl.BlockSpec((length, expand), lambda i: (0, 0)),
            *piece_specs(own.shape[0], 12, 14),
            small,
            small,
        ],
        out_specs=pl.BlockSpec((length, expand), lambda i: (0, 0)),
        out_shape=jax.ShapeDtypeStruct((length, expand), bf16),
        scratch_shapes=[
            pltpu.VMEM((length, LANES), f32),
            pltpu.VMEM((length, LANES), f32),
            pltpu.VMEM((length, LANES), f32),
            pltpu.VMEM((8 * chunks, LANES), f32),
            pltpu.VMEM((2, chunks, STATE, expand), f32),
            pltpu.VMEM((2, chunks, STATE, expand), bf16),
        ],
        compiler_params=pltpu.CompilerParams(vmem_limit_bytes=GRANT),
        cost_estimate=pl.CostEstimate(
            flops=6 * 2**30, bytes_accessed=3 * 2**20, transcendentals=2**21
        ),
        name="sweep_rows",
    )(values, own, other, own, other, bias, rate)


def head_spread(expand):
    head = lax.broadcasted_iota(jnp.int32, (LANES, expand), 0)
    channel = lax.broadcasted_iota(jnp.int32, (LANES, expand), 1)
    return [(head == channel // 32 + 64 * d).astype(f32).astype(bf16) for d in range(2)]


def by_line(coefs, first, height):
    lines = CHUNK // height
    lane = lax.broadcasted_iota(jnp.int32, (LANES, lines * STATE), 0)
    to = lax.broadcasted_iota(jnp.int32, (LANES, lines * STATE), 1)
    copied = dot(coefs, (lane == first + to % STATE).astype(f32).astype(bf16))
    at = lax.broadcasted_iota(jnp.int32, copied.shape, 0)
    place = lax.broadcasted_iota(jnp.int32, copied.shape, 1)
    return jnp.where(at // height == place // STATE, copied, 0.0).astype(bf16)


def column_kernel(
    a_ref, own_ref, other_ref, own_flags, other_flags, bias_ref, rate_ref, coefs_ref, steps_ref, sums_ref, read_ref, *refs
):
    place = here()
    slots = len(refs) - 5
    slot_refs, (proj, kept_lanes, heads, spread, decays) = refs[:slots], refs[slots:]
    expand = a_ref.shape[1]
    groups = slots + 1
    states = slot_refs[0].shape[0] - 16
    group = pl.program_id(0)
    part = states // pl.num_programs(0)
    lines = part // STATE
    height = CHUNK // lines
    lane = lax.broadcasted_iota(jnp.int32, (CHUNK, LANES), 1)

    @pl.when(group == 0)
    def _():
        flags = (own_flags[...].astype(f32) + other_flags[...].astype(f32)).astype(bf16)
        to = lax.broadcasted_iota(jnp.int32, (CHUNK, flags.shape[0]), 0)
        source = lax.broadcasted_iota(jnp.int32, (CHUNK, flags.shape[0]), 1)
        mine = (source // (flags.shape[0] // groups) == place[0]) & (
            source % 8 == to % height // TILE
        )
        marks = dot(mine.astype(f32).astype(bf16), flags)
        kept = jnp.sum(jnp.where(lane == place[1], marks, 0.0), axis=1, keepdims=True)
        kept_lanes[...] = jnp.broadcast_to(kept, kept_lanes.shape)
        proj[...] = rows_of_eight(*paired(own_ref, other_ref, place[1] % 2))
        heads[0:1, :] = head_lanes(bias_ref, 2)
        heads[1:2, :] = head_lanes(rate_ref, 2) * LOG2E
        for d, matrix in enumerate(head_spread(expand)):
            spread[d] = matrix

    values = a_ref[...]
    k, s, q, _ = chunk_terms(values, proj[...], heads[0:1, :], heads[1:2, :], kept_lanes[...])
    coefs_ref[...], steps_ref[...], sums_ref[...] = k, s, q

    inclusive = q + jnp.where(lane < 64, 0.0, s * heads[1:2, :])
    starts, ends = [jnp.zeros((1, LANES), f32)], []
    for line in range(lines):
        ends.append(inclusive[(line + 1) * height - 1 : (line + 1) * height, :])
        starts.append(ends[-1])
    wide = lambda rows: jnp.concatenate(
        [jnp.broadcast_to(r, (height, LANES)) for r in rows], axis=0
    )
    start, end = wide(starts[:lines]), wide(ends)
    tail = (jnp.exp2(jnp.where(lane < 64, q - end, start - q)) * s).astype(bf16)
    enter = jnp.exp2(jnp.where(lane < 64, start - q, q - end))
    is_read = (lane % 64) >= 48
    read_ref[...] = jnp.where(is_read, k, enter).astype(bf16)
    fade = jnp.exp2(
        jnp.concatenate([a - b for a, b in zip(starts[:lines], ends)] + [jnp.zeros((8 - lines, LANES), f32)], axis=0)
    )
    high = fade.astype(bf16)
    low = (fade - high.astype(f32)).astype(bf16)
    writes = k.astype(bf16)
    inputs = values.astype(f32)
    totals, fades = [], []
    for d in range(2):
        weighted = (inputs * dot(tail, spread[d])).astype(bf16)
        write = by_line(writes, 64 * d + 32, height)
        totals.append(dot(write, weighted, ((0,), (0,))).astype(bf16))
        fades.append(dot(high, spread[d]) + dot(low, spread[d]))
    at = pl.ds(pl.multiple_of(group * part, part), part)
    for d, ref in enumerate(slot_refs):
        onward = place[0] + d + 1 < groups

        @pl.when(onward)
        def _():
            ref[at, :] = totals[0]
            decays[d, pl.ds(pl.multiple_of(group * 8, 8), 8), :] = fades[0]

        @pl.when(jnp.logical_not(onward))
        def _():
            ref[at, :] = totals[1]
            decays[d, pl.ds(pl.multiple_of(group * 8, 8), 8), :] = fades[1]

    @pl.when(group == pl.num_programs(0) - 1)
    def _():
        for d, ref in enumerate(slot_refs):
            rows = [decays[d, 8 * g : 8 * g + lines, :] for g in range(states // part)]
            ref[states:, :] = jnp.concatenate(rows, axis=0).astype(bf16)


def column_states(values, own, other, bias, rate, height, slots):
    tokens, expand = values.shape
    groups = tokens // CHUNK
    states = tokens // height * STATE
    small = pl.BlockSpec(bias.shape, lambda i: (0, 0))
    block = pl.BlockSpec((CHUNK, expand), lambda i: (i, 0))
    thin = pl.BlockSpec((CHUNK, LANES), lambda i: (i, 0))
    return pl.pallas_call(
        column_kernel,
        grid=(groups,),
        in_specs=[block, *piece_specs(own.shape[0], 13, 14), small, small],
        out_specs=[thin] * 4
        + [pl.BlockSpec((states + 16, expand), lambda i: (0, 0))] * (slots - 1),
        out_shape=[jax.ShapeDtypeStruct((tokens, LANES), f32)] * 3
        + [jax.ShapeDtypeStruct((tokens, LANES), bf16)]
        + [jax.ShapeDtypeStruct((states + 16, expand), bf16)] * (slots - 1),
        scratch_shapes=[
            pltpu.VMEM((expand, LANES), bf16),
            pltpu.VMEM((CHUNK, LANES), f32),
            pltpu.VMEM((8, LANES), f32),
            pltpu.VMEM((2, LANES, expand), bf16),
            pltpu.VMEM((slots - 1, 8 * groups, expand), f32),
        ],
        compiler_params=pltpu.CompilerParams(vmem_limit_bytes=GRANT),
        cost_estimate=pl.CostEstimate(
            flops=2**31, bytes_accessed=3 * 2**20, transcendentals=2**18
        ),
        name="column_states",
    )(values, own, other, own, other, bias, rate)


def mix_kernel(a_ref, coefs_ref, steps_ref, sums_ref, out_ref, *, height):
    values = a_ref[...]
    q = sums_ref[...]
    weights = local_weights(coefs_ref[...], height)
    q_t, steps_t = q.T, steps_ref[...].T.astype(bf16)
    for tile in range(a_ref.shape[1] // LANES):
        lanes = slice(tile * LANES, (tile + 1) * LANES)
        out_ref[:, lanes] = local_tile(values, tile, weights, q, q_t, steps_t).astype(bf16)


def mixed_columns(values, coefs, steps, sums, height):
    tokens, expand = values.shape
    block = pl.BlockSpec((CHUNK, expand), lambda i: (i, 0))
    thin = pl.BlockSpec((CHUNK, LANES), lambda i: (i, 0))
    return pl.pallas_call(
        functools.partial(mix_kernel, height=height),
        grid=(tokens // CHUNK,),
        in_specs=[block, thin, thin, thin],
        out_specs=block,
        out_shape=jax.ShapeDtypeStruct((tokens, expand), bf16),
        compiler_params=pltpu.CompilerParams(vmem_limit_bytes=GRANT),
        cost_estimate=pl.CostEstimate(
            flops=2**32, bytes_accessed=3 * 2**20, transcendentals=2**21
        ),
        name="mix_columns",
    )(values, coefs, steps, sums)


def entering_kernel(
    local_ref, read_ref, act_ref, skip_ref, x_ref, gain_ref, own_gate, other_gate, own_out, other_out, *refs
):
    place = here()
    slots = len(refs) - 5
    slot_refs, (part_ref, gate_ref, w_out_ref, w_gate, columns) = refs[:slots], refs[slots:]
    expand = local_ref.shape[1]
    states = slot_refs[0].shape[0] - 16
    groups = local_ref.shape[0] // CHUNK
    part = states // groups
    lines = part // STATE
    height = CHUNK // lines
    spread = head_spread(expand)
    row = place[0]
    decays = [ref[states:, :].astype(f32) for ref in slot_refs]
    for g in range(groups):
        at = slice(g * CHUNK, (g + 1) * CHUNK)
        total = local_ref[at, :].astype(f32)
        read = read_ref[at, :]
        for d in range(2):
            order = range(slots) if d == 0 else range(slots - 1, -1, -1)
            entering, product = [], [None] * lines
            sums = [jnp.zeros((STATE, expand), f32)] * lines
            for step, k in enumerate(order):
                reaches = row > step if d == 0 else row + step + 1 <= slots
                for line in range(lines):
                    at_state = g * part + line * STATE
                    state = slot_refs[k][at_state : at_state + STATE, :].astype(f32)
                    if product[line] is not None:
                        state = state * product[line]
                    sums[line] = sums[line] + jnp.where(reaches, state, 0.0)
                    fade = decays[k][g * lines + line : g * lines + line + 1, :]
                    product[line] = fade if product[line] is None else product[line] * fade
            entering = jnp.concatenate(sums, axis=0).astype(bf16)
            carried = dot(by_line(read, 64 * d + 48, height), entering)
            total = total + dot(read, spread[d]) * carried
        columns[at, :] = total.astype(bf16)
    w_gate[...] = input_weights(own_gate, other_gate, place[1] % 2)
    w_out_ref[...] = rows_of_eight(*paired(own_out, other_out, place[1] % 2))
    tokens = local_ref.shape[0]
    breadth = tokens // height
    for g in range(groups):
        at = slice(g * CHUNK, (g + 1) * CHUNK)
        to = lax.broadcasted_iota(jnp.int32, (CHUNK, tokens), 0) + g * CHUNK
        source = lax.broadcasted_iota(jnp.int32, (CHUNK, tokens), 1)
        w, h = source // height, source % height
        back = (to == h * breadth + w).astype(f32).astype(bf16)
        direct = skip_ref[...] * act_ref[at, :].astype(f32)
        part_ref[at, :] = dot(back, columns[...]) + direct
        normed = normalized(x_ref[at, :].astype(f32), gain_ref[...]).astype(bf16)
        gating = dot(normed, w_gate[...], ((1,), (1,))).astype(bf16).astype(f32)
        gate_ref[at, :] = gating / (1.0 + jnp.exp(-gating))


def entered(local, read, act, skip, x, gain, own, other, slots):
    tokens, expand = local.shape
    pairs, channels = own.shape[0], x.shape[1]
    whole = lambda x: pl.BlockSpec(x.shape, lambda i: (0, 0))
    gate = pl.BlockSpec((pairs // 2, 2 * channels), lambda i: (1, 0))
    last = pl.BlockSpec((pairs, channels), lambda i: (0, 2))
    shapes = [
        jax.ShapeDtypeStruct((tokens, expand), f32),
        jax.ShapeDtypeStruct((tokens, expand), f32),
        jax.ShapeDtypeStruct((expand, channels), bf16),
    ]
    return pl.pallas_call(
        entering_kernel,
        grid=(1,),
        in_specs=[whole(a) for a in (local, read, act, skip, x, gain)]
        + [gate, gate, last, last]
        + [whole(a) for a in slots],
        out_specs=[whole(a) for a in shapes],
        out_shape=shapes,
        scratch_shapes=[
            pltpu.VMEM((expand, channels), bf16),
            pltpu.VMEM((tokens, expand), bf16),
        ],
        compiler_params=pltpu.CompilerParams(vmem_limit_bytes=GRANT),
        cost_estimate=pl.CostEstimate(
            flops=2**32, bytes_accessed=12 * 2**20, transcendentals=2**19
        ),
        name="enter_columns",
    )(local, read, act, skip, x, gain, own, other, own, other, *slots)


def output_kernel(part_ref, gate_ref, rows_ref, x_ref, w_ref, out_gain_ref, out_ref):
    summed = part_ref[...] + rows_ref[...].astype(f32)
    mixed = (normalized(summed, out_gain_ref[...]) * gate_ref[...]).astype(bf16)
    out_ref[...] = (x_ref[...].astype(f32) + dot(mixed, w_ref[...])).astype(bf16)


def projected(part, gate, rows, x, w_out, out_gain):
    tokens, expand = part.shape
    channels = x.shape[1]
    block = 128
    one = lambda i: (0, 0)
    wide = pl.BlockSpec((block, expand), lambda i: (i, 0))
    narrow = pl.BlockSpec((block, channels), lambda i: (i, 0))
    return pl.pallas_call(
        output_kernel,
        grid=(tokens // block,),
        in_specs=[
            wide,
            wide,
            wide,
            narrow,
            pl.BlockSpec((expand, channels), one),
            pl.BlockSpec((1, expand), one),
        ],
        out_specs=narrow,
        out_shape=jax.ShapeDtypeStruct((tokens, channels), bf16),
        compiler_params=pltpu.CompilerParams(vmem_limit_bytes=GRANT),
        name="gate_and_project",
    )(part, gate, rows, x, w_out, out_gain)


def on_device(
    tokens, tile_mask, norm_gain, w_in, conv_weight, conv_bias, w_proj, dt_bias, decay_rate, skip_gain, out_gain, w_out
):
    wide = ("chip", "core")
    count_row, count_chip = lax.axis_size("row"), lax.axis_size("chip")
    height, breadth, channels = tokens.shape
    local = height * breadth
    expand = conv_bias.shape[0]

    groups = count_row * count_chip
    parcel = parcels(tile_mask.T, w_in.T, w_out, w_proj, groups)
    own = lax.all_to_all(parcel, ("row", "chip"), 0, 0, tiled=True)
    above, below = shifted(tokens[-1:], "row", 1), shifted(tokens[:1], "row", -1)
    tall = jnp.concatenate([above, tokens, below], axis=0)
    before, after = [
        jnp.concatenate(
            [
                diagonal(tokens[-1:, edge], 1, step),
                shifted(tokens[:, edge], wide, step),
                diagonal(tokens[:1, edge], -1, step),
            ],
            axis=0,
        )
        for edge, step in ((slice(breadth - 1, breadth), 1), (slice(0, 1), -1))
    ]
    after_last = jnp.concatenate([jnp.zeros_like(after[:1]), after], axis=0)
    body = jnp.concatenate(
        [after_last[:-1], jnp.zeros((height + 2, 6, channels), bf16), before, tall], axis=1
    ).reshape((height + 2) * STRIDE, channels)
    x_ext = jnp.concatenate([body, after_last[-1], jnp.zeros((15, channels), bf16)], axis=0)

    own, x_ext = lax.optimization_barrier((own, x_ext))
    other = lax.ppermute(own, "core", [(0, 1), (1, 0)])
    own, other = [p.reshape(groups * 8, p.shape[2]) for p in (own, other)]

    act, turned = filtered(
        x_ext,
        norm_gain.reshape(1, -1),
        own,
        other,
        conv_weight,
        conv_bias.reshape(1, -1),
        local,
    )
    def spun(piece, d):
        return lax.ppermute(piece, "row", [(i, (i + d) % count_row) for i in range(count_row)])

    def dealt(x):
        return lax.all_to_all(
            x.reshape(-1, breadth, expand), wide, 0, 0, tiled=True
        ).reshape(-1, expand)

    lines = dealt(act)
    coefs, steps, sums, read, *states = column_states(
        turned, own, other, dt_bias, decay_rate, height, count_row
    )
    received = [spun(piece, d + 1) for d, piece in enumerate(states)]
    columns_local = mixed_columns(turned, coefs, steps, sums, height)
    lines, columns_local = lax.optimization_barrier((lines, columns_local))
    rows_out = swept_lines(lines, own, other, dt_bias, decay_rate)
    rows_out, received = lax.optimization_barrier((rows_out, received))
    rows_back = dealt(rows_out)
    x = tokens.reshape(local, channels)
    part, gate, full_out = entered(
        columns_local,
        read,
        act,
        skip_gain.reshape(1, -1),
        x,
        norm_gain.reshape(1, -1),
        own,
        other,
        received,
    )
    result = projected(part, gate, rows_back, x, full_out, out_gain.reshape(1, -1))
    return result.reshape(height, breadth, channels)


def solution(mesh):
    rows, columns = mesh.devices.shape
    split = Mesh(mesh.devices.reshape(rows, columns // 2, 2), ("row", "chip", "core"))
    wide, all_axes = ("chip", "core"), ("row", "chip", "core")
    placed = (
        P("row", wide, None),
        P("row", wide),
        P(),
        P(None, all_axes),
        P(),
        P(),
        P(all_axes, None),
        P(),
        P(),
        P(),
        P(),
        P(all_axes, None),
    )
    return jax.shard_map(
        on_device, mesh=split, in_specs=placed, out_specs=P("row", wide, None), check_vma=False
    )
```

time: 168 us -> 140 us (0.83)
  blocking collectives: 41.9 us -> 0 us
  Pallas kernels: 30.7 us -> 53.4 us
  starting transfers between devices: 48.3 us -> 62.9 us
  between operations: 13.8 us -> 0.27 us
  waiting for transfers between devices: 23.8 us -> 17.5 us
  local copies, waits for them, and re-layouts: 7.85 us -> 3.73 us
    all_to_all x2 -> x0, blocking collectives: 41.9 us -> none  [the longest x1 24.7 us: on_device(): lax.all_to_all(rows_out.reshape(count_col, breadth, expand), 'col', 0, 0,...]
    pallas_call x2 -> x5, Pallas kernels: 15.7 us -> 34.6 us  [the longest x1 9.66 us: entered(): pl.pallas_call(entering_kernel, grid=(1,), in_specs=[whole(a) for a in (l...]
    ppermute x0 -> x8, starting transfers between devices: none -> 16.4 us  [the longest x4 9.87 us: diagonal(): return lax.ppermute(x, axes, pairs)]
    all_gather x1 -> x0, waiting for transfers between devices: 11.1 us -> none  [on_device(): lax.all_gather(jnp.concatenate([w_out, w_proj, flags], axis=1), both, axi...]
    ppermute x0 -> x8, waiting for transfers between devices: none -> 6.99 us  [the longest x1 3.6 us: on_device(): other = lax.ppermute(own, 'core', [(0, 1), (1, 0)])]
    broadcast_in_dim x2 -> x0, local copies, waits for them, and re-layouts: 2.32 us -> none  [the longest x1 2.32 us: on_device(): jnp.broadcast_to(own[None], (devices,) + own.shape)]
    pallas_call x1, Pallas kernels: 6.43 us -> 8.47 us  [filtered(): pl.pallas_call(filter_kernel, grid=(expand // width,), in_specs=[pl.Block...]
    ppermute x4, waiting for transfers between devices: 4.91 us -> 3.01 us  [shifted(): return lax.ppermute(x, axis, pairs)]
  transfers between devices with their start and end apart: 8 -> 15, of which waited for: 6 -> 4; matrix products, arithmetic and copies ran while one was open for 2% -> 1% of each run, Pallas kernels for 14% -> 26%
where the time goes in v2:
time: 140 us; the launch traced here: 139 us
  starting transfers between devices  62.9 us (45%)
  Pallas kernels  53.4 us (38%)
  waiting for transfers between devices  17.5 us (12%)
  local copies, waits for them, and re-layouts  3.73 us (3%)
  other arithmetic  1.67 us (1%)
    ppermute x4, starting transfers between devices, shifted(): return lax.ppermute(x, axis, pairs)  19.2 us
    all_to_all x2, starting transfers between devices, dealt(): lax.all_to_all(x.reshape(-1, breadth, expand), wide, 0, 0, tiled=True)  15.2 us
    all_to_all x1, starting transfers between devices, on_device(): own = lax.all_to_all(parcel, ('row', 'chip'), 0, 0, tiled=True)  12.1 us
    pallas_call x1, Pallas kernels, swept_lines(): pl.pallas_call(line_kernel, grid=(1,), in_specs=[pl.BlockSpec((length, ex...  10.3 us
    ppermute x4, starting transfers between devices, diagonal(): return lax.ppermute(x, axes, pairs)  9.87 us
    pallas_call x1, Pallas kernels, entered(): pl.pallas_call(entering_kernel, grid=(1,), in_specs=[whole(a) for a in (l...  9.66 us
    pallas_call x1, Pallas kernels, filtered(): pl.pallas_call(filter_kernel, grid=(expand // width,), in_specs=[pl.Block...  8.47 us
    pallas_call x1, Pallas kernels, column_states(): pl.pallas_call(column_kernel, grid=(groups,), in_specs=[block, *piece_spe...  8.36 us
  transfers between devices with their start and end apart: 15, of which 4 were waited for; matrix products, arithmetic and copies ran while one was open for 1% of the time, Pallas kernels for 26%

profile of v2, /device:TPU:1, one launch (start us, length us, event | category | flops | bytes accessed | tf_op | source)
XLA Modules:
  0.0 139.5 jit_solution(15002402463402652767)
XLA Ops:
  0.0 2.7 %parcels.1 = bf16[64,8,1920]{2,1,0:T(8,128)(2,1)} custom-call(s32[1,2]{1,0:T(1,128)} %bitcast.50, bf16[16,512]{1,0:T(8,128)(2,1)} %bitcast.44, bf16[8,512]{1,0:T(8,128)(2,1)} %out_ref.1, bf16[8,256]{1,0:T(8,128)(2,1)} %proj_ref.1), custom_call_target="tpu_custom_call" | custom-call | tf_op jit(solution)/shard_map/parcels/pallas_call | solution.py:97
  2.7 12.1 %all-to-all-start = ((bf16[64,8,1920]{2,1,0:T(8,128)(2,1)}), bf16[64,8,1920]{2,1,0:T(8,128)(2,1)S(1)}, u32[]{:S(2)}, u32[]{:S(2)}) async-start(bf16[64,8,1920]{2,1,0:T(8,128)(2,1)} %parcels.1), calls=%async_computation | async-start | bytes 3932160 | tf_op jit(solution)/shard_map/all_to_all | solution.py:649
  14.8 4.0 %collective-permute-start = (bf16[1,1,512]{2,0,1:T(2,128)(2,1)S(1)}, bf16[1,1,512]{2,0,1:T(2,128)(2,1)S(1)}, u32[]{:S(2)}, u32[]{:S(2)}) collective-permute-start(bf16[1,1,512]{2,0,1:T(2,128)(2,1)S(1)} %get-tuple-element.45), channel_id=1, source_target_pairs={{1,32},{2,33},{3,34},{4,35},{5,36},{6,37},{7,38},{8,39},{9,40},{10... | collective-permute-start | bytes 3080 | tf_op jit(solution)/shard_map/ppermute | solution.py:42
  18.9 3.2 %collective-permute-start.2 = (bf16[1,1,512]{2,0,1:T(2,128)(2,1)S(1)}, bf16[1,1,512]{2,0,1:T(2,128)(2,1)S(1)}, u32[]{:S(2)}, u32[]{:S(2)}) collective-permute-start(bf16[1,1,512]{2,0,1:T(2,128)(2,1)S(1)} %get-tuple-element.46), channel_id=1, source_target_pairs={{0,33},{1,34},{2,35},{3,36},{4,37},{5,38},{6,39},{7,40},{8,41},{9,... | collective-permute-start | bytes 3080 | tf_op jit(solution)/shard_map/ppermute | solution.py:42
  22.1 1.3 collective-permute-start.4
  23.4 1.3 collective-permute-start.7
  24.7 0.1 fusion
  24.8 1.9 %collective-permute-start.1 = (bf16[32,1,512]{2,0,1:T(8,128)(2,1)S(1)}, bf16[32,1,512]{2,0,1:T(8,128)(2,1)S(1)}, u32[]{:S(2)}, u32[]{:S(2)}) collective-permute-start(bf16[32,1,512]{2,0,1:T(8,128)(2,1)S(1)} %copy.21), channel_id=1, source_target_pairs={{1,0},{2,1},{3,2},{4,3},{5,4},{6,5},{7,6},{8,7},{9,8},{10,9},{11,1... | collective-permute-start | bytes 98312 | tf_op jit(solution)/shard_map/ppermute | solution.py:30
  26.8 0.1 pad.4.clone
  26.9 0.1 pad.2.clone
  27.0 0.0 collective-permute-done
  27.0 14.1 %collective-permute-start.5 = (bf16[1,16,512]{2,1,0:T(8,128)(2,1)S(1)}, bf16[1,16,512]{2,1,0:T(8,128)(2,1)S(1)}, u32[]{:S(2)}, u32[]{:S(2)}) collective-permute-start(bf16[1,16,512]{2,1,0:T(8,128)(2,1)S(1)} %get-tuple-element.51), channel_id=1, source_target_pairs={{0,32},{32,64},{64,96},{1,33},{33,65},{65,97},{2,34},{34,66},{66,9... | collective-permute-start | bytes 49160 | tf_op jit(solution)/shard_map/ppermute | solution.py:30
  41.0 0.0 collective-permute-done.1
  41.0 1.9 %collective-permute-start.3 = (bf16[32,1,512]{2,0,1:T(8,128)(2,1)S(1)}, bf16[32,1,512]{2,0,1:T(8,128)(2,1)S(1)}, u32[]{:S(2)}, u32[]{:S(2)}) collective-permute-start(bf16[32,1,512]{2,0,1:T(8,128)(2,1)S(1)} %copy.23), channel_id=1, source_target_pairs={{0,1},{1,2},{2,3},{3,4},{4,5},{5,6},{6,7},{7,8},{8,9},{9,10},{10,1... | collective-permute-start | bytes 98312 | tf_op jit(solution)/shard_map/ppermute | solution.py:30
  43.0 0.1 pad_maximum_fusion
  43.1 0.0 collective-permute-done.2
  43.1 1.3 collective-permute-start.6
  44.4 0.0 collective-permute-done.4
  44.4 0.0 collective-permute-done.3
  44.4 0.1 copy.19
  44.5 0.1 copy.18
  44.5 0.0 collective-permute-done.5
  44.5 3.0 %collective-permute-done.6 = bf16[1,16,512]{2,1,0:T(8,128)(2,1)S(1)} collective-permute-done((bf16[1,16,512]{2,1,0:T(8,128)(2,1)S(1)}, bf16[1,16,512]{2,1,0:T(8,128)(2,1)S(1)}, u32[]{:S(2)}, u32[]{:S(2)}) %collective-permute-start.6) | collective-permute-done | bytes 16416 | tf_op jit(solution)/shard_map/ppermute | solution.py:30
  47.5 0.4 maximum_maximum_fusion.1
  48.0 0.0 collective-permute-done.7
  48.0 1.2 maximum_maximum_fusion.x_ref
  49.1 0.0 all-to-all-done
  49.1 1.6 %collective-permute-start.8 = (bf16[64,8,1920]{2,1,0:T(8,128)(2,1)S(1)}, bf16[64,8,1920]{2,1,0:T(8,128)(2,1)S(1)}, u32[]{:S(2)}, u32[]{:S(2)}) collective-permute-start(bf16[64,8,1920]{2,1,0:T(8,128)(2,1)S(1)} %all-to-all-done), channel_id=1, source_target_pairs={{0,1},{1,0},{2,3},{3,2},{4,5},{5,4},{6,7},{7,6},{8,9},{9,8},{10,11... | collective-permute-start | bytes 5898248 | tf_op jit(solution)/shard_map/ppermute | solution.py:670
  50.8 3.6 %collective-permute-done.8 = bf16[64,8,1920]{2,1,0:T(8,128)(2,1)S(1)} collective-permute-done((bf16[64,8,1920]{2,1,0:T(8,128)(2,1)S(1)}, bf16[64,8,1920]{2,1,0:T(8,128)(2,1)S(1)}, u32[]{:S(2)}, u32[]{:S(2)}) %collective-permute-start.8) | collective-permute-done | bytes 1966112 | tf_op jit(solution)/shard_map/ppermute | solution.py:670
  54.4 1.3 copy-done.1
  55.7 8.5 %norm_project_filter.1 = (bf16[512,1024]{1,0:T(8,128)(2,1)}, bf16[512,1024]{1,0:T(8,128)(2,1)}) custom-call(bf16[832,512]{1,0:T(8,128)(2,1)} %maximum_maximum_fusion.x_ref, f32[1,512]{1,0:T(1,128)} %bitcast.47, bf16[512,1920]{1,0:T(8,128)(2,1)} %bitcast.23, bf16[512,1920]{1,0:T(8,128)(2,1)} %bitcast.30, f32[9,1024]{1,0:T(8,128)} %taps_ref.1, f32[1,1024]{1,0:T(1,128)} %bitcast.45), custom_call_target="tpu_custom_call" | custom-call | flops 872415232 | bytes 6291456 | tf_op jit(solution)/shard_map/norm_project_filter/pallas_call | solution.py:168
  64.2 6.9 %all-to-all-start.1 = ((bf16[32,16,1024]{2,1,0:T(8,128)(2,1)}), bf16[32,16,1024]{2,1,0:T(8,128)(2,1)S(1)}, u32[]{:S(2)}, u32[]{:S(2)}) async-start(bf16[32,16,1024]{2,1,0:T(8,128)(2,1)} %bitcast.41), calls=%async_computation.1 | async-start | bytes 2097152 | tf_op jit(solution)/shard_map/all_to_all | solution.py:686
  71.1 8.4 %column_states.1 = (f32[512,128]{1,0:T(8,128)}, f32[512,128]{1,0:T(8,128)}, f32[512,128]{1,0:T(8,128)}, bf16[512,128]{1,0:T(8,128)(2,1)}, bf16[272,1024]{1,0:T(8...) custom-call(bf16[512,1024]{1,0:T(8,128)(2,1)} %get-tuple-element.28.a_ref, bf16[512,1920]{1,0:T(8,128)(2,1)} %bitcast.24, ...), custom_call_target="tpu_custom_call" | custom-call | flops 2147483648 | bytes 3145728 | tf_op jit(solution)/shard_map/column_states/pallas_call | solution.py:470
  79.5 1.2 collective-permute-start.9
  80.7 1.7 %collective-permute-start.10 = (bf16[272,1024]{1,0:T(8,128)(2,1)}, bf16[272,1024]{1,0:T(8,128)(2,1)S(1)}, u32[]{:S(2)}, u32[]{:S(2)}) collective-permute-start(bf16[272,1024]{1,0:T(8,128)(2,1)} %get-tuple-element.36), channel_id=1, source_target_pairs={{0,64},{32,96},{64,0},{96,32},{1,65},{33,97},{65,1},{97,33},{2,66}... | collective-permute-start | bytes 1671176 | tf_op jit(solution)/shard_map/ppermute | solution.py:683
  82.4 2.0 %collective-permute-start.11 = (bf16[272,1024]{1,0:T(8,128)(2,1)}, bf16[272,1024]{1,0:T(8,128)(2,1)S(1)}, u32[]{:S(2)}, u32[]{:S(2)}) collective-permute-start(bf16[272,1024]{1,0:T(8,128)(2,1)} %get-tuple-element.37), channel_id=1, source_target_pairs={{0,96},{32,0},{64,32},{96,64},{1,97},{33,1},{65,33},{97,65},{2,98}... | collective-permute-start | bytes 1671176 | tf_op jit(solution)/shard_map/ppermute | solution.py:683
  84.4 8.2 %mix_columns.1.local_ref = bf16[512,1024]{1,0:T(8,128)(2,1)} custom-call(bf16[512,1024]{1,0:T(8,128)(2,1)} %get-tuple-element.28.a_ref, f32[512,128]{1,0:T(8,128)} %get-tuple-element.29.coefs_ref, f32[512,128]{1,0:T(8,128)} %get-tuple-element.30.steps_ref, f32[512,128]{1,0:T(8,128)} %get-tuple-element.31.sums_ref), custom_call_target="tpu_custom_call" | custom-call | flops 4294967296 | bytes 3145728 | tf_op jit(solution)/shard_map/mix_columns/pallas_call | solution.py:508
  92.6 0.0 all-to-all-done.1
  92.6 1.0 copy-done.4
  93.6 10.3 %sweep_rows.1 = bf16[512,1024]{1,0:T(8,128)(2,1)} custom-call(bf16[512,1024]{1,0:T(8,128)(2,1)} %bitcast.42, bf16[512,1920]{1,0:T(8,128)(2,1)} %bitcast.26, bf16[512,1920]{1,0:T(8,128)(2,1)} %bitcast.33, bf16[512,1920]{1,0:T(8,128)(2,1)} %bitcast.27, bf16[512,1920]{1,0:T(8,128)(2,1)} %bitcast.34, f32[4,32]{1,0:T(4,128)} %bias_ref.3, f32[4,32]{1,0:T(4,128)} %rate_ref.3), custom_call_target="tpu_custom_call" | custom-call | flops 6442450944 | bytes 3145728 | tf_op jit(solution)/shard_map/sweep_rows/pallas_call | solution.py:337
  103.9 0.0 collective-permute-done.9.refs_0_
  103.9 3.4 %collective-permute-done.10.refs_1_ = bf16[272,1024]{1,0:T(8,128)(2,1)S(1)} collective-permute-done((bf16[272,1024]{1,0:T(8,128)(2,1)}, bf16[272,1024]{1,0:T(8,128)(2,1)S(1)}, u32[]{:S(2)}, u32[]{:S(2)}) %collective-permute-start.10) | collective-permute-done | bytes 557088 | tf_op jit(solution)/shard_map/ppermute | solution.py:683
  107.3 0.0 collective-permute-done.11.refs_2_
  107.3 8.3 %all-to-all-start.2 = ((bf16[32,16,1024]{2,1,0:T(8,128)(2,1)}), bf16[32,16,1024]{2,1,0:T(8,128)(2,1)S(1)}, u32[]{:S(2)}, u32[]{:S(2)}) async-start(bf16[32,16,1024]{2,1,0:T(8,128)(2,1)} %bitcast.43), calls=%async_computation.2 | async-start | bytes 2097152 | tf_op jit(solution)/shard_map/all_to_all | solution.py:686
  115.6 9.7 %enter_columns.1 = (f32[512,1024]{1,0:T(8,128)}, f32[512,1024]{1,0:T(8,128)}, bf16[1024,512]{1,0:T(8,128)(2,1)}) custom-call(bf16[512,1024]{1,0:T(8,128)(2,1)} %mix_columns.1.local_ref, bf16[512,128]{1,0:T(8,128)(2,1)} %get-tuple-element.33.read_ref, bf16[512,1024]{1,0:T(8,128)(2,1)} %get-tuple-element.27.act_ref, f32[1,1024]{1,0:T(1,128)} %bitcast.51, ...), custom_call_target="tpu_custom_call" | custom-call | flops 4294967296 | bytes 12582912 | tf_op jit(solution)/shard_map/enter_columns/pallas_call | solution.py:587
  125.3 7.5 %all-to-all-done.2 = bf16[32,16,1024]{2,1,0:T(8,128)(2,1)S(1)} async-done(((bf16[32,16,1024]{2,1,0:T(8,128)(2,1)}), bf16[32,16,1024]{2,1,0:T(8,128)(2,1)S(1)}, u32[]{:S(2)}, u32[]{:S(2)}) %all-to-all-start.2) | async-done | bytes 1048608 | tf_op jit(solution)/shard_map/all_to_all | solution.py:686
  132.8 1.0 copy-done.2
  133.8 5.7 %gate_and_project.1 = bf16[512,512]{1,0:T(8,128)(2,1)} custom-call(f32[512,1024]{1,0:T(8,128)} %get-tuple-element.41.part_ref, f32[512,1024]{1,0:T(8,128)} %get-tuple-element.42.gate_ref, bf16[512,1024]{1,0:T(8,128)(2,1)} %bitcast.37, bf16[512,512]{1,0:T(8,128)(2,1)} %bitcast.40, bf16[1024,512]{1,0:T(8,128)(2,1)} %get-tuple-element.44.w_ref, f32[1,1024]{1,0:T(1,128)} %bitcast.46), custom_call_target="tpu_custom_call" | custom-call | tf_op jit(solution)/shard_map/gate_and_project/pallas_call | solution.py:620
  (21 shorter events, 0.1 us)
Async XLA Ops:
  2.7 12.1 %copy-start.3 = (bf16[32,16,512]{2,1,0:T(8,128)(2,1)S(1)}, bf16[32,16,512]{2,1,0:T(8,128)(2,1)}, u32[]{:S(2)}) copy-start(bf16[32,16,512]{2,1,0:T(8,128)(2,1)} %param.12) | copy-start | bytes 1572868
  2.7 46.5 %all-to-all-start = ((bf16[64,8,1920]{2,1,0:T(8,128)(2,1)}), bf16[64,8,1920]{2,1,0:T(8,128)(2,1)S(1)}, u32[]{:S(2)}, u32[]{:S(2)}) async-start(bf16[64,8,1920]{2,1,0:T(8,128)(2,1)} %parcels.1), calls=%async_computation | async-start | bytes 3932160 | tf_op jit(solution)/shard_map/all_to_all | solution.py:649
  14.8 12.2 %collective-permute-start = (bf16[1,1,512]{2,0,1:T(2,128)(2,1)S(1)}, bf16[1,1,512]{2,0,1:T(2,128)(2,1)S(1)}, u32[]{:S(2)}, u32[]{:S(2)}) collective-permute-start(bf16[1,1,512]{2,0,1:T(2,128)(2,1)S(1)} %get-tuple-element.45), channel_id=1, source_target_pairs={{1,32},{2,33},{3,34},{4,35},{5,36},{6,37},{7,38},{8,39},{9,40},{10... | collective-permute-start | bytes 3080 | tf_op jit(solution)/shard_map/ppermute | solution.py:42
  18.9 24.2 %collective-permute-start.2 = (bf16[1,1,512]{2,0,1:T(2,128)(2,1)S(1)}, bf16[1,1,512]{2,0,1:T(2,128)(2,1)S(1)}, u32[]{:S(2)}, u32[]{:S(2)}) collective-permute-start(bf16[1,1,512]{2,0,1:T(2,128)(2,1)S(1)} %get-tuple-element.46), channel_id=1, source_target_pairs={{0,33},{1,34},{2,35},{3,36},{4,37},{5,38},{6,39},{7,40},{8,41},{9,... | collective-permute-start | bytes 3080 | tf_op jit(solution)/shard_map/ppermute | solution.py:42
  22.1 22.3 %collective-permute-start.4 = (bf16[1,1,512]{2,0,1:T(2,128)(2,1)S(1)}, bf16[1,1,512]{2,0,1:T(2,128)(2,1)S(1)}, u32[]{:S(2)}, u32[]{:S(2)}) collective-permute-start(bf16[1,1,512]{2,0,1:T(2,128)(2,1)S(1)} %get-tuple-element.47), channel_id=1, source_target_pairs={{32,1},{33,2},{34,3},{35,4},{36,5},{37,6},{38,7},{39,8},{40,9},{41... | collective-permute-start | bytes 3080 | tf_op jit(solution)/shard_map/ppermute | solution.py:42
  23.4 24.6 %collective-permute-start.7 = (bf16[1,1,512]{2,1,0:T(2,128)(2,1)S(1)}, bf16[1,1,512]{2,1,0:T(2,128)(2,1)S(1)}, u32[]{:S(2)}, u32[]{:S(2)}) collective-permute-start(bf16[1,1,512]{2,1,0:T(2,128)(2,1)S(1)} %get-tuple-element.48), channel_id=1, source_target_pairs={{33,0},{34,1},{35,2},{36,3},{37,4},{38,5},{39,6},{40,7},{41,8},{42... | collective-permute-start | bytes 3080 | tf_op jit(solution)/shard_map/ppermute | solution.py:42
  24.8 16.2 %collective-permute-start.1 = (bf16[32,1,512]{2,0,1:T(8,128)(2,1)S(1)}, bf16[32,1,512]{2,0,1:T(8,128)(2,1)S(1)}, u32[]{:S(2)}, u32[]{:S(2)}) collective-permute-start(bf16[32,1,512]{2,0,1:T(8,128)(2,1)S(1)} %copy.21), channel_id=1, source_target_pairs={{1,0},{2,1},{3,2},{4,3},{5,4},{6,5},{7,6},{8,7},{9,8},{10,9},{11,1... | collective-permute-start | bytes 98312 | tf_op jit(solution)/shard_map/ppermute | solution.py:30
  27.0 17.6 %collective-permute-start.5 = (bf16[1,16,512]{2,1,0:T(8,128)(2,1)S(1)}, bf16[1,16,512]{2,1,0:T(8,128)(2,1)S(1)}, u32[]{:S(2)}, u32[]{:S(2)}) collective-permute-start(bf16[1,16,512]{2,1,0:T(8,128)(2,1)S(1)} %get-tuple-element.51), channel_id=1, source_target_pairs={{0,32},{32,64},{64,96},{1,33},{33,65},{65,97},{2,34},{34,66},{66,9... | collective-permute-start | bytes 49160 | tf_op jit(solution)/shard_map/ppermute | solution.py:30
  41.0 3.3 %collective-permute-start.3 = (bf16[32,1,512]{2,0,1:T(8,128)(2,1)S(1)}, bf16[32,1,512]{2,0,1:T(8,128)(2,1)S(1)}, u32[]{:S(2)}, u32[]{:S(2)}) collective-permute-start(bf16[32,1,512]{2,0,1:T(8,128)(2,1)S(1)} %copy.23), channel_id=1, source_target_pairs={{0,1},{1,2},{2,3},{3,4},{4,5},{5,6},{6,7},{7,8},{8,9},{9,10},{10,1... | collective-permute-start | bytes 98312 | tf_op jit(solution)/shard_map/ppermute | solution.py:30
  43.1 4.5 %collective-permute-start.6 = (bf16[1,16,512]{2,1,0:T(8,128)(2,1)S(1)}, bf16[1,16,512]{2,1,0:T(8,128)(2,1)S(1)}, u32[]{:S(2)}, u32[]{:S(2)}) collective-permute-start(bf16[1,16,512]{2,1,0:T(8,128)(2,1)S(1)} %get-tuple-element.52), channel_id=1, source_target_pairs={{32,0},{64,32},{96,64},{33,1},{65,33},{97,65},{34,2},{66,34},{98,6... | collective-permute-start | bytes 49160 | tf_op jit(solution)/shard_map/ppermute | solution.py:30
  49.1 5.3 %copy-start = (bf16[64,8,1920]{2,1,0:T(8,128)(2,1)}, bf16[64,8,1920]{2,1,0:T(8,128)(2,1)S(1)}, u32[]{:S(2)}) copy-start(bf16[64,8,1920]{2,1,0:T(8,128)(2,1)S(1)} %all-to-all-done) | copy-start | bytes 5898244
  49.1 5.2 %collective-permute-start.8 = (bf16[64,8,1920]{2,1,0:T(8,128)(2,1)S(1)}, bf16[64,8,1920]{2,1,0:T(8,128)(2,1)S(1)}, u32[]{:S(2)}, u32[]{:S(2)}) collective-permute-start(bf16[64,8,1920]{2,1,0:T(8,128)(2,1)S(1)} %all-to-all-done), channel_id=1, source_target_pairs={{0,1},{1,0},{2,3},{3,2},{4,5},{5,4},{6,7},{7,6},{8,9},{9,8},{10,11... | collective-permute-start | bytes 5898248 | tf_op jit(solution)/shard_map/ppermute | solution.py:670
  54.4 1.3 copy-start.1
  64.2 28.5 %all-to-all-start.1 = ((bf16[32,16,1024]{2,1,0:T(8,128)(2,1)}), bf16[32,16,1024]{2,1,0:T(8,128)(2,1)S(1)}, u32[]{:S(2)}, u32[]{:S(2)}) async-start(bf16[32,16,1024]{2,1,0:T(8,128)(2,1)} %bitcast.41), calls=%async_computation.1 | async-start | bytes 2097152 | tf_op jit(solution)/shard_map/all_to_all | solution.py:686
  79.5 24.5 %collective-permute-start.9 = (bf16[272,1024]{1,0:T(8,128)(2,1)}, bf16[272,1024]{1,0:T(8,128)(2,1)S(1)}, u32[]{:S(2)}, u32[]{:S(2)}) collective-permute-start(bf16[272,1024]{1,0:T(8,128)(2,1)} %get-tuple-element.35), channel_id=1, source_target_pairs={{0,32},{32,64},{64,96},{96,0},{1,33},{33,65},{65,97},{97,1},{2,34}... | collective-permute-start | bytes 1671176 | tf_op jit(solution)/shard_map/ppermute | solution.py:683
  80.7 26.6 %collective-permute-start.10 = (bf16[272,1024]{1,0:T(8,128)(2,1)}, bf16[272,1024]{1,0:T(8,128)(2,1)S(1)}, u32[]{:S(2)}, u32[]{:S(2)}) collective-permute-start(bf16[272,1024]{1,0:T(8,128)(2,1)} %get-tuple-element.36), channel_id=1, source_target_pairs={{0,64},{32,96},{64,0},{96,32},{1,65},{33,97},{65,1},{97,33},{2,66}... | collective-permute-start | bytes 1671176 | tf_op jit(solution)/shard_map/ppermute | solution.py:683
  82.4 24.9 %collective-permute-start.11 = (bf16[272,1024]{1,0:T(8,128)(2,1)}, bf16[272,1024]{1,0:T(8,128)(2,1)S(1)}, u32[]{:S(2)}, u32[]{:S(2)}) collective-permute-start(bf16[272,1024]{1,0:T(8,128)(2,1)} %get-tuple-element.37), channel_id=1, source_target_pairs={{0,96},{32,0},{64,32},{96,64},{1,97},{33,1},{65,33},{97,65},{2,98}... | collective-permute-start | bytes 1671176 | tf_op jit(solution)/shard_map/ppermute | solution.py:683
  92.6 1.0 copy-start.4
  103.9 11.7 %copy-start.5 = (bf16[272,1024]{1,0:T(8,128)(2,1)}, bf16[272,1024]{1,0:T(8,128)(2,1)S(1)}, u32[]{:S(2)}) copy-start(bf16[272,1024]{1,0:T(8,128)(2,1)S(1)} %collective-permute-done.9.refs_0_) | copy-start | bytes 1671172
  107.3 8.3 %copy-start.6 = (bf16[272,1024]{1,0:T(8,128)(2,1)}, bf16[272,1024]{1,0:T(8,128)(2,1)S(1)}, u32[]{:S(2)}) copy-start(bf16[272,1024]{1,0:T(8,128)(2,1)S(1)} %collective-permute-done.10.refs_1_) | copy-start | bytes 1671172
  107.3 8.3 %copy-start.7 = (bf16[272,1024]{1,0:T(8,128)(2,1)}, bf16[272,1024]{1,0:T(8,128)(2,1)S(1)}, u32[]{:S(2)}) copy-start(bf16[272,1024]{1,0:T(8,128)(2,1)S(1)} %collective-permute-done.11.refs_2_) | copy-start | bytes 1671172
  107.3 25.4 %all-to-all-start.2 = ((bf16[32,16,1024]{2,1,0:T(8,128)(2,1)}), bf16[32,16,1024]{2,1,0:T(8,128)(2,1)S(1)}, u32[]{:S(2)}, u32[]{:S(2)}) async-start(bf16[32,16,1024]{2,1,0:T(8,128)(2,1)} %bitcast.43), calls=%async_computation.2 | async-start | bytes 2097152 | tf_op jit(solution)/shard_map/all_to_all | solution.py:686
  132.8 1.0 copy-start.2

commit v3 on v2

v3 whole, which is shorter than its diff:
```python
import jax
import jax.numpy as jnp
from jax import lax
from jax.experimental import pallas as pl
from jax.experimental.pallas import tpu as pltpu
from jax.sharding import Mesh, PartitionSpec as P

STATE = 16
HEADS = 32
TILE = 16
CHUNK = 128
LANES = 128
BLOCK = 32
PARTS = CHUNK // BLOCK
STRIDE = 24
LOG2E = 1.4426950408889634
GRANT = 56 * 2**20

f32 = jnp.float32
bf16 = jnp.bfloat16


def dot(a, b, contract=((1,), (0,))):
    return lax.dot_general(a, b, (contract, ((), ())), preferred_element_type=f32)


def shifted(x, axis, step):
    count = lax.axis_size(axis)
    pairs = [(i, i + step) for i in range(count) if 0 <= i + step < count]
    return lax.ppermute(x, axis, pairs)


def diagonal(x, down, right):
    axes = ("row", "chip", "core")
    rows, columns = lax.axis_size("row"), lax.axis_size(("chip", "core"))
    pairs = [
        (r * columns + c, (r + down) * columns + c + right)
        for r in range(rows)
        for c in range(columns)
        if 0 <= r + down < rows and 0 <= c + right < columns
    ]
    return lax.ppermute(x, axes, pairs)


def here():
    return lax.axis_index("row"), 2 * lax.axis_index("chip") + lax.axis_index("core")


def normalized(x, gain):
    average = jnp.mean(x, axis=-1, keepdims=True)
    centered = x - average
    spread = jnp.mean(centered * centered, axis=-1, keepdims=True)
    return centered * lax.rsqrt(spread + 1e-05) * gain


def paired(own_ref, other_ref, core):
    own, other = own_ref[...].astype(f32), other_ref[...].astype(f32)
    return jnp.where(core == 0, own, other), jnp.where(core == 0, other, own)


def rows_of_eight(*pieces):
    count = pieces[0].shape[0] // 8
    parts = [p.reshape(count, 8, p.shape[1]) for p in pieces]
    return jnp.concatenate(parts, axis=1).reshape(-1, pieces[0].shape[1]).astype(bf16)


def input_weights(own_ref, other_ref, core):
    half = own_ref.shape[1] // 2
    even, odd = paired(own_ref, other_ref, core)
    return rows_of_eight(even[:, :half], even[:, half:], odd[:, :half], odd[:, half:])


def parcel_kernel(mask, in_ref, out_ref, proj_ref, parcel_ref):
    place = here()
    row = lax.broadcasted_iota(jnp.int32, (8, LANES), 0)
    lane = lax.broadcasted_iota(jnp.int32, (8, LANES), 1)
    flags = jnp.zeros((8, LANES), f32)
    for i in range(mask.shape[1]):
        flags = jnp.where(
            (row == i) & (lane == place[1]), mask[:, i : i + 1].astype(f32), flags
        )
    turned = in_ref[...].astype(f32)
    parts = [turned[:8], turned[8:], out_ref[...].astype(f32), proj_ref[...].astype(f32), flags]
    at = 0
    for part in parts:
        width = part.shape[1]
        parcel_ref[:, :, at : at + width] = jnp.broadcast_to(
            part.astype(bf16)[None], (parcel_ref.shape[0], 8, width)
        )
        at += width


def parcels(mask, turned, w_out, w_proj, groups):
    width = 2 * turned.shape[1] + w_out.shape[1] + w_proj.shape[1] + LANES
    block = 16
    one = lambda i: (0, 0)
    return pl.pallas_call(
        parcel_kernel,
        grid=(groups // block,),
        in_specs=[
            pl.BlockSpec(mask.shape, one),
            pl.BlockSpec(turned.shape, one),
            pl.BlockSpec(w_out.shape, one),
            pl.BlockSpec(w_proj.shape, one),
        ],
        out_specs=pl.BlockSpec((block, 8, width), lambda i: (i, 0, 0)),
        out_shape=jax.ShapeDtypeStruct((groups, 8, width), bf16),
        compiler_params=pltpu.CompilerParams(vmem_limit_bytes=GRANT),
        name="parcels",
    )(mask, turned, w_out, w_proj)


def head_lanes(ref, first):
    heads = ref.shape[1]
    head = lax.broadcasted_iota(jnp.int32, (heads, LANES), 0)
    lane = lax.broadcasted_iota(jnp.int32, (heads, LANES), 1)
    placed = [
        lax.dot_general(
            ref[...],
            (lane == head + 64 * d).astype(f32),
            (((1,), (0,)), ((), ())),
            precision=lax.Precision.HIGHEST,
            preferred_element_type=f32,
        )
        for d in range(2)
    ]
    return placed[0][first : first + 1] + placed[1][first + 1 : first + 2]


def chunk_terms(values, w_proj, bias, rate, kept):
    coefs = dot(values, w_proj)
    at = lax.broadcasted_iota(jnp.int32, (CHUNK, LANES), 0)
    lane = lax.broadcasted_iota(jnp.int32, (CHUNK, LANES), 1)
    v = coefs + bias
    steps = kept * (jnp.maximum(v, 0.0) + jnp.log1p(jnp.exp(-jnp.abs(v))))
    decays = steps * rate
    lower = ((lane <= at) & (lane // BLOCK == at // BLOCK)).astype(f32).astype(bf16)
    high = decays.astype(bf16)
    rest = decays - high.astype(f32)
    middle = rest.astype(bf16)
    low = (rest - middle.astype(f32)).astype(bf16)
    total = dot(
        jnp.concatenate([lower] * 3, axis=1), jnp.concatenate([high, middle, low], axis=0)
    )
    sums = jnp.where(lane < 64, total, total - decays)
    ends = [total[(b + 1) * BLOCK - 1 : (b + 1) * BLOCK, :] for b in range(PARTS)]
    return coefs, steps, sums, ends


def edge_factors(sums, steps, ends):
    lane = lax.broadcasted_iota(jnp.int32, (CHUNK, LANES), 1)
    end = jnp.concatenate([jnp.broadcast_to(e, (BLOCK, LANES)) for e in ends], axis=0)
    tail = jnp.exp2(jnp.where(lane < 64, sums - end, -sums)) * steps
    enter = jnp.exp2(jnp.where(lane < 64, -sums, sums - end))
    rows = ends + [jnp.zeros((8 - PARTS, LANES), f32)]
    fade = jnp.exp2(-jnp.concatenate(rows, axis=0))
    return tail.astype(bf16), enter.astype(bf16), fade


def head_spread(expand):
    head = lax.broadcasted_iota(jnp.int32, (LANES, expand), 0)
    channel = lax.broadcasted_iota(jnp.int32, (LANES, expand), 1)
    return [(head == channel // 32 + 64 * d).astype(f32).astype(bf16) for d in range(2)]


def by_block(coefs, first):
    lane = lax.broadcasted_iota(jnp.int32, (LANES, PARTS * STATE), 0)
    to = lax.broadcasted_iota(jnp.int32, (LANES, PARTS * STATE), 1)
    copied = dot(coefs, (lane == first + to % STATE).astype(f32).astype(bf16))
    at = lax.broadcasted_iota(jnp.int32, copied.shape, 0)
    place = lax.broadcasted_iota(jnp.int32, copied.shape, 1)
    return jnp.where(at // BLOCK == place // STATE, copied, 0.0).astype(bf16)


def block_states(values, coefs, tail, spread):
    writes, inputs = coefs.astype(bf16), values.astype(f32)
    states = []
    for d in range(2):
        weighted = (inputs * dot(tail, spread[d])).astype(bf16)
        states.append(dot(by_block(writes, 64 * d + 32), weighted, ((0,), (0,))))
    return states


def mixing_scratch():
    return [
        pltpu.VMEM((LANES, CHUNK), f32),
        pltpu.VMEM((LANES, CHUNK), f32),
        pltpu.VMEM((4 * PARTS, 8, LANES), f32),
    ]


def mix_chunk(values, coefs, steps, sums, spread, scratch, more, store):
    sums_t, steps_t, rows = scratch
    expand = values.shape[1]
    sums_t[...], steps_t[...] = sums.T, steps.T
    row_lane = lax.broadcasted_iota(jnp.int32, (8, LANES), 1)
    for a, (ref, first) in enumerate(((sums_t, 0), (sums_t, 64), (steps_t, 0), (steps_t, 64))):
        lines = [ref[pl.ds(first + k, 8, stride=4), :] for k in range(4)]
        for b in range(PARTS):
            merged = None
            for k in range(4):
                turn = (k - b) * BLOCK % LANES
                line = pltpu.roll(lines[k], turn, 1) if turn else lines[k]
                merged = line if merged is None else jnp.where(row_lane // BLOCK == k, line, merged)
            rows[a * PARTS + b] = merged
    at = lax.broadcasted_iota(jnp.int32, (BLOCK, LANES), 0)
    source = lax.broadcasted_iota(jnp.int32, (BLOCK, LANES), 1) % BLOCK
    causal = source <= at
    c = coefs.astype(bf16)
    products = []
    for b in range(PARTS):
        block = c[b * BLOCK : (b + 1) * BLOCK, :]
        four = jnp.concatenate([block] * 4, axis=0)
        forward = dot(block[:, 48:64], four[:, 32:48], ((1,), (1,)))
        backward = dot(block[:, 112:128], four[:, 96:112], ((1,), (1,)))
        products.append(
            (jnp.where(causal, forward, 0.0), jnp.where(source >= at, backward, 0.0))
        )
    high = sums.astype(bf16)
    parts = jnp.concatenate([high, (sums - high.astype(f32)).astype(bf16)], axis=1)
    head_of = lax.broadcasted_iota(jnp.int32, (BLOCK, LANES), 1) // 32
    for pair in range(0, expand, 2 * LANES):
        wide = slice(pair, pair + 2 * LANES)
        own = [
            dot(parts, jnp.concatenate([spread[d][:, wide]] * 2, axis=0)) for d in range(2)
        ]
        extra = more(wide)
        for lane in range(0, 2 * LANES, LANES):
            tile = (pair + lane) // LANES
            lanes = slice(pair + lane, pair + lane + LANES)
            for b in range(PARTS):
                span = slice(b * BLOCK, (b + 1) * BLOCK)
                row = [rows[a * PARTS + b, tile : tile + 1, :] for a in range(4)]
                exponent = jnp.where(
                    causal,
                    row[0] - own[0][span, lane : lane + LANES],
                    own[1][span, lane : lane + LANES] - row[1],
                )
                scale = products[b][0] * row[2] + products[b][1] * row[3]
                mixing = (jnp.exp2(exponent) * scale).astype(bf16)
                inputs = values[span, lanes]
                apart = jnp.concatenate(
                    [jnp.where(head_of == k, inputs, jnp.zeros_like(inputs)) for k in range(4)],
                    axis=0,
                )
                total = dot(mixing, apart)
                if extra is not None:
                    total = total + extra[span, lane : lane + LANES]
                store(span, lanes, total.astype(bf16))


def line_kernel(
    a_ref, own_ref, other_ref, own_flags, other_flags, bias_ref, rate_ref, out_ref, coefs, steps, sums, enters, fades, states, entering, *scratch
):
    place = here()
    length, expand = a_ref.shape
    chunks = length // CHUNK
    part = PARTS * STATE
    lane = lax.broadcasted_iota(jnp.int32, (CHUNK, LANES), 1)
    spread = head_spread(expand)
    w_proj = rows_of_eight(*paired(own_ref, other_ref, place[1] % 2))
    bias, rate = head_lanes(bias_ref, 0), head_lanes(rate_ref, 0) * LOG2E
    flags = own_flags[...].astype(f32) + other_flags[...].astype(f32)
    line = lax.broadcasted_iota(jnp.int32, flags.shape, 0)
    mine = (line // (flags.shape[0] // 4) == place[0]) & (line % 8 == place[1] // TILE)
    mask = jnp.sum(jnp.where(mine, flags, 0.0), axis=0, keepdims=True)
    position = lax.broadcasted_iota(jnp.int32, (CHUNK, LANES), 0)
    for c in range(chunks):
        tile_at = lane == (position + c * CHUNK) // TILE
        kept = jnp.sum(jnp.where(tile_at, mask, 0.0), axis=1, keepdims=True)
        at = slice(c * CHUNK, (c + 1) * CHUNK)
        values = a_ref[at, :]
        k, s, q, ends = chunk_terms(values, w_proj, bias, rate, kept)
        tail, enter, fade = edge_factors(q, s, ends)
        coefs[at, :], steps[at, :], sums[at, :], enters[at, :] = k, s, q, enter
        fades[8 * c : 8 * c + 8, :] = fade
        for d, state in enumerate(block_states(values, k, tail, spread)):
            states[d, c * part : (c + 1) * part, :] = state
    fade = fades[...]
    high = fade.astype(bf16)
    low = (fade - high.astype(f32)).astype(bf16)
    blocks = chunks * PARTS
    for d in range(2):
        decay = dot(high, spread[d]) + dot(low, spread[d])
        running = jnp.zeros((STATE, expand), f32)
        for b in range(blocks) if d == 0 else range(blocks - 1, -1, -1):
            at = slice(b * STATE, (b + 1) * STATE)
            entering[d, at, :] = running.astype(bf16)
            row = b // PARTS * 8 + b % PARTS
            running = running * decay[row : row + 1, :] + states[d, at, :]
    for c in range(chunks):
        at = slice(c * CHUNK, (c + 1) * CHUNK)
        k, enter = coefs[at, :], enters[at, :]
        read = k.astype(bf16)
        reads = [by_block(read, 64 * d + 48) for d in range(2)]

        def carried(lanes):
            total = None
            for d in range(2):
                state = dot(reads[d], entering[d, c * part : (c + 1) * part, lanes])
                term = dot(enter, spread[d][:, lanes]) * state
                total = term if total is None else total + term
            return total

        def store(span, lanes, value):
            out_ref[c * CHUNK + span.start : c * CHUNK + span.stop, lanes] = value

        mix_chunk(
            a_ref[at, :], k, steps[at, :], sums[at, :], spread, scratch, carried, store
        )


def piece_specs(rows, *columns):
    return [pl.BlockSpec((rows, LANES), lambda i, c=c: (0, c)) for c in columns for _ in range(2)]


def swept_lines(values, own, other, bias, rate):
    length, expand = values.shape
    chunks = length // CHUNK
    small = pl.BlockSpec(bias.shape, lambda i: (0, 0))
    return pl.pallas_call(
        line_kernel,
        grid=(1,),
        in_specs=[
            pl.BlockSpec((length, expand), lambda i: (0, 0)),
            *piece_specs(own.shape[0], 12, 14),
            small,
            small,
        ],
        out_specs=pl.BlockSpec((length, expand), lambda i: (0, 0)),
        out_shape=jax.ShapeDtypeStruct((length, expand), bf16),
        scratch_shapes=[
            pltpu.VMEM((length, LANES), f32),
            pltpu.VMEM((length, LANES), f32),
            pltpu.VMEM((length, LANES), f32),
            pltpu.VMEM((length, LANES), bf16),
            pltpu.VMEM((8 * chunks, LANES), f32),
            pltpu.VMEM((2, length // BLOCK * STATE, expand), f32),
            pltpu.VMEM((2, length // BLOCK * STATE, expand), bf16),
            *mixing_scratch(),
        ],
        compiler_params=pltpu.CompilerParams(vmem_limit_bytes=GRANT),
        cost_estimate=pl.CostEstimate(
            flops=6 * 2**30, bytes_accessed=3 * 2**20, transcendentals=2**21
        ),
        name="sweep_rows",
    )(values, own, other, own, other, bias, rate)


def column_states(
    values_ref, own_ref, other_ref, own_flags, other_flags, bias_ref, rate_ref, coefs_ref, steps_ref, sums_ref, read_ref, slot_refs
):
    row, column = here()
    expand = values_ref.shape[1]
    slots = len(slot_refs)
    states = slot_refs[0].shape[0] - 16
    groups = values_ref.shape[0] // CHUNK
    part = states // groups
    lane = lax.broadcasted_iota(jnp.int32, (CHUNK, LANES), 1)
    flags = (own_flags[...].astype(f32) + other_flags[...].astype(f32)).astype(bf16)
    to = lax.broadcasted_iota(jnp.int32, (CHUNK, flags.shape[0]), 0)
    source = lax.broadcasted_iota(jnp.int32, (CHUNK, flags.shape[0]), 1)
    mine = (source // (flags.shape[0] // (slots + 1)) == row) & (
        source % 8 == to % BLOCK // TILE
    )
    marks = dot(mine.astype(f32).astype(bf16), flags)
    kept = jnp.sum(jnp.where(lane == column, marks, 0.0), axis=1, keepdims=True)
    proj = rows_of_eight(*paired(own_ref, other_ref, column % 2))
    bias, rate = head_lanes(bias_ref, 2), head_lanes(rate_ref, 2) * LOG2E
    spread = head_spread(expand)
    rows = [[] for _ in slot_refs]
    for g in range(groups):
        at = slice(g * CHUNK, (g + 1) * CHUNK)
        values = values_ref[at, :]
        k, s, q, ends = chunk_terms(values, proj, bias, rate, kept)
        coefs_ref[at, :], steps_ref[at, :], sums_ref[at, :] = k.astype(bf16), s.astype(bf16), q
        tail, enter, fade = edge_factors(q, s, ends)
        read_ref[at, :] = jnp.where(lane % 64 >= 48, k.astype(bf16), enter)
        high = fade.astype(bf16)
        low = (fade - high.astype(f32)).astype(bf16)
        down, up = block_states(values, k, tail, spread)
        fades = [dot(high, m) + dot(low, m) for m in spread]
        for d, ref in enumerate(slot_refs):
            onward = row + d + 1 <= slots
            ref[g * part : (g + 1) * part, :] = jnp.where(onward, down, up).astype(bf16)
            rows[d].append(jnp.where(onward, fades[0], fades[1])[:PARTS])
    for d, ref in enumerate(slot_refs):
        ref[states:, :] = jnp.concatenate(rows[d], axis=0).astype(bf16)


def filter_kernel(
    x_ref, gain_ref, own_ref, other_ref, taps_ref, bias_ref, *refs
):
    place = here()
    column_refs, (act_ref, turned_ref), refs = refs[:6], refs[6:8], refs[8:]
    outs, slot_refs, (normed, branch, order, turned) = refs[:4], refs[4:-4], refs[-4:]
    padded = x_ref.shape[0]
    tokens, width = act_ref.shape
    height = padded // STRIDE - 2
    breadth = tokens // height

    @pl.when(pl.program_id(0) == 0)
    def _():
        step = 64
        for at in range(0, padded, step):
            x = x_ref[at : at + step, :].astype(f32)
            normed[at : at + step, :] = normalized(x, gain_ref[...]).astype(bf16)
        to = lax.broadcasted_iota(jnp.int32, (tokens, tokens), 0)
        source = lax.broadcasted_iota(jnp.int32, (tokens, tokens), 1)
        w, h = to // height, to % height
        order[...] = (source == h * breadth + w).astype(f32).astype(bf16)

    weights = input_weights(own_ref, other_ref, place[1] % 2)
    product = dot(normed[...], weights, ((1,), (1,)))
    branch[...] = product.astype(bf16).astype(f32)
    rows = 4
    span = rows * STRIDE + 8
    for lane in range(0, width, LANES):
        lanes = slice(lane, lane + LANES)
        taps = [taps_ref[k : k + 1, lanes] for k in range(9)]
        for h in range(0, height, rows):
            windows = [
                branch[(h + i) * STRIDE : (h + i) * STRIDE + span, lanes] for i in range(3)
            ]
            left, middle, right = [
                windows[0] * taps[j] + windows[1] * taps[3 + j] + windows[2] * taps[6 + j]
                for j in range(3)
            ]
            convolved = (
                middle
                + pltpu.roll(left, 1, 0)
                + pltpu.roll(right, span - 1, 0)
                + bias_ref[:, lanes]
            )
            activated = convolved / (1.0 + jnp.exp(-convolved))
            kept = activated[: rows * STRIDE].reshape(rows, STRIDE, LANES)[:, 8:, :]
            act_ref[h * breadth : (h + rows) * breadth, lanes] = kept.reshape(
                rows * breadth, LANES
            ).astype(bf16)
    across = dot(order[...], act_ref[...]).astype(bf16)
    turned_ref[...] = across
    step = pl.program_id(0)
    turned[:, pl.ds(pl.multiple_of(step * width, width), width)] = across

    @pl.when(step == pl.num_programs(0) - 1)
    def _():
        column_states(turned, *column_refs, *outs, slot_refs)


def filtered(x, gain, own, other, taps, bias, tokens, dt_bias, rate, slots):
    expand = bias.shape[1]
    padded, channels = x.shape
    width = 256
    states = tokens // BLOCK * STATE + 16
    one = lambda c: (0, 0)
    piece = pl.BlockSpec((width // 4, 2 * channels), lambda c: (c, 0))
    return pl.pallas_call(
        filter_kernel,
        grid=(expand // width,),
        in_specs=[
            pl.BlockSpec((padded, channels), lambda c: (0, 0)),
            pl.BlockSpec((1, channels), lambda c: (0, 0)),
            piece,
            piece,
            pl.BlockSpec((9, width), lambda c: (0, c)),
            pl.BlockSpec((1, width), lambda c: (0, c)),
            *piece_specs(own.shape[0], 13, 14),
            pl.BlockSpec(dt_bias.shape, one),
            pl.BlockSpec(rate.shape, one),
        ],
        out_specs=[pl.BlockSpec((tokens, width), lambda c: (0, c))] * 2
        + [pl.BlockSpec((tokens, LANES), one)] * 4
        + [pl.BlockSpec((states, expand), one)] * (slots - 1),
        out_shape=[jax.ShapeDtypeStruct((tokens, expand), bf16)] * 2
        + [jax.ShapeDtypeStruct((tokens, LANES), t) for t in (bf16, bf16, f32, bf16)]
        + [jax.ShapeDtypeStruct((states, expand), bf16)] * (slots - 1),
        scratch_shapes=[
            pltpu.VMEM((padded, channels), bf16),
            pltpu.VMEM((padded, width), f32),
            pltpu.VMEM((tokens, tokens), bf16),
            pltpu.VMEM((tokens, expand), bf16),
        ],
        compiler_params=pltpu.CompilerParams(vmem_limit_bytes=GRANT),
        cost_estimate=pl.CostEstimate(
            flops=2 * padded * channels * expand, bytes_accessed=6 * 2**20, transcendentals=tokens * expand
        ),
        name="norm_project_filter",
    )(x, gain, own, other, taps, bias, own, other, own, other, dt_bias, rate)


def mix_kernel(a_ref, coefs_ref, steps_ref, sums_ref, out_ref, spread, *scratch):
    @pl.when(pl.program_id(0) == 0)
    def _():
        for d, matrix in enumerate(head_spread(a_ref.shape[1])):
            spread[d] = matrix

    def store(span, lanes, value):
        out_ref[span, lanes] = value

    mix_chunk(
        a_ref[...],
        coefs_ref[...],
        steps_ref[...].astype(f32),
        sums_ref[...],
        [spread[0], spread[1]],
        scratch,
        lambda lanes: None,
        store,
    )


def mixed_columns(values, coefs, steps, sums):
    tokens, expand = values.shape
    block = pl.BlockSpec((CHUNK, expand), lambda i: (i, 0))
    thin = pl.BlockSpec((CHUNK, LANES), lambda i: (i, 0))
    return pl.pallas_call(
        mix_kernel,
        grid=(tokens // CHUNK,),
        in_specs=[block, thin, thin, thin],
        out_specs=block,
        out_shape=jax.ShapeDtypeStruct((tokens, expand), bf16),
        scratch_shapes=[pltpu.VMEM((2, LANES, expand), bf16), *mixing_scratch()],
        compiler_params=pltpu.CompilerParams(vmem_limit_bytes=GRANT),
        cost_estimate=pl.CostEstimate(
            flops=2**32, bytes_accessed=3 * 2**20, transcendentals=2**21
        ),
        name="mix_columns",
    )(values, coefs, steps, sums)


def entering_kernel(
    local_ref, read_ref, act_ref, skip_ref, x_ref, gain_ref, own_gate, other_gate, own_out, other_out, *refs
):
    place = here()
    slots = len(refs) - 5
    slot_refs, (part_ref, gate_ref, w_out_ref, w_gate, columns) = refs[:slots], refs[slots:]
    expand = local_ref.shape[1]
    states = slot_refs[0].shape[0] - 16
    groups = local_ref.shape[0] // CHUNK
    part = states // groups
    lines = part // STATE
    height = CHUNK // lines
    spread = head_spread(expand)
    row = place[0]
    decays = [ref[states:, :].astype(f32) for ref in slot_refs]
    for g in range(groups):
        at = slice(g * CHUNK, (g + 1) * CHUNK)
        total = local_ref[at, :].astype(f32)
        read = read_ref[at, :]
        for d in range(2):
            order = range(slots) if d == 0 else range(slots - 1, -1, -1)
            entering, product = [], [None] * lines
            sums = [jnp.zeros((STATE, expand), f32)] * lines
            for step, k in enumerate(order):
                reaches = row > step if d == 0 else row + step + 1 <= slots
                for line in range(lines):
                    at_state = g * part + line * STATE
                    state = slot_refs[k][at_state : at_state + STATE, :].astype(f32)
                    if product[line] is not None:
                        state = state * product[line]
                    sums[line] = sums[line] + jnp.where(reaches, state, 0.0)
                    fade = decays[k][g * lines + line : g * lines + line + 1, :]
                    product[line] = fade if product[line] is None else product[line] * fade
            entering = jnp.concatenate(sums, axis=0).astype(bf16)
            carried = dot(by_block(read, 64 * d + 48), entering)
            total = total + dot(read, spread[d]) * carried
        columns[at, :] = total.astype(bf16)
    w_gate[...] = input_weights(own_gate, other_gate, place[1] % 2)
    w_out_ref[...] = rows_of_eight(*paired(own_out, other_out, place[1] % 2))
    tokens = local_ref.shape[0]
    breadth = tokens // height
    for g in range(groups):
        at = slice(g * CHUNK, (g + 1) * CHUNK)
        to = lax.broadcasted_iota(jnp.int32, (CHUNK, tokens), 0) + g * CHUNK
        source = lax.broadcasted_iota(jnp.int32, (CHUNK, tokens), 1)
        w, h = source // height, source % height
        back = (to == h * breadth + w).astype(f32).astype(bf16)
        direct = skip_ref[...] * act_ref[at, :].astype(f32)
        part_ref[at, :] = dot(back, columns[...]) + direct
        normed = normalized(x_ref[at, :].astype(f32), gain_ref[...]).astype(bf16)
        gating = dot(normed, w_gate[...], ((1,), (1,))).astype(bf16).astype(f32)
        gate_ref[at, :] = (gating / (1.0 + jnp.exp(-gating))).astype(bf16)


def entered(local, read, act, skip, x, gain, own, other, slots):
    tokens, expand = local.shape
    pairs, channels = own.shape[0], x.shape[1]
    whole = lambda x: pl.BlockSpec(x.shape, lambda i: (0, 0))
    gate = pl.BlockSpec((pairs // 2, 2 * channels), lambda i: (1, 0))
    last = pl.BlockSpec((pairs, channels), lambda i: (0, 2))
    shapes = [
        jax.ShapeDtypeStruct((tokens, expand), f32),
        jax.ShapeDtypeStruct((tokens, expand), bf16),
        jax.ShapeDtypeStruct((expand, channels), bf16),
    ]
    return pl.pallas_call(
        entering_kernel,
        grid=(1,),
        in_specs=[whole(a) for a in (local, read, act, skip, x, gain)]
        + [gate, gate, last, last]
        + [whole(a) for a in slots],
        out_specs=[whole(a) for a in shapes],
        out_shape=shapes,
        scratch_shapes=[
            pltpu.VMEM((expand, channels), bf16),
            pltpu.VMEM((tokens, expand), bf16),
        ],
        compiler_params=pltpu.CompilerParams(vmem_limit_bytes=GRANT),
        cost_estimate=pl.CostEstimate(
            flops=2**32, bytes_accessed=12 * 2**20, transcendentals=2**19
        ),
        name="enter_columns",
    )(local, read, act, skip, x, gain, own, other, own, other, *slots)


def output_kernel(part_ref, gate_ref, rows_ref, x_ref, w_ref, out_gain_ref, out_ref):
    summed = part_ref[...] + rows_ref[...].astype(f32)
    mixed = (normalized(summed, out_gain_ref[...]) * gate_ref[...].astype(f32)).astype(bf16)
    out_ref[...] = (x_ref[...].astype(f32) + dot(mixed, w_ref[...])).astype(bf16)


def projected(part, gate, rows, x, w_out, out_gain):
    tokens, expand = part.shape
    channels = x.shape[1]
    block = 128
    one = lambda i: (0, 0)
    wide = pl.BlockSpec((block, expand), lambda i: (i, 0))
    narrow = pl.BlockSpec((block, channels), lambda i: (i, 0))
    return pl.pallas_call(
        output_kernel,
        grid=(tokens // block,),
        in_specs=[
            wide,
            wide,
            wide,
            narrow,
            pl.BlockSpec((expand, channels), one),
            pl.BlockSpec((1, expand), one),
        ],
        out_specs=narrow,
        out_shape=jax.ShapeDtypeStruct((tokens, channels), bf16),
        compiler_params=pltpu.CompilerParams(vmem_limit_bytes=GRANT),
        name="gate_and_project",
    )(part, gate, rows, x, w_out, out_gain)


def on_device(
    tokens, tile_mask, norm_gain, w_in, conv_weight, conv_bias, w_proj, dt_bias, decay_rate, skip_gain, out_gain, w_out
):
    wide = ("chip", "core")
    count_row, count_chip = lax.axis_size("row"), lax.axis_size("chip")
    height, breadth, channels = tokens.shape
    local = height * breadth
    expand = conv_bias.shape[0]

    groups = count_row * count_chip
    parcel = parcels(tile_mask.T, w_in.T, w_out, w_proj, groups)
    own = lax.all_to_all(parcel, ("row", "chip"), 0, 0, tiled=True)
    above, below = shifted(tokens[-1:], "row", 1), shifted(tokens[:1], "row", -1)
    tall = jnp.concatenate([above, tokens, below], axis=0)
    before, after = [
        jnp.concatenate(
            [
                diagonal(tokens[-1:, edge], 1, step),
                shifted(tokens[:, edge], wide, step),
                diagonal(tokens[:1, edge], -1, step),
            ],
            axis=0,
        )
        for edge, step in ((slice(breadth - 1, breadth), 1), (slice(0, 1), -1))
    ]
    after_last = jnp.concatenate([jnp.zeros_like(after[:1]), after], axis=0)
    body = jnp.concatenate(
        [after_last[:-1], jnp.zeros((height + 2, 6, channels), bf16), before, tall], axis=1
    ).reshape((height + 2) * STRIDE, channels)
    x_ext = jnp.concatenate([body, after_last[-1], jnp.zeros((15, channels), bf16)], axis=0)

    own, x_ext = lax.optimization_barrier((own, x_ext))
    other = lax.ppermute(own, "core", [(0, 1), (1, 0)])
    own, other = [p.reshape(groups * 8, p.shape[2]) for p in (own, other)]

    act, turned, coefs, steps, sums, read, *states = filtered(
        x_ext,
        norm_gain.reshape(1, -1),
        own,
        other,
        conv_weight,
        conv_bias.reshape(1, -1),
        local,
        dt_bias,
        decay_rate,
        count_row,
    )
    def spun(piece, d):
        return lax.ppermute(piece, "row", [(i, (i + d) % count_row) for i in range(count_row)])

    def dealt(x):
        return lax.all_to_all(
            x.reshape(-1, breadth, expand), wide, 0, 0, tiled=True
        ).reshape(-1, expand)

    lines = dealt(act)
    received = [spun(piece, d + 1) for d, piece in enumerate(states)]
    columns_local = mixed_columns(turned, coefs, steps, sums)
    lines, columns_local = lax.optimization_barrier((lines, columns_local))
    rows_out = swept_lines(lines, own, other, dt_bias, decay_rate)
    rows_out, received = lax.optimization_barrier((rows_out, received))
    rows_back = dealt(rows_out)
    x = tokens.reshape(local, channels)
    part, gate, full_out = entered(
        columns_local,
        read,
        act,
        skip_gain.reshape(1, -1),
        x,
        norm_gain.reshape(1, -1),
        own,
        other,
        received,
    )
    result = projected(part, gate, rows_back, x, full_out, out_gain.reshape(1, -1))
    return result.reshape(height, breadth, channels)


def solution(mesh):
    rows, columns = mesh.devices.shape
    split = Mesh(mesh.devices.reshape(rows, columns // 2, 2), ("row", "chip", "core"))
    wide, all_axes = ("chip", "core"), ("row", "chip", "core")
    placed = (
        P("row", wide, None),
        P("row", wide),
        P(),
        P(None, all_axes),
        P(),
        P(),
        P(all_axes, None),
        P(),
        P(),
        P(),
        P(),
        P(all_axes, None),
    )
    return jax.shard_map(
        on_device, mesh=split, in_specs=placed, out_specs=P("row", wide, None), check_vma=False
    )
```

time: 140 us -> 138 us (0.986)
  Pallas kernels: 53.4 us -> 49.8 us
  waiting for transfers between devices: 17.5 us -> 19.8 us
    pallas_call x2 -> x1, Pallas kernels: 16.6 us -> 6.84 us  [mixed_columns(): pl.pallas_call(mix_kernel, grid=(tokens // CHUNK,), in_specs=[block, thin...]
    pallas_call x1, Pallas kernels: 8.47 us -> 14.4 us  [filtered(): pl.pallas_call(filter_kernel, grid=(expand // width,), in_specs=[pl.Block...]
    all_to_all x2, waiting for transfers between devices: 7.48 us -> 13.2 us  [dealt(): lax.all_to_all(x.reshape(-1, breadth, expand), wide, 0, 0, tiled=True)]
    ppermute x3, waiting for transfers between devices: 3.38 us -> 0.01 us  [spun(): lax.ppermute(piece, 'row', [(i, (i + d) % count_row) for i in range(count...]
    all_to_all x2, starting transfers between devices: 15.2 us -> 13.8 us  [dealt(): lax.all_to_all(x.reshape(-1, breadth, expand), wide, 0, 0, tiled=True)]
    unnamed x19 -> x21, local copies, waits for them, and re-layouts: 3.34 us -> 3.33 us
  transfers between devices with their start and end apart: 15 -> 15, of which waited for: 4 -> 4; matrix products, arithmetic and copies ran while one was open for 1% -> 2% of each run, Pallas kernels for 26% -> 20%
where the time goes in v3:
time: 138 us; the launch traced here: 137 us
  starting transfers between devices  61.6 us (45%)
  Pallas kernels  49.8 us (36%)
  waiting for transfers between devices  19.8 us (14%)
  local copies, waits for them, and re-layouts  3.71 us (3%)
  other arithmetic  1.71 us (1%)
    ppermute x4, starting transfers between devices, shifted(): return lax.ppermute(x, axis, pairs)  19.2 us
    pallas_call x1, Pallas kernels, filtered(): pl.pallas_call(filter_kernel, grid=(expand // width,), in_specs=[pl.Block...  14.4 us
    all_to_all x2, starting transfers between devices, dealt(): lax.all_to_all(x.reshape(-1, breadth, expand), wide, 0, 0, tiled=True)  13.8 us
    all_to_all x2, waiting for transfers between devices, dealt(): lax.all_to_all(x.reshape(-1, breadth, expand), wide, 0, 0, tiled=True)  13.2 us
    all_to_all x1, starting transfers between devices, on_device(): own = lax.all_to_all(parcel, ('row', 'chip'), 0, 0, tiled=True)  12.1 us
    pallas_call x1, Pallas kernels, swept_lines(): pl.pallas_call(line_kernel, grid=(1,), in_specs=[pl.BlockSpec((length, ex...  11.2 us
    ppermute x4, starting transfers between devices, diagonal(): return lax.ppermute(x, axes, pairs)  9.87 us
    pallas_call x1, Pallas kernels, entered(): pl.pallas_call(entering_kernel, grid=(1,), in_specs=[whole(a) for a in (l...  9.36 us
  transfers between devices with their start and end apart: 15, of which 4 were waited for; matrix products, arithmetic and copies ran while one was open for 2% of the time, Pallas kernels for 20%

profile of v3, /device:TPU:1, one launch (start us, length us, event | category | flops | bytes accessed | tf_op | source)
XLA Modules:
  0.0 136.8 jit_solution(12836182043927746669)
XLA Ops:
  0.0 2.7 %parcels.1 = bf16[64,8,1920]{2,1,0:T(8,128)(2,1)} custom-call(s32[1,2]{1,0:T(1,128)} %bitcast.50, bf16[16,512]{1,0:T(8,128)(2,1)} %bitcast.44, bf16[8,512]{1,0:T(8,128)(2,1)} %out_ref.1, bf16[8,256]{1,0:T(8,128)(2,1)} %proj_ref.1), custom_call_target="tpu_custom_call" | custom-call | tf_op jit(solution)/shard_map/parcels/pallas_call | solution.py:97
  2.7 12.1 %all-to-all-start = ((bf16[64,8,1920]{2,1,0:T(8,128)(2,1)}), bf16[64,8,1920]{2,1,0:T(8,128)(2,1)S(1)}, u32[]{:S(2)}, u32[]{:S(2)}) async-start(bf16[64,8,1920]{2,1,0:T(8,128)(2,1)} %parcels.1), calls=%async_computation | async-start | bytes 3932160 | tf_op jit(solution)/shard_map/all_to_all | solution.py:658
  14.8 4.0 %collective-permute-start = (bf16[1,1,512]{2,0,1:T(2,128)(2,1)S(1)}, bf16[1,1,512]{2,0,1:T(2,128)(2,1)S(1)}, u32[]{:S(2)}, u32[]{:S(2)}) collective-permute-start(bf16[1,1,512]{2,0,1:T(2,128)(2,1)S(1)} %get-tuple-element.45), channel_id=1, source_target_pairs={{1,32},{2,33},{3,34},{4,35},{5,36},{6,37},{7,38},{8,39},{9,40},{10... | collective-permute-start | bytes 3080 | tf_op jit(solution)/shard_map/ppermute | solution.py:42
  18.9 3.2 %collective-permute-start.2 = (bf16[1,1,512]{2,0,1:T(2,128)(2,1)S(1)}, bf16[1,1,512]{2,0,1:T(2,128)(2,1)S(1)}, u32[]{:S(2)}, u32[]{:S(2)}) collective-permute-start(bf16[1,1,512]{2,0,1:T(2,128)(2,1)S(1)} %get-tuple-element.46), channel_id=1, source_target_pairs={{0,33},{1,34},{2,35},{3,36},{4,37},{5,38},{6,39},{7,40},{8,41},{9,... | collective-permute-start | bytes 3080 | tf_op jit(solution)/shard_map/ppermute | solution.py:42
  22.1 1.3 collective-permute-start.4
  23.4 1.3 collective-permute-start.7
  24.7 0.1 fusion
  24.8 1.9 %collective-permute-start.1 = (bf16[32,1,512]{2,0,1:T(8,128)(2,1)S(1)}, bf16[32,1,512]{2,0,1:T(8,128)(2,1)S(1)}, u32[]{:S(2)}, u32[]{:S(2)}) collective-permute-start(bf16[32,1,512]{2,0,1:T(8,128)(2,1)S(1)} %copy.21), channel_id=1, source_target_pairs={{1,0},{2,1},{3,2},{4,3},{5,4},{6,5},{7,6},{8,7},{9,8},{10,9},{11,1... | collective-permute-start | bytes 98312 | tf_op jit(solution)/shard_map/ppermute | solution.py:30
  26.8 0.1 pad.4.clone
  26.9 0.1 pad.2.clone
  27.0 0.0 collective-permute-done
  27.0 14.1 %collective-permute-start.5 = (bf16[1,16,512]{2,1,0:T(8,128)(2,1)S(1)}, bf16[1,16,512]{2,1,0:T(8,128)(2,1)S(1)}, u32[]{:S(2)}, u32[]{:S(2)}) collective-permute-start(bf16[1,16,512]{2,1,0:T(8,128)(2,1)S(1)} %get-tuple-element.51), channel_id=1, source_target_pairs={{0,32},{32,64},{64,96},{1,33},{33,65},{65,97},{2,34},{34,66},{66,9... | collective-permute-start | bytes 49160 | tf_op jit(solution)/shard_map/ppermute | solution.py:30
  41.0 0.0 collective-permute-done.1
  41.0 1.9 %collective-permute-start.3 = (bf16[32,1,512]{2,0,1:T(8,128)(2,1)S(1)}, bf16[32,1,512]{2,0,1:T(8,128)(2,1)S(1)}, u32[]{:S(2)}, u32[]{:S(2)}) collective-permute-start(bf16[32,1,512]{2,0,1:T(8,128)(2,1)S(1)} %copy.23), channel_id=1, source_target_pairs={{0,1},{1,2},{2,3},{3,4},{4,5},{5,6},{6,7},{7,8},{8,9},{9,10},{10,1... | collective-permute-start | bytes 98312 | tf_op jit(solution)/shard_map/ppermute | solution.py:30
  43.0 0.1 pad_maximum_fusion
  43.1 0.0 collective-permute-done.2
  43.1 1.3 collective-permute-start.6
  44.4 0.0 collective-permute-done.4
  44.4 0.0 collective-permute-done.3
  44.4 0.1 copy.19
  44.5 0.1 copy.18
  44.5 0.0 collective-permute-done.5
  44.5 3.0 %collective-permute-done.6 = bf16[1,16,512]{2,1,0:T(8,128)(2,1)S(1)} collective-permute-done((bf16[1,16,512]{2,1,0:T(8,128)(2,1)S(1)}, bf16[1,16,512]{2,1,0:T(8,128)(2,1)S(1)}, u32[]{:S(2)}, u32[]{:S(2)}) %collective-permute-start.6) | collective-permute-done | bytes 16416 | tf_op jit(solution)/shard_map/ppermute | solution.py:30
  47.5 0.4 maximum_maximum_fusion.1
  48.0 0.0 collective-permute-done.7
  48.0 1.2 maximum_maximum_fusion.x_ref
  49.2 0.0 all-to-all-done
  49.2 1.6 %collective-permute-start.8 = (bf16[64,8,1920]{2,1,0:T(8,128)(2,1)S(1)}, bf16[64,8,1920]{2,1,0:T(8,128)(2,1)S(1)}, u32[]{:S(2)}, u32[]{:S(2)}) collective-permute-start(bf16[64,8,1920]{2,1,0:T(8,128)(2,1)S(1)} %all-to-all-done), channel_id=1, source_target_pairs={{0,1},{1,0},{2,3},{3,2},{4,5},{5,4},{6,7},{7,6},{8,9},{9,8},{10,11... | collective-permute-start | bytes 5898248 | tf_op jit(solution)/shard_map/ppermute | solution.py:679
  50.8 3.6 %collective-permute-done.8 = bf16[64,8,1920]{2,1,0:T(8,128)(2,1)S(1)} collective-permute-done((bf16[64,8,1920]{2,1,0:T(8,128)(2,1)S(1)}, bf16[64,8,1920]{2,1,0:T(8,128)(2,1)S(1)}, u32[]{:S(2)}, u32[]{:S(2)}) %collective-permute-start.8) | collective-permute-done | bytes 1966112 | tf_op jit(solution)/shard_map/ppermute | solution.py:679
  54.4 1.3 copy-done.1
  55.7 14.4 %norm_project_filter.1 = (bf16[512,1024]{1,0:T(8,128)(2,1)}, bf16[512,1024]{1,0:T(8,128)(2,1)}, bf16[512,128]{1,0:T(8,128)(2,1)}, bf16[512,128]{1,0:T(8,128)(2,1...) custom-call(bf16[832,512]{1,0:T(8,128)(2,1)} %maximum_maximum_fusion, ...), custom_call_target="tpu_custom_call" | custom-call | flops 872415232 | bytes 6291456 | tf_op jit(solution)/shard_map/norm_project_filter/pallas_call | solution.py:457
  70.2 0.0 copy-start.7
  70.2 7.1 %all-to-all-start.1 = ((bf16[32,16,1024]{2,1,0:T(8,128)(2,1)}), bf16[32,16,1024]{2,1,0:T(8,128)(2,1)S(1)}, u32[]{:S(2)}, u32[]{:S(2)}) async-start(bf16[32,16,1024]{2,1,0:T(8,128)(2,1)} %bitcast.41), calls=%async_computation.1 | async-start | bytes 2097152 | tf_op jit(solution)/shard_map/all_to_all | solution.py:698
  77.3 1.3 collective-permute-start.9
  78.5 1.7 %collective-permute-start.10 = (bf16[272,1024]{1,0:T(8,128)(2,1)}, bf16[272,1024]{1,0:T(8,128)(2,1)S(1)}, u32[]{:S(2)}, u32[]{:S(2)}) collective-permute-start(bf16[272,1024]{1,0:T(8,128)(2,1)} %get-tuple-element.36), channel_id=1, source_target_pairs={{0,64},{32,96},{64,0},{96,32},{1,65},{33,97},{65,1},{97,33},{2,66}... | collective-permute-start | bytes 1671176 | tf_op jit(solution)/shard_map/ppermute | solution.py:695
  80.2 2.0 %collective-permute-start.11 = (bf16[272,1024]{1,0:T(8,128)(2,1)S(1)}, bf16[272,1024]{1,0:T(8,128)(2,1)S(1)}, u32[]{:S(2)}, u32[]{:S(2)}) collective-permute-start(bf16[272,1024]{1,0:T(8,128)(2,1)S(1)} %copy-done.7), channel_id=1, source_target_pairs={{0,96},{32,0},{64,32},{96,64},{1,97},{33,1},{65,33},{97,65},{2,98}... | collective-permute-start | bytes 1671176 | tf_op jit(solution)/shard_map/ppermute | solution.py:695
  82.2 6.8 %mix_columns.1.local_ref = bf16[512,1024]{1,0:T(8,128)(2,1)} custom-call(bf16[512,1024]{1,0:T(8,128)(2,1)} %get-tuple-element.28.a_ref, bf16[512,128]{1,0:T(8,128)(2,1)} %get-tuple-element.29.coefs_ref, bf16[512,128]{1,0:T(8,128)(2,1)} %get-tuple-element.30.steps_ref, f32[512,128]{1,0:T(8,128)} %get-tuple-element.31.sums_ref), custom_call_target="tpu_custom_call" | custom-call | flops 4294967296 | bytes 3145728 | tf_op jit(solution)/shard_map/mix_columns/pallas_call | solution.py:516
  89.1 5.4 %all-to-all-done.1 = bf16[32,16,1024]{2,1,0:T(8,128)(2,1)S(1)} async-done(((bf16[32,16,1024]{2,1,0:T(8,128)(2,1)}), bf16[32,16,1024]{2,1,0:T(8,128)(2,1)S(1)}, u32[]{:S(2)}, u32[]{:S(2)}) %all-to-all-start.1) | async-done | bytes 1048608 | tf_op jit(solution)/shard_map/all_to_all | solution.py:698
  94.5 1.0 copy-done.4
  95.4 11.2 %sweep_rows.1 = bf16[512,1024]{1,0:T(8,128)(2,1)} custom-call(bf16[512,1024]{1,0:T(8,128)(2,1)} %bitcast.43, bf16[512,1920]{1,0:T(8,128)(2,1)} %bitcast.26, bf16[512,1920]{1,0:T(8,128)(2,1)} %bitcast.33, bf16[512,1920]{1,0:T(8,128)(2,1)} %bitcast.27, bf16[512,1920]{1,0:T(8,128)(2,1)} %bitcast.34, f32[4,32]{1,0:T(4,128)} %bias_ref.1, f32[4,32]{1,0:T(4,128)} %rate_ref.1), custom_call_target="tpu_custom_call" | custom-call | flops 6442450944 | bytes 3145728 | tf_op jit(solution)/shard_map/sweep_rows/pallas_call | solution.py:321
  106.6 0.0 collective-permute-done.9.refs_0_
  106.6 0.0 collective-permute-done.10.refs_1_
  106.6 0.0 collective-permute-done.11.refs_2_
  106.7 6.7 %all-to-all-start.2 = ((bf16[32,16,1024]{2,1,0:T(8,128)(2,1)}), bf16[32,16,1024]{2,1,0:T(8,128)(2,1)S(1)}, u32[]{:S(2)}, u32[]{:S(2)}) async-start(bf16[32,16,1024]{2,1,0:T(8,128)(2,1)} %bitcast.42), calls=%async_computation.2 | async-start | bytes 2097152 | tf_op jit(solution)/shard_map/all_to_all | solution.py:698
  113.4 9.4 %enter_columns.1 = (f32[512,1024]{1,0:T(8,128)}, bf16[512,1024]{1,0:T(8,128)(2,1)}, bf16[1024,512]{1,0:T(8,128)(2,1)}) custom-call(bf16[512,1024]{1,0:T(8,128)(2,1)} %mix_columns.1.local_ref, bf16[512,128]{1,0:T(8,128)(2,1)} %get-tuple-element.33.read_ref, bf16[512,1024]{1,0:T(8,128)(2,1)} %get-tuple-element.27.act_ref, f32[1,1024]{1,0:T(1,128)} %bitcast.51, ...), custom_call_target="tpu_custom_call" | custom-call | flops 4294967296 | bytes 12582912 | tf_op jit(solution)/shard_map/enter_columns/pallas_call | solution.py:596
  122.8 7.8 %all-to-all-done.2 = bf16[32,16,1024]{2,1,0:T(8,128)(2,1)S(1)} async-done(((bf16[32,16,1024]{2,1,0:T(8,128)(2,1)}), bf16[32,16,1024]{2,1,0:T(8,128)(2,1)S(1)}, u32[]{:S(2)}, u32[]{:S(2)}) %all-to-all-start.2) | async-done | bytes 1048608 | tf_op jit(solution)/shard_map/all_to_all | solution.py:698
  130.6 1.0 copy-done.2
  131.6 5.3 %gate_and_project.1 = bf16[512,512]{1,0:T(8,128)(2,1)} custom-call(f32[512,1024]{1,0:T(8,128)} %get-tuple-element.41.part_ref, bf16[512,1024]{1,0:T(8,128)(2,1)} %get-tuple-element.42.gate_ref, bf16[512,1024]{1,0:T(8,128)(2,1)} %bitcast.37, bf16[512,512]{1,0:T(8,128)(2,1)} %bitcast.40, bf16[1024,512]{1,0:T(8,128)(2,1)} %get-tuple-element.44.w_ref, ...), custom_call_target="tpu_custom_call" | custom-call | tf_op jit(solution)/shard_map/gate_and_project/pallas_call | solution.py:629
  (22 shorter events, 0.1 us)
Async XLA Ops:
  2.7 12.1 %copy-start.3 = (bf16[32,16,512]{2,1,0:T(8,128)(2,1)S(1)}, bf16[32,16,512]{2,1,0:T(8,128)(2,1)}, u32[]{:S(2)}) copy-start(bf16[32,16,512]{2,1,0:T(8,128)(2,1)} %param.12) | copy-start | bytes 1572868
  2.7 46.5 %all-to-all-start = ((bf16[64,8,1920]{2,1,0:T(8,128)(2,1)}), bf16[64,8,1920]{2,1,0:T(8,128)(2,1)S(1)}, u32[]{:S(2)}, u32[]{:S(2)}) async-start(bf16[64,8,1920]{2,1,0:T(8,128)(2,1)} %parcels.1), calls=%async_computation | async-start | bytes 3932160 | tf_op jit(solution)/shard_map/all_to_all | solution.py:658
  14.8 12.2 %collective-permute-start = (bf16[1,1,512]{2,0,1:T(2,128)(2,1)S(1)}, bf16[1,1,512]{2,0,1:T(2,128)(2,1)S(1)}, u32[]{:S(2)}, u32[]{:S(2)}) collective-permute-start(bf16[1,1,512]{2,0,1:T(2,128)(2,1)S(1)} %get-tuple-element.45), channel_id=1, source_target_pairs={{1,32},{2,33},{3,34},{4,35},{5,36},{6,37},{7,38},{8,39},{9,40},{10... | collective-permute-start | bytes 3080 | tf_op jit(solution)/shard_map/ppermute | solution.py:42
  18.9 24.2 %collective-permute-start.2 = (bf16[1,1,512]{2,0,1:T(2,128)(2,1)S(1)}, bf16[1,1,512]{2,0,1:T(2,128)(2,1)S(1)}, u32[]{:S(2)}, u32[]{:S(2)}) collective-permute-start(bf16[1,1,512]{2,0,1:T(2,128)(2,1)S(1)} %get-tuple-element.46), channel_id=1, source_target_pairs={{0,33},{1,34},{2,35},{3,36},{4,37},{5,38},{6,39},{7,40},{8,41},{9,... | collective-permute-start | bytes 3080 | tf_op jit(solution)/shard_map/ppermute | solution.py:42
  22.1 22.3 %collective-permute-start.4 = (bf16[1,1,512]{2,0,1:T(2,128)(2,1)S(1)}, bf16[1,1,512]{2,0,1:T(2,128)(2,1)S(1)}, u32[]{:S(2)}, u32[]{:S(2)}) collective-permute-start(bf16[1,1,512]{2,0,1:T(2,128)(2,1)S(1)} %get-tuple-element.47), channel_id=1, source_target_pairs={{32,1},{33,2},{34,3},{35,4},{36,5},{37,6},{38,7},{39,8},{40,9},{41... | collective-permute-start | bytes 3080 | tf_op jit(solution)/shard_map/ppermute | solution.py:42
  23.4 24.6 %collective-permute-start.7 = (bf16[1,1,512]{2,1,0:T(2,128)(2,1)S(1)}, bf16[1,1,512]{2,1,0:T(2,128)(2,1)S(1)}, u32[]{:S(2)}, u32[]{:S(2)}) collective-permute-start(bf16[1,1,512]{2,1,0:T(2,128)(2,1)S(1)} %get-tuple-element.48), channel_id=1, source_target_pairs={{33,0},{34,1},{35,2},{36,3},{37,4},{38,5},{39,6},{40,7},{41,8},{42... | collective-permute-start | bytes 3080 | tf_op jit(solution)/shard_map/ppermute | solution.py:42
  24.8 16.2 %collective-permute-start.1 = (bf16[32,1,512]{2,0,1:T(8,128)(2,1)S(1)}, bf16[32,1,512]{2,0,1:T(8,128)(2,1)S(1)}, u32[]{:S(2)}, u32[]{:S(2)}) collective-permute-start(bf16[32,1,512]{2,0,1:T(8,128)(2,1)S(1)} %copy.21), channel_id=1, source_target_pairs={{1,0},{2,1},{3,2},{4,3},{5,4},{6,5},{7,6},{8,7},{9,8},{10,9},{11,1... | collective-permute-start | bytes 98312 | tf_op jit(solution)/shard_map/ppermute | solution.py:30
  27.0 17.6 %collective-permute-start.5 = (bf16[1,16,512]{2,1,0:T(8,128)(2,1)S(1)}, bf16[1,16,512]{2,1,0:T(8,128)(2,1)S(1)}, u32[]{:S(2)}, u32[]{:S(2)}) collective-permute-start(bf16[1,16,512]{2,1,0:T(8,128)(2,1)S(1)} %get-tuple-element.51), channel_id=1, source_target_pairs={{0,32},{32,64},{64,96},{1,33},{33,65},{65,97},{2,34},{34,66},{66,9... | collective-permute-start | bytes 49160 | tf_op jit(solution)/shard_map/ppermute | solution.py:30
  41.0 3.3 %collective-permute-start.3 = (bf16[32,1,512]{2,0,1:T(8,128)(2,1)S(1)}, bf16[32,1,512]{2,0,1:T(8,128)(2,1)S(1)}, u32[]{:S(2)}, u32[]{:S(2)}) collective-permute-start(bf16[32,1,512]{2,0,1:T(8,128)(2,1)S(1)} %copy.23), channel_id=1, source_target_pairs={{0,1},{1,2},{2,3},{3,4},{4,5},{5,6},{6,7},{7,8},{8,9},{9,10},{10,1... | collective-permute-start | bytes 98312 | tf_op jit(solution)/shard_map/ppermute | solution.py:30
  43.1 4.5 %collective-permute-start.6 = (bf16[1,16,512]{2,1,0:T(8,128)(2,1)S(1)}, bf16[1,16,512]{2,1,0:T(8,128)(2,1)S(1)}, u32[]{:S(2)}, u32[]{:S(2)}) collective-permute-start(bf16[1,16,512]{2,1,0:T(8,128)(2,1)S(1)} %get-tuple-element.52), channel_id=1, source_target_pairs={{32,0},{64,32},{96,64},{33,1},{65,33},{97,65},{34,2},{66,34},{98,6... | collective-permute-start | bytes 49160 | tf_op jit(solution)/shard_map/ppermute | solution.py:30
  49.2 5.3 %copy-start = (bf16[64,8,1920]{2,1,0:T(8,128)(2,1)}, bf16[64,8,1920]{2,1,0:T(8,128)(2,1)S(1)}, u32[]{:S(2)}) copy-start(bf16[64,8,1920]{2,1,0:T(8,128)(2,1)S(1)} %all-to-all-done) | copy-start | bytes 5898244
  49.2 5.2 %collective-permute-start.8 = (bf16[64,8,1920]{2,1,0:T(8,128)(2,1)S(1)}, bf16[64,8,1920]{2,1,0:T(8,128)(2,1)S(1)}, u32[]{:S(2)}, u32[]{:S(2)}) collective-permute-start(bf16[64,8,1920]{2,1,0:T(8,128)(2,1)S(1)} %all-to-all-done), channel_id=1, source_target_pairs={{0,1},{1,0},{2,3},{3,2},{4,5},{5,4},{6,7},{7,6},{8,9},{9,8},{10,11... | collective-permute-start | bytes 5898248 | tf_op jit(solution)/shard_map/ppermute | solution.py:679
  54.4 1.3 copy-start.1
  70.2 10.1 %copy-start.7 = (bf16[272,1024]{1,0:T(8,128)(2,1)S(1)}, bf16[272,1024]{1,0:T(8,128)(2,1)}, u32[]{:S(2)}) copy-start(bf16[272,1024]{1,0:T(8,128)(2,1)} %get-tuple-element.37) | copy-start | bytes 1671172
  70.2 24.3 %all-to-all-start.1 = ((bf16[32,16,1024]{2,1,0:T(8,128)(2,1)}), bf16[32,16,1024]{2,1,0:T(8,128)(2,1)S(1)}, u32[]{:S(2)}, u32[]{:S(2)}) async-start(bf16[32,16,1024]{2,1,0:T(8,128)(2,1)} %bitcast.41), calls=%async_computation.1 | async-start | bytes 2097152 | tf_op jit(solution)/shard_map/all_to_all | solution.py:698
  77.3 29.4 %collective-permute-start.9 = (bf16[272,1024]{1,0:T(8,128)(2,1)}, bf16[272,1024]{1,0:T(8,128)(2,1)S(1)}, u32[]{:S(2)}, u32[]{:S(2)}) collective-permute-start(bf16[272,1024]{1,0:T(8,128)(2,1)} %get-tuple-element.35), channel_id=1, source_target_pairs={{0,32},{32,64},{64,96},{96,0},{1,33},{33,65},{65,97},{97,1},{2,34}... | collective-permute-start | bytes 1671176 | tf_op jit(solution)/shard_map/ppermute | solution.py:695
  78.5 28.1 %collective-permute-start.10 = (bf16[272,1024]{1,0:T(8,128)(2,1)}, bf16[272,1024]{1,0:T(8,128)(2,1)S(1)}, u32[]{:S(2)}, u32[]{:S(2)}) collective-permute-start(bf16[272,1024]{1,0:T(8,128)(2,1)} %get-tuple-element.36), channel_id=1, source_target_pairs={{0,64},{32,96},{64,0},{96,32},{1,65},{33,97},{65,1},{97,33},{2,66}... | collective-permute-start | bytes 1671176 | tf_op jit(solution)/shard_map/ppermute | solution.py:695
  80.2 26.4 %collective-permute-start.11 = (bf16[272,1024]{1,0:T(8,128)(2,1)S(1)}, bf16[272,1024]{1,0:T(8,128)(2,1)S(1)}, u32[]{:S(2)}, u32[]{:S(2)}) collective-permute-start(bf16[272,1024]{1,0:T(8,128)(2,1)S(1)} %copy-done.7), channel_id=1, source_target_pairs={{0,96},{32,0},{64,32},{96,64},{1,97},{33,1},{65,33},{97,65},{2,98}... | collective-permute-start | bytes 1671176 | tf_op jit(solution)/shard_map/ppermute | solution.py:695
  94.5 1.0 copy-start.4
  106.6 6.8 %copy-start.5 = (bf16[272,1024]{1,0:T(8,128)(2,1)}, bf16[272,1024]{1,0:T(8,128)(2,1)S(1)}, u32[]{:S(2)}) copy-start(bf16[272,1024]{1,0:T(8,128)(2,1)S(1)} %collective-permute-done.9.refs_0_) | copy-start | bytes 1671172
  106.6 6.8 %copy-start.6 = (bf16[272,1024]{1,0:T(8,128)(2,1)}, bf16[272,1024]{1,0:T(8,128)(2,1)S(1)}, u32[]{:S(2)}) copy-start(bf16[272,1024]{1,0:T(8,128)(2,1)S(1)} %collective-permute-done.10.refs_1_) | copy-start | bytes 1671172
  106.7 6.8 %copy-start.8 = (bf16[272,1024]{1,0:T(8,128)(2,1)}, bf16[272,1024]{1,0:T(8,128)(2,1)S(1)}, u32[]{:S(2)}) copy-start(bf16[272,1024]{1,0:T(8,128)(2,1)S(1)} %collective-permute-done.11.refs_2_) | copy-start | bytes 1671172
  106.7 23.9 %all-to-all-start.2 = ((bf16[32,16,1024]{2,1,0:T(8,128)(2,1)}), bf16[32,16,1024]{2,1,0:T(8,128)(2,1)S(1)}, u32[]{:S(2)}, u32[]{:S(2)}) async-start(bf16[32,16,1024]{2,1,0:T(8,128)(2,1)} %bitcast.42), calls=%async_computation.2 | async-start | bytes 2097152 | tf_op jit(solution)/shard_map/all_to_all | solution.py:698
  130.6 1.0 copy-start.2

commit v4 on v3

--- a/solution.py
+++ b/solution.py
@@ -92,7 +92,7 @@
 
 def parcels(mask, turned, w_out, w_proj, groups):
     width = 2 * turned.shape[1] + w_out.shape[1] + w_proj.shape[1] + LANES
-    block = 16
+    block = 32
     one = lambda i: (0, 0)
     return pl.pallas_call(
         parcel_kernel,
@@ -450,7 +450,7 @@
 def filtered(x, gain, own, other, taps, bias, tokens, dt_bias, rate, slots):
     expand = bias.shape[1]
     padded, channels = x.shape
-    width = 256
+    width = 1024
     states = tokens // BLOCK * STATE + 16
     one = lambda c: (0, 0)
     piece = pl.BlockSpec((width // 4, 2 * channels), lambda c: (c, 0))
@@ -494,28 +494,32 @@
         for d, matrix in enumerate(head_spread(a_ref.shape[1])):
             spread[d] = matrix
 
-    def store(span, lanes, value):
-        out_ref[span, lanes] = value
-
-    mix_chunk(
-        a_ref[...],
-        coefs_ref[...],
-        steps_ref[...].astype(f32),
-        sums_ref[...],
-        [spread[0], spread[1]],
-        scratch,
-        lambda lanes: None,
-        store,
-    )
+    for c in range(a_ref.shape[0] // CHUNK):
+        at = slice(c * CHUNK, (c + 1) * CHUNK)
+
+        def store(span, lanes, value):
+            out_ref[c * CHUNK + span.start : c * CHUNK + span.stop, lanes] = value
+
+        mix_chunk(
+            a_ref[at, :],
+            coefs_ref[at, :],
+            steps_ref[at, :].astype(f32),
+            sums_ref[at, :],
+            [spread[0], spread[1]],
+            scratch,
+            lambda lanes: None,
+            store,
+        )
 
 
 def mixed_columns(values, coefs, steps, sums):
     tokens, expand = values.shape
-    block = pl.BlockSpec((CHUNK, expand), lambda i: (i, 0))
-    thin = pl.BlockSpec((CHUNK, LANES), lambda i: (i, 0))
+    rows = 2 * CHUNK
+    block = pl.BlockSpec((rows, expand), lambda i: (i, 0))
+    thin = pl.BlockSpec((rows, LANES), lambda i: (i, 0))
     return pl.pallas_call(
         mix_kernel,
-        grid=(tokens // CHUNK,),
+        grid=(tokens // rows,),
         in_specs=[block, thin, thin, thin],
         out_specs=block,
         out_shape=jax.ShapeDtypeStruct((tokens, expand), bf16),
@@ -622,7 +626,7 @@
 def projected(part, gate, rows, x, w_out, out_gain):
     tokens, expand = part.shape
     channels = x.shape[1]
-    block = 128
+    block = 256
     one = lambda i: (0, 0)
     wide = pl.BlockSpec((block, expand), lambda i: (i, 0))
     narrow = pl.BlockSpec((block, channels), lambda i: (i, 0))

time: 138 us -> 133 us (0.964)
  Pallas kernels: 49.8 us -> 45.4 us
    pallas_call x1, Pallas kernels: 14.4 us -> 11.8 us  [filtered(): pl.pallas_call(filter_kernel, grid=(expand // width,), in_specs=[pl.Block...]
  transfers between devices with their start and end apart: 15 -> 15, of which waited for: 4 -> 4; matrix products, arithmetic and copies ran while one was open for 2% -> 2% of each run, Pallas kernels for 20% -> 21%
where the time goes in v4:
time: 133 us
  starting transfers between devices  61.6 us (46%)
  Pallas kernels  45.4 us (34%)
  waiting for transfers between devices  20 us (15%)
  local copies, waits for them, and re-layouts  3.71 us (3%)
  other arithmetic  1.71 us (1%)
    ppermute x4, starting transfers between devices, shifted(): return lax.ppermute(x, axis, pairs)  19.2 us
    all_to_all x2, starting transfers between devices, dealt(): lax.all_to_all(x.reshape(-1, breadth, expand), wide, 0, 0, tiled=True)  13.9 us
    all_to_all x2, waiting for transfers between devices, dealt(): lax.all_to_all(x.reshape(-1, breadth, expand), wide, 0, 0, tiled=True)  13.4 us
    all_to_all x1, starting transfers between devices, on_device(): own = lax.all_to_all(parcel, ('row', 'chip'), 0, 0, tiled=True)  12.1 us
    pallas_call x1, Pallas kernels, filtered(): pl.pallas_call(filter_kernel, grid=(expand // width,), in_specs=[pl.Block...  11.8 us
    pallas_call x1, Pallas kernels, swept_lines(): pl.pallas_call(line_kernel, grid=(1,), in_specs=[pl.BlockSpec((length, ex...  11.2 us
    ppermute x4, starting transfers between devices, diagonal(): return lax.ppermute(x, axes, pairs)  9.87 us
    pallas_call x1, Pallas kernels, entered(): pl.pallas_call(entering_kernel, grid=(1,), in_specs=[whole(a) for a in (l...  9.36 us
  transfers between devices with their start and end apart: 15, of which 4 were waited for; matrix products, arithmetic and copies ran while one was open for 2% of the time, Pallas kernels for 21%

profile of v4, /device:TPU:1, one launch (start us, length us, event | category | flops | bytes accessed | tf_op | source)
XLA Modules:
  0.0 132.6 jit_solution(18124178753333418992)
XLA Ops:
  0.0 2.1 %parcels.1 = bf16[64,8,1920]{2,1,0:T(8,128)(2,1)} custom-call(s32[1,2]{1,0:T(1,128)} %bitcast.50, bf16[16,512]{1,0:T(8,128)(2,1)} %bitcast.44, bf16[8,512]{1,0:T(8,128)(2,1)} %out_ref.1, bf16[8,256]{1,0:T(8,128)(2,1)} %proj_ref.1), custom_call_target="tpu_custom_call" | custom-call | tf_op jit(solution)/shard_map/parcels/pallas_call | solution.py:97
  2.1 12.1 %all-to-all-start = ((bf16[64,8,1920]{2,1,0:T(8,128)(2,1)}), bf16[64,8,1920]{2,1,0:T(8,128)(2,1)S(1)}, u32[]{:S(2)}, u32[]{:S(2)}) async-start(bf16[64,8,1920]{2,1,0:T(8,128)(2,1)} %parcels.1), calls=%async_computation | async-start | bytes 3932160 | tf_op jit(solution)/shard_map/all_to_all | solution.py:662
  14.2 0.0 copy-done.3
  14.2 4.0 %collective-permute-start = (bf16[1,1,512]{2,0,1:T(2,128)(2,1)S(1)}, bf16[1,1,512]{2,0,1:T(2,128)(2,1)S(1)}, u32[]{:S(2)}, u32[]{:S(2)}) collective-permute-start(bf16[1,1,512]{2,0,1:T(2,128)(2,1)S(1)} %get-tuple-element.45), channel_id=1, source_target_pairs={{1,32},{2,33},{3,34},{4,35},{5,36},{6,37},{7,38},{8,39},{9,40},{10... | collective-permute-start | bytes 3080 | tf_op jit(solution)/shard_map/ppermute | solution.py:42
  18.3 3.2 %collective-permute-start.2 = (bf16[1,1,512]{2,0,1:T(2,128)(2,1)S(1)}, bf16[1,1,512]{2,0,1:T(2,128)(2,1)S(1)}, u32[]{:S(2)}, u32[]{:S(2)}) collective-permute-start(bf16[1,1,512]{2,0,1:T(2,128)(2,1)S(1)} %get-tuple-element.46), channel_id=1, source_target_pairs={{0,33},{1,34},{2,35},{3,36},{4,37},{5,38},{6,39},{7,40},{8,41},{9,... | collective-permute-start | bytes 3080 | tf_op jit(solution)/shard_map/ppermute | solution.py:42
  21.5 1.3 collective-permute-start.4
  22.8 1.3 collective-permute-start.7
  24.1 0.1 fusion
  24.3 1.9 %collective-permute-start.1 = (bf16[32,1,512]{2,0,1:T(8,128)(2,1)S(1)}, bf16[32,1,512]{2,0,1:T(8,128)(2,1)S(1)}, u32[]{:S(2)}, u32[]{:S(2)}) collective-permute-start(bf16[32,1,512]{2,0,1:T(8,128)(2,1)S(1)} %copy.21), channel_id=1, source_target_pairs={{1,0},{2,1},{3,2},{4,3},{5,4},{6,5},{7,6},{8,7},{9,8},{10,9},{11,1... | collective-permute-start | bytes 98312 | tf_op jit(solution)/shard_map/ppermute | solution.py:30
  26.2 0.1 pad.4.clone
  26.3 0.1 pad.2.clone
  26.4 0.0 collective-permute-done
  26.4 14.1 %collective-permute-start.5 = (bf16[1,16,512]{2,1,0:T(8,128)(2,1)S(1)}, bf16[1,16,512]{2,1,0:T(8,128)(2,1)S(1)}, u32[]{:S(2)}, u32[]{:S(2)}) collective-permute-start(bf16[1,16,512]{2,1,0:T(8,128)(2,1)S(1)} %get-tuple-element.51), channel_id=1, source_target_pairs={{0,32},{32,64},{64,96},{1,33},{33,65},{65,97},{2,34},{34,66},{66,9... | collective-permute-start | bytes 49160 | tf_op jit(solution)/shard_map/ppermute | solution.py:30
  40.5 0.0 collective-permute-done.1
  40.5 1.9 %collective-permute-start.3 = (bf16[32,1,512]{2,0,1:T(8,128)(2,1)S(1)}, bf16[32,1,512]{2,0,1:T(8,128)(2,1)S(1)}, u32[]{:S(2)}, u32[]{:S(2)}) collective-permute-start(bf16[32,1,512]{2,0,1:T(8,128)(2,1)S(1)} %copy.23), channel_id=1, source_target_pairs={{0,1},{1,2},{2,3},{3,4},{4,5},{5,6},{6,7},{7,8},{8,9},{9,10},{10,1... | collective-permute-start | bytes 98312 | tf_op jit(solution)/shard_map/ppermute | solution.py:30
  42.4 0.1 pad_maximum_fusion
  42.5 0.0 collective-permute-done.2
  42.5 1.3 collective-permute-start.6
  43.8 0.0 collective-permute-done.4
  43.8 0.0 collective-permute-done.3
  43.9 0.1 copy.19
  43.9 0.1 copy.18
  44.0 0.0 collective-permute-done.5
  44.0 3.0 %collective-permute-done.6 = bf16[1,16,512]{2,1,0:T(8,128)(2,1)S(1)} collective-permute-done((bf16[1,16,512]{2,1,0:T(8,128)(2,1)S(1)}, bf16[1,16,512]{2,1,0:T(8,128)(2,1)S(1)}, u32[]{:S(2)}, u32[]{:S(2)}) %collective-permute-start.6) | collective-permute-done | bytes 16416 | tf_op jit(solution)/shard_map/ppermute | solution.py:30
  47.0 0.4 maximum_maximum_fusion.1
  47.4 0.0 collective-permute-done.7
  47.4 1.2 maximum_maximum_fusion.x_ref
  48.6 0.0 all-to-all-done
  48.6 1.6 %collective-permute-start.8 = (bf16[64,8,1920]{2,1,0:T(8,128)(2,1)S(1)}, bf16[64,8,1920]{2,1,0:T(8,128)(2,1)S(1)}, u32[]{:S(2)}, u32[]{:S(2)}) collective-permute-start(bf16[64,8,1920]{2,1,0:T(8,128)(2,1)S(1)} %all-to-all-done), channel_id=1, source_target_pairs={{0,1},{1,0},{2,3},{3,2},{4,5},{5,4},{6,7},{7,6},{8,9},{9,8},{10,11... | collective-permute-start | bytes 5898248 | tf_op jit(solution)/shard_map/ppermute | solution.py:683
  50.3 3.6 %collective-permute-done.8 = bf16[64,8,1920]{2,1,0:T(8,128)(2,1)S(1)} collective-permute-done((bf16[64,8,1920]{2,1,0:T(8,128)(2,1)S(1)}, bf16[64,8,1920]{2,1,0:T(8,128)(2,1)S(1)}, u32[]{:S(2)}, u32[]{:S(2)}) %collective-permute-start.8) | collective-permute-done | bytes 1966112 | tf_op jit(solution)/shard_map/ppermute | solution.py:683
  53.9 1.3 copy-done.1
  55.2 11.8 %norm_project_filter.1 = (bf16[512,1024]{1,0:T(8,128)(2,1)}, bf16[512,1024]{1,0:T(8,128)(2,1)}, bf16[512,128]{1,0:T(8,128)(2,1)}, bf16[512,128]{1,0:T(8,128)(2,1...) custom-call(bf16[832,512]{1,0:T(8,128)(2,1)} %maximum_maximum_fusion, ...), custom_call_target="tpu_custom_call" | custom-call | flops 872415232 | bytes 6291456 | tf_op jit(solution)/shard_map/norm_project_filter/pallas_call | solution.py:457
  67.0 7.1 %all-to-all-start.1 = ((bf16[32,16,1024]{2,1,0:T(8,128)(2,1)}), bf16[32,16,1024]{2,1,0:T(8,128)(2,1)S(1)}, u32[]{:S(2)}, u32[]{:S(2)}) async-start(bf16[32,16,1024]{2,1,0:T(8,128)(2,1)} %bitcast.41), calls=%async_computation.1 | async-start | bytes 2097152 | tf_op jit(solution)/shard_map/all_to_all | solution.py:702
  74.1 1.2 collective-permute-start.9
  75.3 1.7 %collective-permute-start.10 = (bf16[272,1024]{1,0:T(8,128)(2,1)}, bf16[272,1024]{1,0:T(8,128)(2,1)S(1)}, u32[]{:S(2)}, u32[]{:S(2)}) collective-permute-start(bf16[272,1024]{1,0:T(8,128)(2,1)} %get-tuple-element.36), channel_id=1, source_target_pairs={{0,64},{32,96},{64,0},{96,32},{1,65},{33,97},{65,1},{97,33},{2,66}... | collective-permute-start | bytes 1671176 | tf_op jit(solution)/shard_map/ppermute | solution.py:699
  77.0 2.0 %collective-permute-start.11 = (bf16[272,1024]{1,0:T(8,128)(2,1)S(1)}, bf16[272,1024]{1,0:T(8,128)(2,1)S(1)}, u32[]{:S(2)}, u32[]{:S(2)}) collective-permute-start(bf16[272,1024]{1,0:T(8,128)(2,1)S(1)} %copy-done.7), channel_id=1, source_target_pairs={{0,96},{32,0},{64,32},{96,64},{1,97},{33,1},{65,33},{97,65},{2,98}... | collective-permute-start | bytes 1671176 | tf_op jit(solution)/shard_map/ppermute | solution.py:699
  79.0 6.7 %mix_columns.1.local_ref = bf16[512,1024]{1,0:T(8,128)(2,1)} custom-call(bf16[512,1024]{1,0:T(8,128)(2,1)} %get-tuple-element.28.a_ref, bf16[512,128]{1,0:T(8,128)(2,1)} %get-tuple-element.29.coefs_ref, bf16[512,128]{1,0:T(8,128)(2,1)} %get-tuple-element.30.steps_ref, f32[512,128]{1,0:T(8,128)} %get-tuple-element.31.sums_ref), custom_call_target="tpu_custom_call" | custom-call | flops 4294967296 | bytes 3145728 | tf_op jit(solution)/shard_map/mix_columns/pallas_call | solution.py:520
  85.7 5.6 %all-to-all-done.1 = bf16[32,16,1024]{2,1,0:T(8,128)(2,1)S(1)} async-done(((bf16[32,16,1024]{2,1,0:T(8,128)(2,1)}), bf16[32,16,1024]{2,1,0:T(8,128)(2,1)S(1)}, u32[]{:S(2)}, u32[]{:S(2)}) %all-to-all-start.1) | async-done | bytes 1048608 | tf_op jit(solution)/shard_map/all_to_all | solution.py:702
  91.3 1.0 copy-done.4
  92.3 11.2 %sweep_rows.1 = bf16[512,1024]{1,0:T(8,128)(2,1)} custom-call(bf16[512,1024]{1,0:T(8,128)(2,1)} %bitcast.43, bf16[512,1920]{1,0:T(8,128)(2,1)} %bitcast.26, bf16[512,1920]{1,0:T(8,128)(2,1)} %bitcast.33, bf16[512,1920]{1,0:T(8,128)(2,1)} %bitcast.27, bf16[512,1920]{1,0:T(8,128)(2,1)} %bitcast.34, f32[4,32]{1,0:T(4,128)} %bias_ref.1, f32[4,32]{1,0:T(4,128)} %rate_ref.1), custom_call_target="tpu_custom_call" | custom-call | flops 6442450944 | bytes 3145728 | tf_op jit(solution)/shard_map/sweep_rows/pallas_call | solution.py:321
  103.5 0.0 collective-permute-done.9.refs_0_
  103.5 0.0 collective-permute-done.10.refs_1_
  103.5 0.0 collective-permute-done.11.refs_2_
  103.5 6.7 %all-to-all-start.2 = ((bf16[32,16,1024]{2,1,0:T(8,128)(2,1)}), bf16[32,16,1024]{2,1,0:T(8,128)(2,1)S(1)}, u32[]{:S(2)}, u32[]{:S(2)}) async-start(bf16[32,16,1024]{2,1,0:T(8,128)(2,1)} %bitcast.42), calls=%async_computation.2 | async-start | bytes 2097152 | tf_op jit(solution)/shard_map/all_to_all | solution.py:702
  110.3 9.4 %enter_columns.1 = (f32[512,1024]{1,0:T(8,128)}, bf16[512,1024]{1,0:T(8,128)(2,1)}, bf16[1024,512]{1,0:T(8,128)(2,1)}) custom-call(bf16[512,1024]{1,0:T(8,128)(2,1)} %mix_columns.1.local_ref, bf16[512,128]{1,0:T(8,128)(2,1)} %get-tuple-element.33.read_ref, bf16[512,1024]{1,0:T(8,128)(2,1)} %get-tuple-element.27.act_ref, f32[1,1024]{1,0:T(1,128)} %bitcast.51, ...), custom_call_target="tpu_custom_call" | custom-call | flops 4294967296 | bytes 12582912 | tf_op jit(solution)/shard_map/enter_columns/pallas_call | solution.py:600
  119.6 7.8 %all-to-all-done.2 = bf16[32,16,1024]{2,1,0:T(8,128)(2,1)S(1)} async-done(((bf16[32,16,1024]{2,1,0:T(8,128)(2,1)}), bf16[32,16,1024]{2,1,0:T(8,128)(2,1)S(1)}, u32[]{:S(2)}, u32[]{:S(2)}) %all-to-all-start.2) | async-done | bytes 1048608 | tf_op jit(solution)/shard_map/all_to_all | solution.py:702
  127.4 1.0 copy-done.2
  128.4 4.2 %gate_and_project.1 = bf16[512,512]{1,0:T(8,128)(2,1)} custom-call(f32[512,1024]{1,0:T(8,128)} %get-tuple-element.41.part_ref, bf16[512,1024]{1,0:T(8,128)(2,1)} %get-tuple-element.42.gate_ref, bf16[512,1024]{1,0:T(8,128)(2,1)} %bitcast.37, bf16[512,512]{1,0:T(8,128)(2,1)} %bitcast.40, bf16[1024,512]{1,0:T(8,128)(2,1)} %get-tuple-element.44.w_ref, ...), custom_call_target="tpu_custom_call" | custom-call | tf_op jit(solution)/shard_map/gate_and_project/pallas_call | solution.py:633
  (22 shorter events, 0.1 us)
Async XLA Ops:
  2.1 12.1 %copy-start.3 = (bf16[32,16,512]{2,1,0:T(8,128)(2,1)S(1)}, bf16[32,16,512]{2,1,0:T(8,128)(2,1)}, u32[]{:S(2)}) copy-start(bf16[32,16,512]{2,1,0:T(8,128)(2,1)} %param.12) | copy-start | bytes 1572868
  2.1 46.5 %all-to-all-start = ((bf16[64,8,1920]{2,1,0:T(8,128)(2,1)}), bf16[64,8,1920]{2,1,0:T(8,128)(2,1)S(1)}, u32[]{:S(2)}, u32[]{:S(2)}) async-start(bf16[64,8,1920]{2,1,0:T(8,128)(2,1)} %parcels.1), calls=%async_computation | async-start | bytes 3932160 | tf_op jit(solution)/shard_map/all_to_all | solution.py:662
  14.2 12.2 %collective-permute-start = (bf16[1,1,512]{2,0,1:T(2,128)(2,1)S(1)}, bf16[1,1,512]{2,0,1:T(2,128)(2,1)S(1)}, u32[]{:S(2)}, u32[]{:S(2)}) collective-permute-start(bf16[1,1,512]{2,0,1:T(2,128)(2,1)S(1)} %get-tuple-element.45), channel_id=1, source_target_pairs={{1,32},{2,33},{3,34},{4,35},{5,36},{6,37},{7,38},{8,39},{9,40},{10... | collective-permute-start | bytes 3080 | tf_op jit(solution)/shard_map/ppermute | solution.py:42
  18.3 24.2 %collective-permute-start.2 = (bf16[1,1,512]{2,0,1:T(2,128)(2,1)S(1)}, bf16[1,1,512]{2,0,1:T(2,128)(2,1)S(1)}, u32[]{:S(2)}, u32[]{:S(2)}) collective-permute-start(bf16[1,1,512]{2,0,1:T(2,128)(2,1)S(1)} %get-tuple-element.46), channel_id=1, source_target_pairs={{0,33},{1,34},{2,35},{3,36},{4,37},{5,38},{6,39},{7,40},{8,41},{9,... | collective-permute-start | bytes 3080 | tf_op jit(solution)/shard_map/ppermute | solution.py:42
  21.5 22.3 %collective-permute-start.4 = (bf16[1,1,512]{2,0,1:T(2,128)(2,1)S(1)}, bf16[1,1,512]{2,0,1:T(2,128)(2,1)S(1)}, u32[]{:S(2)}, u32[]{:S(2)}) collective-permute-start(bf16[1,1,512]{2,0,1:T(2,128)(2,1)S(1)} %get-tuple-element.47), channel_id=1, source_target_pairs={{32,1},{33,2},{34,3},{35,4},{36,5},{37,6},{38,7},{39,8},{40,9},{41... | collective-permute-start | bytes 3080 | tf_op jit(solution)/shard_map/ppermute | solution.py:42
  22.8 24.6 %collective-permute-start.7 = (bf16[1,1,512]{2,1,0:T(2,128)(2,1)S(1)}, bf16[1,1,512]{2,1,0:T(2,128)(2,1)S(1)}, u32[]{:S(2)}, u32[]{:S(2)}) collective-permute-start(bf16[1,1,512]{2,1,0:T(2,128)(2,1)S(1)} %get-tuple-element.48), channel_id=1, source_target_pairs={{33,0},{34,1},{35,2},{36,3},{37,4},{38,5},{39,6},{40,7},{41,8},{42... | collective-permute-start | bytes 3080 | tf_op jit(solution)/shard_map/ppermute | solution.py:42
  24.3 16.2 %collective-permute-start.1 = (bf16[32,1,512]{2,0,1:T(8,128)(2,1)S(1)}, bf16[32,1,512]{2,0,1:T(8,128)(2,1)S(1)}, u32[]{:S(2)}, u32[]{:S(2)}) collective-permute-start(bf16[32,1,512]{2,0,1:T(8,128)(2,1)S(1)} %copy.21), channel_id=1, source_target_pairs={{1,0},{2,1},{3,2},{4,3},{5,4},{6,5},{7,6},{8,7},{9,8},{10,9},{11,1... | collective-permute-start | bytes 98312 | tf_op jit(solution)/shard_map/ppermute | solution.py:30
  26.4 17.6 %collective-permute-start.5 = (bf16[1,16,512]{2,1,0:T(8,128)(2,1)S(1)}, bf16[1,16,512]{2,1,0:T(8,128)(2,1)S(1)}, u32[]{:S(2)}, u32[]{:S(2)}) collective-permute-start(bf16[1,16,512]{2,1,0:T(8,128)(2,1)S(1)} %get-tuple-element.51), channel_id=1, source_target_pairs={{0,32},{32,64},{64,96},{1,33},{33,65},{65,97},{2,34},{34,66},{66,9... | collective-permute-start | bytes 49160 | tf_op jit(solution)/shard_map/ppermute | solution.py:30
  40.5 3.3 %collective-permute-start.3 = (bf16[32,1,512]{2,0,1:T(8,128)(2,1)S(1)}, bf16[32,1,512]{2,0,1:T(8,128)(2,1)S(1)}, u32[]{:S(2)}, u32[]{:S(2)}) collective-permute-start(bf16[32,1,512]{2,0,1:T(8,128)(2,1)S(1)} %copy.23), channel_id=1, source_target_pairs={{0,1},{1,2},{2,3},{3,4},{4,5},{5,6},{6,7},{7,8},{8,9},{9,10},{10,1... | collective-permute-start | bytes 98312 | tf_op jit(solution)/shard_map/ppermute | solution.py:30
  42.5 4.5 %collective-permute-start.6 = (bf16[1,16,512]{2,1,0:T(8,128)(2,1)S(1)}, bf16[1,16,512]{2,1,0:T(8,128)(2,1)S(1)}, u32[]{:S(2)}, u32[]{:S(2)}) collective-permute-start(bf16[1,16,512]{2,1,0:T(8,128)(2,1)S(1)} %get-tuple-element.52), channel_id=1, source_target_pairs={{32,0},{64,32},{96,64},{33,1},{65,33},{97,65},{34,2},{66,34},{98,6... | collective-permute-start | bytes 49160 | tf_op jit(solution)/shard_map/ppermute | solution.py:30
  48.6 5.3 %copy-start = (bf16[64,8,1920]{2,1,0:T(8,128)(2,1)}, bf16[64,8,1920]{2,1,0:T(8,128)(2,1)S(1)}, u32[]{:S(2)}) copy-start(bf16[64,8,1920]{2,1,0:T(8,128)(2,1)S(1)} %all-to-all-done) | copy-start | bytes 5898244
  48.6 5.2 %collective-permute-start.8 = (bf16[64,8,1920]{2,1,0:T(8,128)(2,1)S(1)}, bf16[64,8,1920]{2,1,0:T(8,128)(2,1)S(1)}, u32[]{:S(2)}, u32[]{:S(2)}) collective-permute-start(bf16[64,8,1920]{2,1,0:T(8,128)(2,1)S(1)} %all-to-all-done), channel_id=1, source_target_pairs={{0,1},{1,0},{2,3},{3,2},{4,5},{5,4},{6,7},{7,6},{8,9},{9,8},{10,11... | collective-permute-start | bytes 5898248 | tf_op jit(solution)/shard_map/ppermute | solution.py:683
  53.9 1.3 copy-start.1
  67.0 10.1 %copy-start.7 = (bf16[272,1024]{1,0:T(8,128)(2,1)S(1)}, bf16[272,1024]{1,0:T(8,128)(2,1)}, u32[]{:S(2)}) copy-start(bf16[272,1024]{1,0:T(8,128)(2,1)} %get-tuple-element.37) | copy-start | bytes 1671172
  67.0 24.3 %all-to-all-start.1 = ((bf16[32,16,1024]{2,1,0:T(8,128)(2,1)}), bf16[32,16,1024]{2,1,0:T(8,128)(2,1)S(1)}, u32[]{:S(2)}, u32[]{:S(2)}) async-start(bf16[32,16,1024]{2,1,0:T(8,128)(2,1)} %bitcast.41), calls=%async_computation.1 | async-start | bytes 2097152 | tf_op jit(solution)/shard_map/all_to_all | solution.py:702
  74.1 29.4 %collective-permute-start.9 = (bf16[272,1024]{1,0:T(8,128)(2,1)}, bf16[272,1024]{1,0:T(8,128)(2,1)S(1)}, u32[]{:S(2)}, u32[]{:S(2)}) collective-permute-start(bf16[272,1024]{1,0:T(8,128)(2,1)} %get-tuple-element.35), channel_id=1, source_target_pairs={{0,32},{32,64},{64,96},{96,0},{1,33},{33,65},{65,97},{97,1},{2,34}... | collective-permute-start | bytes 1671176 | tf_op jit(solution)/shard_map/ppermute | solution.py:699
  75.3 28.1 %collective-permute-start.10 = (bf16[272,1024]{1,0:T(8,128)(2,1)}, bf16[272,1024]{1,0:T(8,128)(2,1)S(1)}, u32[]{:S(2)}, u32[]{:S(2)}) collective-permute-start(bf16[272,1024]{1,0:T(8,128)(2,1)} %get-tuple-element.36), channel_id=1, source_target_pairs={{0,64},{32,96},{64,0},{96,32},{1,65},{33,97},{65,1},{97,33},{2,66}... | collective-permute-start | bytes 1671176 | tf_op jit(solution)/shard_map/ppermute | solution.py:699
  77.0 26.5 %collective-permute-start.11 = (bf16[272,1024]{1,0:T(8,128)(2,1)S(1)}, bf16[272,1024]{1,0:T(8,128)(2,1)S(1)}, u32[]{:S(2)}, u32[]{:S(2)}) collective-permute-start(bf16[272,1024]{1,0:T(8,128)(2,1)S(1)} %copy-done.7), channel_id=1, source_target_pairs={{0,96},{32,0},{64,32},{96,64},{1,97},{33,1},{65,33},{97,65},{2,98}... | collective-permute-start | bytes 1671176 | tf_op jit(solution)/shard_map/ppermute | solution.py:699
  91.3 1.0 copy-start.4
  103.5 6.8 %copy-start.5 = (bf16[272,1024]{1,0:T(8,128)(2,1)}, bf16[272,1024]{1,0:T(8,128)(2,1)S(1)}, u32[]{:S(2)}) copy-start(bf16[272,1024]{1,0:T(8,128)(2,1)S(1)} %collective-permute-done.9.refs_0_) | copy-start | bytes 1671172
  103.5 6.8 %copy-start.6 = (bf16[272,1024]{1,0:T(8,128)(2,1)}, bf16[272,1024]{1,0:T(8,128)(2,1)S(1)}, u32[]{:S(2)}) copy-start(bf16[272,1024]{1,0:T(8,128)(2,1)S(1)} %collective-permute-done.10.refs_1_) | copy-start | bytes 1671172
  103.5 6.8 %copy-start.8 = (bf16[272,1024]{1,0:T(8,128)(2,1)}, bf16[272,1024]{1,0:T(8,128)(2,1)S(1)}, u32[]{:S(2)}) copy-start(bf16[272,1024]{1,0:T(8,128)(2,1)S(1)} %collective-permute-done.11.refs_2_) | copy-start | bytes 1671172
  103.5 23.9 %all-to-all-start.2 = ((bf16[32,16,1024]{2,1,0:T(8,128)(2,1)}), bf16[32,16,1024]{2,1,0:T(8,128)(2,1)S(1)}, u32[]{:S(2)}, u32[]{:S(2)}) async-start(bf16[32,16,1024]{2,1,0:T(8,128)(2,1)} %bitcast.42), calls=%async_computation.2 | async-start | bytes 2097152 | tf_op jit(solution)/shard_map/all_to_all | solution.py:702
  127.4 1.0 copy-start.2

commit v5 on v4

--- a/solution.py
+++ b/solution.py
@@ -339,7 +339,7 @@
             pltpu.VMEM((2, length // BLOCK * STATE, expand), bf16),
             *mixing_scratch(),
         ],
-        compiler_params=pltpu.CompilerParams(vmem_limit_bytes=GRANT),
+        compiler_params=pltpu.CompilerParams(vmem_limit_bytes=30 * 2**20),
         cost_estimate=pl.CostEstimate(
             flops=6 * 2**30, bytes_accessed=3 * 2**20, transcendentals=2**21
         ),
@@ -432,7 +432,8 @@
                 + pltpu.roll(right, span - 1, 0)
                 + bias_ref[:, lanes]
             )
-            activated = convolved / (1.0 + jnp.exp(-convolved))
+            half = 0.5 * convolved
+            activated = half + half * jnp.tanh(half)
             kept = activated[: rows * STRIDE].reshape(rows, STRIDE, LANES)[:, 8:, :]
             act_ref[h * breadth : (h + rows) * breadth, lanes] = kept.reshape(
                 rows * breadth, LANES

time: 133 us -> 133 us (level)
    pallas_call x1, Pallas kernels: 11.2 us -> 9.83 us  [swept_lines(): pl.pallas_call(line_kernel, grid=(1,), in_specs=[pl.BlockSpec((length, ex...]
    unnamed x21 -> x19, local copies, waits for them, and re-layouts: 3.33 us -> 3.86 us
  transfers between devices with their start and end apart: 15 -> 15, of which waited for: 4 -> 4; matrix products, arithmetic and copies ran while one was open for 2% -> 2% of each run, Pallas kernels for 21% -> 20%
where the time goes in v5:
time: 133 us; the launch traced here: 132 us
  starting transfers between devices  62.4 us (47%)
  Pallas kernels  44.1 us (33%)
  waiting for transfers between devices  19.9 us (15%)
  local copies, waits for them, and re-layouts  4.25 us (3%)
  other arithmetic  1.69 us (1%)
    ppermute x4, starting transfers between devices, shifted(): return lax.ppermute(x, axis, pairs)  19.2 us
    all_to_all x2, starting transfers between devices, dealt(): lax.all_to_all(x.reshape(-1, breadth, expand), wide, 0, 0, tiled=True)  14.6 us
    all_to_all x2, waiting for transfers between devices, dealt(): lax.all_to_all(x.reshape(-1, breadth, expand), wide, 0, 0, tiled=True)  13.2 us
    all_to_all x1, starting transfers between devices, on_device(): own = lax.all_to_all(parcel, ('row', 'chip'), 0, 0, tiled=True)  12.1 us
    pallas_call x1, Pallas kernels, filtered(): pl.pallas_call(filter_kernel, grid=(expand // width,), in_specs=[pl.Block...  11.8 us
    ppermute x4, starting transfers between devices, diagonal(): return lax.ppermute(x, axes, pairs)  9.87 us
    pallas_call x1, Pallas kernels, swept_lines(): pl.pallas_call(line_kernel, grid=(1,), in_specs=[pl.BlockSpec((length, ex...  9.83 us
    pallas_call x1, Pallas kernels, entered(): pl.pallas_call(entering_kernel, grid=(1,), in_specs=[whole(a) for a in (l...  9.36 us
  transfers between devices with their start and end apart: 15, of which 4 were waited for; matrix products, arithmetic and copies ran while one was open for 2% of the time, Pallas kernels for 20%

profile of v5, /device:TPU:1, one launch (start us, length us, event | category | flops | bytes accessed | tf_op | source)
XLA Modules:
  0.0 132.5 jit_solution(4159125263882084347)
XLA Ops:
  0.0 2.1 %parcels.1 = bf16[64,8,1920]{2,1,0:T(8,128)(2,1)} custom-call(s32[1,2]{1,0:T(1,128)} %bitcast.49, bf16[16,512]{1,0:T(8,128)(2,1)} %bitcast.43, bf16[8,512]{1,0:T(8,128)(2,1)} %out_ref.1, bf16[8,256]{1,0:T(8,128)(2,1)} %proj_ref.1), custom_call_target="tpu_custom_call" | custom-call | tf_op jit(solution)/shard_map/parcels/pallas_call | solution.py:97
  2.1 12.1 %all-to-all-start = ((bf16[64,8,1920]{2,1,0:T(8,128)(2,1)}), bf16[64,8,1920]{2,1,0:T(8,128)(2,1)S(1)}, u32[]{:S(2)}, u32[]{:S(2)}) async-start(bf16[64,8,1920]{2,1,0:T(8,128)(2,1)} %parcels.1), calls=%async_computation | async-start | bytes 3932160 | tf_op jit(solution)/shard_map/all_to_all | solution.py:663
  14.2 4.0 %collective-permute-start = (bf16[1,1,512]{2,0,1:T(2,128)(2,1)S(1)}, bf16[1,1,512]{2,0,1:T(2,128)(2,1)S(1)}, u32[]{:S(2)}, u32[]{:S(2)}) collective-permute-start(bf16[1,1,512]{2,0,1:T(2,128)(2,1)S(1)} %get-tuple-element.45), channel_id=1, source_target_pairs={{1,32},{2,33},{3,34},{4,35},{5,36},{6,37},{7,38},{8,39},{9,40},{10... | collective-permute-start | bytes 3080 | tf_op jit(solution)/shard_map/ppermute | solution.py:42
  18.3 3.2 %collective-permute-start.2 = (bf16[1,1,512]{2,0,1:T(2,128)(2,1)S(1)}, bf16[1,1,512]{2,0,1:T(2,128)(2,1)S(1)}, u32[]{:S(2)}, u32[]{:S(2)}) collective-permute-start(bf16[1,1,512]{2,0,1:T(2,128)(2,1)S(1)} %get-tuple-element.46), channel_id=1, source_target_pairs={{0,33},{1,34},{2,35},{3,36},{4,37},{5,38},{6,39},{7,40},{8,41},{9,... | collective-permute-start | bytes 3080 | tf_op jit(solution)/shard_map/ppermute | solution.py:42
  21.5 1.3 collective-permute-start.4
  22.8 1.3 collective-permute-start.7
  24.1 0.1 fusion
  24.3 1.9 %collective-permute-start.1 = (bf16[32,1,512]{2,0,1:T(8,128)(2,1)S(1)}, bf16[32,1,512]{2,0,1:T(8,128)(2,1)S(1)}, u32[]{:S(2)}, u32[]{:S(2)}) collective-permute-start(bf16[32,1,512]{2,0,1:T(8,128)(2,1)S(1)} %copy.21), channel_id=1, source_target_pairs={{1,0},{2,1},{3,2},{4,3},{5,4},{6,5},{7,6},{8,7},{9,8},{10,9},{11,1... | collective-permute-start | bytes 98312 | tf_op jit(solution)/shard_map/ppermute | solution.py:30
  26.2 0.1 pad.4.clone
  26.3 0.1 pad.2.clone
  26.4 0.0 collective-permute-done
  26.4 14.1 %collective-permute-start.5 = (bf16[1,16,512]{2,1,0:T(8,128)(2,1)S(1)}, bf16[1,16,512]{2,1,0:T(8,128)(2,1)S(1)}, u32[]{:S(2)}, u32[]{:S(2)}) collective-permute-start(bf16[1,16,512]{2,1,0:T(8,128)(2,1)S(1)} %get-tuple-element.51), channel_id=1, source_target_pairs={{0,32},{32,64},{64,96},{1,33},{33,65},{65,97},{2,34},{34,66},{66,9... | collective-permute-start | bytes 49160 | tf_op jit(solution)/shard_map/ppermute | solution.py:30
  40.5 0.0 collective-permute-done.1
  40.5 1.9 %collective-permute-start.3 = (bf16[32,1,512]{2,0,1:T(8,128)(2,1)S(1)}, bf16[32,1,512]{2,0,1:T(8,128)(2,1)S(1)}, u32[]{:S(2)}, u32[]{:S(2)}) collective-permute-start(bf16[32,1,512]{2,0,1:T(8,128)(2,1)S(1)} %copy.23), channel_id=1, source_target_pairs={{0,1},{1,2},{2,3},{3,4},{4,5},{5,6},{6,7},{7,8},{8,9},{9,10},{10,1... | collective-permute-start | bytes 98312 | tf_op jit(solution)/shard_map/ppermute | solution.py:30
  42.4 0.1 pad_maximum_fusion
  42.5 0.0 collective-permute-done.2
  42.5 1.3 collective-permute-start.6
  43.8 0.0 collective-permute-done.4
  43.8 0.0 collective-permute-done.3
  43.8 0.1 copy.19
  43.9 0.1 copy.18
  44.0 0.0 collective-permute-done.5
  44.0 3.0 %collective-permute-done.6 = bf16[1,16,512]{2,1,0:T(8,128)(2,1)S(1)} collective-permute-done((bf16[1,16,512]{2,1,0:T(8,128)(2,1)S(1)}, bf16[1,16,512]{2,1,0:T(8,128)(2,1)S(1)}, u32[]{:S(2)}, u32[]{:S(2)}) %collective-permute-start.6) | collective-permute-done | bytes 16416 | tf_op jit(solution)/shard_map/ppermute | solution.py:30
  47.0 0.4 maximum_maximum_fusion.1
  47.4 0.0 collective-permute-done.7
  47.4 1.2 maximum_maximum_fusion.x_ref
  48.6 0.0 all-to-all-done
  48.6 1.6 %collective-permute-start.8 = (bf16[64,8,1920]{2,1,0:T(8,128)(2,1)S(1)}, bf16[64,8,1920]{2,1,0:T(8,128)(2,1)S(1)}, u32[]{:S(2)}, u32[]{:S(2)}) collective-permute-start(bf16[64,8,1920]{2,1,0:T(8,128)(2,1)S(1)} %all-to-all-done), channel_id=1, source_target_pairs={{0,1},{1,0},{2,3},{3,2},{4,5},{5,4},{6,7},{7,6},{8,9},{9,8},{10,11... | collective-permute-start | bytes 5898248 | tf_op jit(solution)/shard_map/ppermute | solution.py:684
  50.2 3.6 %collective-permute-done.8 = bf16[64,8,1920]{2,1,0:T(8,128)(2,1)S(1)} collective-permute-done((bf16[64,8,1920]{2,1,0:T(8,128)(2,1)S(1)}, bf16[64,8,1920]{2,1,0:T(8,128)(2,1)S(1)}, u32[]{:S(2)}, u32[]{:S(2)}) %collective-permute-start.8) | collective-permute-done | bytes 1966112 | tf_op jit(solution)/shard_map/ppermute | solution.py:684
  53.8 1.3 copy-done.2
  55.1 11.8 %norm_project_filter.1 = (bf16[512,1024]{1,0:T(8,128)(2,1)}, bf16[512,1024]{1,0:T(8,128)(2,1)}, bf16[512,128]{1,0:T(8,128)(2,1)}, bf16[512,128]{1,0:T(8,128)(2,1...) custom-call(bf16[832,512]{1,0:T(8,128)(2,1)} %maximum_maximum_fusion, ...), custom_call_target="tpu_custom_call" | custom-call | flops 872415232 | bytes 6291456 | tf_op jit(solution)/shard_map/norm_project_filter/pallas_call | solution.py:458
  66.9 7.0 %all-to-all-start.1 = ((bf16[32,16,1024]{2,1,0:T(8,128)(2,1)}), bf16[32,16,1024]{2,1,0:T(8,128)(2,1)S(1)}, u32[]{:S(2)}, u32[]{:S(2)}) async-start(bf16[32,16,1024]{2,1,0:T(8,128)(2,1)} %bitcast.42), calls=%async_computation.1 | async-start | bytes 2097152 | tf_op jit(solution)/shard_map/all_to_all | solution.py:703
  73.9 1.2 collective-permute-start.9
  75.1 1.7 %collective-permute-start.10 = (bf16[272,1024]{1,0:T(8,128)(2,1)}, bf16[272,1024]{1,0:T(8,128)(2,1)}, u32[]{:S(2)}, u32[]{:S(2)}) collective-permute-start(bf16[272,1024]{1,0:T(8,128)(2,1)} %get-tuple-element.36), channel_id=1, source_target_pairs={{0,64},{32,96},{64,0},{96,32},{1,65},{33,97},{65,1},{97,33},{2,66}... | collective-permute-start | bytes 1671176 | tf_op jit(solution)/shard_map/ppermute | solution.py:700
  76.8 2.0 %collective-permute-start.11 = (bf16[272,1024]{1,0:T(8,128)(2,1)}, bf16[272,1024]{1,0:T(8,128)(2,1)}, u32[]{:S(2)}, u32[]{:S(2)}) collective-permute-start(bf16[272,1024]{1,0:T(8,128)(2,1)} %get-tuple-element.37), channel_id=1, source_target_pairs={{0,96},{32,0},{64,32},{96,64},{1,97},{33,1},{65,33},{97,65},{2,98}... | collective-permute-start | bytes 1671176 | tf_op jit(solution)/shard_map/ppermute | solution.py:700
  78.8 6.8 %mix_columns.1.local_ref = bf16[512,1024]{1,0:T(8,128)(2,1)} custom-call(bf16[512,1024]{1,0:T(8,128)(2,1)} %get-tuple-element.28.a_ref, bf16[512,128]{1,0:T(8,128)(2,1)} %get-tuple-element.29.coefs_ref, bf16[512,128]{1,0:T(8,128)(2,1)} %get-tuple-element.30.steps_ref, f32[512,128]{1,0:T(8,128)} %get-tuple-element.31.sums_ref), custom_call_target="tpu_custom_call" | custom-call | flops 4294967296 | bytes 3145728 | tf_op jit(solution)/shard_map/mix_columns/pallas_call | solution.py:521
  85.6 5.4 %all-to-all-done.1 = bf16[32,16,1024]{2,1,0:T(8,128)(2,1)S(1)} async-done(((bf16[32,16,1024]{2,1,0:T(8,128)(2,1)}), bf16[32,16,1024]{2,1,0:T(8,128)(2,1)S(1)}, u32[]{:S(2)}, u32[]{:S(2)}) %all-to-all-start.1) | async-done | bytes 1048608 | tf_op jit(solution)/shard_map/all_to_all | solution.py:703
  91.1 0.0 copy-done.5
  91.1 1.5 %copy-done.3 = bf16[64,8,1920]{2,1,0:T(8,128)(2,1)S(1)} copy-done((bf16[64,8,1920]{2,1,0:T(8,128)(2,1)S(1)}, bf16[64,8,1920]{2,1,0:T(8,128)(2,1)}, u32[]{:S(2)}) %copy-start.3) | copy-done | bytes 1966104
  92.6 9.8 %sweep_rows.1 = bf16[512,1024]{1,0:T(8,128)(2,1)} custom-call(bf16[512,1024]{1,0:T(8,128)(2,1)S(1)} %bitcast.37, bf16[512,1920]{1,0:T(8,128)(2,1)S(1)} %bitcast.28, bf16[512,1920]{1,0:T(8,128)(2,1)S(1)} %bitcast.35, bf16[512,1920]{1,0:T(8,128)(2,1)S(1)} %bitcast.29, bf16[512,1920]{1,0:T(8,128)(2,1)S(1)} %bitcast.36, f32[4,32]{1,0:T(4,128)S(1)} %copy-done.4, ...), custom_call_target="tpu_custom_call" | custom-call | flops 6442450944 | bytes 3145728 | tf_op jit(solution)/shard_map/sweep_rows/pallas_call | solution.py:321
  102.5 0.0 collective-permute-done.9.refs_0_
  102.5 0.0 collective-permute-done.10.refs_1_
  102.5 0.0 collective-permute-done.11.refs_2_
  102.5 7.7 %all-to-all-start.2 = ((bf16[32,16,1024]{2,1,0:T(8,128)(2,1)}), bf16[32,16,1024]{2,1,0:T(8,128)(2,1)S(1)}, u32[]{:S(2)}, u32[]{:S(2)}) async-start(bf16[32,16,1024]{2,1,0:T(8,128)(2,1)} %bitcast.12), calls=%async_computation.2 | async-start | bytes 2097152 | tf_op jit(solution)/shard_map/all_to_all | solution.py:703
  110.1 9.4 %enter_columns.1 = (f32[512,1024]{1,0:T(8,128)}, bf16[512,1024]{1,0:T(8,128)(2,1)}, bf16[1024,512]{1,0:T(8,128)(2,1)}) custom-call(bf16[512,1024]{1,0:T(8,128)(2,1)} %mix_columns.1.local_ref, bf16[512,128]{1,0:T(8,128)(2,1)} %get-tuple-element.33.read_ref, bf16[512,1024]{1,0:T(8,128)(2,1)} %get-tuple-element.27.act_ref, f32[1,1024]{1,0:T(1,128)} %bitcast.50, ...), custom_call_target="tpu_custom_call" | custom-call | flops 4294967296 | bytes 12582912 | tf_op jit(solution)/shard_map/enter_columns/pallas_call | solution.py:601
  119.5 7.8 %all-to-all-done.2 = bf16[32,16,1024]{2,1,0:T(8,128)(2,1)S(1)} async-done(((bf16[32,16,1024]{2,1,0:T(8,128)(2,1)}), bf16[32,16,1024]{2,1,0:T(8,128)(2,1)S(1)}, u32[]{:S(2)}, u32[]{:S(2)}) %all-to-all-start.2) | async-done | bytes 1048608 | tf_op jit(solution)/shard_map/all_to_all | solution.py:703
  127.3 1.0 copy-done.6
  128.3 4.2 %gate_and_project.1 = bf16[512,512]{1,0:T(8,128)(2,1)} custom-call(f32[512,1024]{1,0:T(8,128)} %get-tuple-element.41.part_ref, bf16[512,1024]{1,0:T(8,128)(2,1)} %get-tuple-element.42.gate_ref, bf16[512,1024]{1,0:T(8,128)(2,1)} %bitcast.38, bf16[512,512]{1,0:T(8,128)(2,1)} %bitcast.41, bf16[1024,512]{1,0:T(8,128)(2,1)} %get-tuple-element.44.w_ref, ...), custom_call_target="tpu_custom_call" | custom-call | tf_op jit(solution)/shard_map/gate_and_project/pallas_call | solution.py:634
  (20 shorter events, 0.1 us)
Async XLA Ops:
  2.1 12.1 %copy-start.7 = (bf16[32,16,512]{2,1,0:T(8,128)(2,1)S(1)}, bf16[32,16,512]{2,1,0:T(8,128)(2,1)}, u32[]{:S(2)}) copy-start(bf16[32,16,512]{2,1,0:T(8,128)(2,1)} %param.12) | copy-start | bytes 1572868
  2.1 46.5 %all-to-all-start = ((bf16[64,8,1920]{2,1,0:T(8,128)(2,1)}), bf16[64,8,1920]{2,1,0:T(8,128)(2,1)S(1)}, u32[]{:S(2)}, u32[]{:S(2)}) async-start(bf16[64,8,1920]{2,1,0:T(8,128)(2,1)} %parcels.1), calls=%async_computation | async-start | bytes 3932160 | tf_op jit(solution)/shard_map/all_to_all | solution.py:663
  14.2 12.2 %collective-permute-start = (bf16[1,1,512]{2,0,1:T(2,128)(2,1)S(1)}, bf16[1,1,512]{2,0,1:T(2,128)(2,1)S(1)}, u32[]{:S(2)}, u32[]{:S(2)}) collective-permute-start(bf16[1,1,512]{2,0,1:T(2,128)(2,1)S(1)} %get-tuple-element.45), channel_id=1, source_target_pairs={{1,32},{2,33},{3,34},{4,35},{5,36},{6,37},{7,38},{8,39},{9,40},{10... | collective-permute-start | bytes 3080 | tf_op jit(solution)/shard_map/ppermute | solution.py:42
  18.3 24.2 %collective-permute-start.2 = (bf16[1,1,512]{2,0,1:T(2,128)(2,1)S(1)}, bf16[1,1,512]{2,0,1:T(2,128)(2,1)S(1)}, u32[]{:S(2)}, u32[]{:S(2)}) collective-permute-start(bf16[1,1,512]{2,0,1:T(2,128)(2,1)S(1)} %get-tuple-element.46), channel_id=1, source_target_pairs={{0,33},{1,34},{2,35},{3,36},{4,37},{5,38},{6,39},{7,40},{8,41},{9,... | collective-permute-start | bytes 3080 | tf_op jit(solution)/shard_map/ppermute | solution.py:42
  21.5 22.3 %collective-permute-start.4 = (bf16[1,1,512]{2,0,1:T(2,128)(2,1)S(1)}, bf16[1,1,512]{2,0,1:T(2,128)(2,1)S(1)}, u32[]{:S(2)}, u32[]{:S(2)}) collective-permute-start(bf16[1,1,512]{2,0,1:T(2,128)(2,1)S(1)} %get-tuple-element.47), channel_id=1, source_target_pairs={{32,1},{33,2},{34,3},{35,4},{36,5},{37,6},{38,7},{39,8},{40,9},{41... | collective-permute-start | bytes 3080 | tf_op jit(solution)/shard_map/ppermute | solution.py:42
  22.8 24.6 %collective-permute-start.7 = (bf16[1,1,512]{2,1,0:T(2,128)(2,1)S(1)}, bf16[1,1,512]{2,1,0:T(2,128)(2,1)S(1)}, u32[]{:S(2)}, u32[]{:S(2)}) collective-permute-start(bf16[1,1,512]{2,1,0:T(2,128)(2,1)S(1)} %get-tuple-element.48), channel_id=1, source_target_pairs={{33,0},{34,1},{35,2},{36,3},{37,4},{38,5},{39,6},{40,7},{41,8},{42... | collective-permute-start | bytes 3080 | tf_op jit(solution)/shard_map/ppermute | solution.py:42
  24.3 16.2 %collective-permute-start.1 = (bf16[32,1,512]{2,0,1:T(8,128)(2,1)S(1)}, bf16[32,1,512]{2,0,1:T(8,128)(2,1)S(1)}, u32[]{:S(2)}, u32[]{:S(2)}) collective-permute-start(bf16[32,1,512]{2,0,1:T(8,128)(2,1)S(1)} %copy.21), channel_id=1, source_target_pairs={{1,0},{2,1},{3,2},{4,3},{5,4},{6,5},{7,6},{8,7},{9,8},{10,9},{11,1... | collective-permute-start | bytes 98312 | tf_op jit(solution)/shard_map/ppermute | solution.py:30
  26.4 17.6 %collective-permute-start.5 = (bf16[1,16,512]{2,1,0:T(8,128)(2,1)S(1)}, bf16[1,16,512]{2,1,0:T(8,128)(2,1)S(1)}, u32[]{:S(2)}, u32[]{:S(2)}) collective-permute-start(bf16[1,16,512]{2,1,0:T(8,128)(2,1)S(1)} %get-tuple-element.51), channel_id=1, source_target_pairs={{0,32},{32,64},{64,96},{1,33},{33,65},{65,97},{2,34},{34,66},{66,9... | collective-permute-start | bytes 49160 | tf_op jit(solution)/shard_map/ppermute | solution.py:30
  40.5 3.3 %collective-permute-start.3 = (bf16[32,1,512]{2,0,1:T(8,128)(2,1)S(1)}, bf16[32,1,512]{2,0,1:T(8,128)(2,1)S(1)}, u32[]{:S(2)}, u32[]{:S(2)}) collective-permute-start(bf16[32,1,512]{2,0,1:T(8,128)(2,1)S(1)} %copy.23), channel_id=1, source_target_pairs={{0,1},{1,2},{2,3},{3,4},{4,5},{5,6},{6,7},{7,8},{8,9},{9,10},{10,1... | collective-permute-start | bytes 98312 | tf_op jit(solution)/shard_map/ppermute | solution.py:30
  42.5 4.5 %collective-permute-start.6 = (bf16[1,16,512]{2,1,0:T(8,128)(2,1)S(1)}, bf16[1,16,512]{2,1,0:T(8,128)(2,1)S(1)}, u32[]{:S(2)}, u32[]{:S(2)}) collective-permute-start(bf16[1,16,512]{2,1,0:T(8,128)(2,1)S(1)} %get-tuple-element.52), channel_id=1, source_target_pairs={{32,0},{64,32},{96,64},{33,1},{65,33},{97,65},{34,2},{66,34},{98,6... | collective-permute-start | bytes 49160 | tf_op jit(solution)/shard_map/ppermute | solution.py:30
  48.6 5.3 %copy-start = (bf16[64,8,1920]{2,1,0:T(8,128)(2,1)}, bf16[64,8,1920]{2,1,0:T(8,128)(2,1)S(1)}, u32[]{:S(2)}) copy-start(bf16[64,8,1920]{2,1,0:T(8,128)(2,1)S(1)} %all-to-all-done) | copy-start | bytes 5898244
  48.6 5.2 %collective-permute-start.8 = (bf16[64,8,1920]{2,1,0:T(8,128)(2,1)S(1)}, bf16[64,8,1920]{2,1,0:T(8,128)(2,1)S(1)}, u32[]{:S(2)}, u32[]{:S(2)}) collective-permute-start(bf16[64,8,1920]{2,1,0:T(8,128)(2,1)S(1)} %all-to-all-done), channel_id=1, source_target_pairs={{0,1},{1,0},{2,3},{3,2},{4,5},{5,4},{6,7},{7,6},{8,9},{9,8},{10,11... | collective-permute-start | bytes 5898248 | tf_op jit(solution)/shard_map/ppermute | solution.py:684
  53.8 1.3 copy-start.2
  66.9 24.1 %all-to-all-start.1 = ((bf16[32,16,1024]{2,1,0:T(8,128)(2,1)}), bf16[32,16,1024]{2,1,0:T(8,128)(2,1)S(1)}, u32[]{:S(2)}, u32[]{:S(2)}) async-start(bf16[32,16,1024]{2,1,0:T(8,128)(2,1)} %bitcast.42), calls=%async_computation.1 | async-start | bytes 2097152 | tf_op jit(solution)/shard_map/all_to_all | solution.py:703
  73.9 28.6 %collective-permute-start.9 = (bf16[272,1024]{1,0:T(8,128)(2,1)}, bf16[272,1024]{1,0:T(8,128)(2,1)}, u32[]{:S(2)}, u32[]{:S(2)}) collective-permute-start(bf16[272,1024]{1,0:T(8,128)(2,1)} %get-tuple-element.35), channel_id=1, source_target_pairs={{0,32},{32,64},{64,96},{96,0},{1,33},{33,65},{65,97},{97,1},{2,34}... | collective-permute-start | bytes 1671176 | tf_op jit(solution)/shard_map/ppermute | solution.py:700
  75.1 27.3 %collective-permute-start.10 = (bf16[272,1024]{1,0:T(8,128)(2,1)}, bf16[272,1024]{1,0:T(8,128)(2,1)}, u32[]{:S(2)}, u32[]{:S(2)}) collective-permute-start(bf16[272,1024]{1,0:T(8,128)(2,1)} %get-tuple-element.36), channel_id=1, source_target_pairs={{0,64},{32,96},{64,0},{96,32},{1,65},{33,97},{65,1},{97,33},{2,66}... | collective-permute-start | bytes 1671176 | tf_op jit(solution)/shard_map/ppermute | solution.py:700
  76.8 25.6 %collective-permute-start.11 = (bf16[272,1024]{1,0:T(8,128)(2,1)}, bf16[272,1024]{1,0:T(8,128)(2,1)}, u32[]{:S(2)}, u32[]{:S(2)}) collective-permute-start(bf16[272,1024]{1,0:T(8,128)(2,1)} %get-tuple-element.37), channel_id=1, source_target_pairs={{0,96},{32,0},{64,32},{96,64},{1,97},{33,1},{65,33},{97,65},{2,98}... | collective-permute-start | bytes 1671176 | tf_op jit(solution)/shard_map/ppermute | solution.py:700
  78.8 12.2 %copy-start.1 = (bf16[64,8,1920]{2,1,0:T(8,128)(2,1)S(1)}, bf16[64,8,1920]{2,1,0:T(8,128)(2,1)}, u32[]{:S(2)}) copy-start(bf16[64,8,1920]{2,1,0:T(8,128)(2,1)} %copy-done) | copy-start | bytes 5898244
  78.8 12.2 %copy-start.4 = (f32[4,32]{1,0:T(4,128)S(1)}, f32[4,32]{1,0:T(4,128)}, u32[]{:S(2)}) copy-start(f32[4,32]{1,0:T(4,128)} %bias_ref.1) | copy-start | bytes 1540
  78.8 12.2 %copy-start.5 = (f32[4,32]{1,0:T(4,128)S(1)}, f32[4,32]{1,0:T(4,128)}, u32[]{:S(2)}) copy-start(f32[4,32]{1,0:T(4,128)} %rate_ref.1) | copy-start | bytes 1540
  91.1 1.5 %copy-start.3 = (bf16[64,8,1920]{2,1,0:T(8,128)(2,1)S(1)}, bf16[64,8,1920]{2,1,0:T(8,128)(2,1)}, u32[]{:S(2)}) copy-start(bf16[64,8,1920]{2,1,0:T(8,128)(2,1)} %copy-done.2) | copy-start | bytes 5898244
  102.5 24.8 %all-to-all-start.2 = ((bf16[32,16,1024]{2,1,0:T(8,128)(2,1)}), bf16[32,16,1024]{2,1,0:T(8,128)(2,1)S(1)}, u32[]{:S(2)}, u32[]{:S(2)}) async-start(bf16[32,16,1024]{2,1,0:T(8,128)(2,1)} %bitcast.12), calls=%async_computation.2 | async-start | bytes 2097152 | tf_op jit(solution)/shard_map/all_to_all | solution.py:703
  127.3 1.0 copy-start.6
